TPU v7x, 128 devices: a whole 4x4x4 slice. The times are simulated.
128 devices in a mesh: rep: 8 (over y, core), tp: 16 (over x, z).
Axes of the slice: x: 4, y: 4, z: 4, core: 2. Of those that a mesh axis runs over, the one named last changes fastest.
Arguments:
- inputs: bfloat16 [32768, 1024], P(('rep', 'tp')), may hold values from -6 to 6
- cotangent: bfloat16 [32768, 16384], P('rep', 'tp'), may hold values from -1 to 1
- master: float32 [1024, 16384], P('rep', 'tp'), may hold values from -6 to 6
- moment: float32 [1024, 16384], P('rep', 'tp'), may hold values from -6 to 6
- second: float32 [1024, 16384], P('rep', 'tp'), may hold values from 0.5 to 4
Outputs:
- combined: float32 [1024, 16384], P('rep', 'tp')
- moment_new: float32 [1024, 16384], P('rep', 'tp')
- second_new: float32 [1024, 16384], P('rep', 'tp')
- master_new: float32 [1024, 16384], P('rep', 'tp')
- weights: bfloat16 [1024, 16384], P(None, 'tp')
All inputs are finite; a program needn't handle non-finite values.
Results may differ from a plain program's by a relative error of at most 0.001.
Values may be sent and summed in bfloat16 or wider, within the bound.
No kernel may reach another device: no remote copies, remote signals or barrier semaphores. Data moves between devices by JAX's collectives and lax.ppermute only.
A program may use at most 64 MiB of HBM per device.

v0:
```python
import jax
import jax.numpy as jnp
from jax import lax
from jax.sharding import PartitionSpec as P

EPS_SUM = 1e-06
BETA_ONE = 0.9
BETA_TWO = 0.999
LEARN = 0.01
CORRECT_ONE = 1.0 - 0.9**50
CORRECT_TWO = 1.0 - 0.999**50


def from_partner(value, axis, stride):
    return lax.ppermute(value, axis, [(i, i ^ 1 << stride) for i in range(lax.axis_size(axis))])


def trade_halves(sent_rows, distance_bit):
    return from_partner(sent_rows, "rep", distance_bit)


def combine_level(kept_rows, received, is_upper, distance_bit, levels):
    lower_part = jnp.where(is_upper, received, kept_rows)
    upper_part = jnp.where(is_upper, kept_rows, received)
    partial_value = jnp.stack(
        [
            jnp.sum(lower_part * lower_part),
            jnp.sum(upper_part * upper_part),
            jnp.sum(lower_part * upper_part),
        ]
    )
    for inner_bit in range(distance_bit, levels):
        partial_value = partial_value + from_partner(partial_value, "rep", inner_bit)
    partial_value = lax.psum(partial_value, "tp")
    low_low = partial_value[0]
    high_high = partial_value[1]
    cross_term = partial_value[2]
    lower_coef = 1.0 - cross_term / (2.0 * (low_low + EPS_SUM))
    upper_coef = 1.0 - cross_term / (2.0 * (high_high + EPS_SUM))
    return lower_coef * lower_part + upper_coef * upper_part


def per_device(inputs, cotangent, master, moment, second):
    replicas = lax.axis_size("rep")
    levels = replicas.bit_length() - 1
    my_index = lax.axis_index("rep")
    segment = lax.dot_general(
        lax.all_gather(inputs, "tp", axis=0, tiled=True),
        cotangent,
        (((0,), (0,)), ((), ())),
        preferred_element_type=jnp.float32,
    )
    first_level = 0
    for level_index in range(first_level, levels):
        distance_bit = levels - 1 - level_index
        is_upper = my_index >> distance_bit & 1 == 1
        half_rows = segment.shape[0] // 2
        front_half = segment[:half_rows]
        back_half = segment[half_rows:]
        kept_rows = jnp.where(is_upper, back_half, front_half)
        sent_rows = jnp.where(is_upper, front_half, back_half)
        received = trade_halves(sent_rows, distance_bit)
        segment = combine_level(kept_rows, received, is_upper, distance_bit, levels)
    moment_new = BETA_ONE * moment + (1.0 - BETA_ONE) * segment
    second_new = BETA_TWO * second + (1.0 - BETA_TWO) * segment * segment
    master_new = master - LEARN * (moment_new / CORRECT_ONE) / (
        jnp.sqrt(second_new / CORRECT_TWO) + 1e-08
    )
    weights = lax.all_gather(master_new.astype(jnp.bfloat16), "rep", axis=0, tiled=True)
    return (segment, moment_new, second_new, master_new, weights)


def solution(mesh):
    return jax.shard_map(
        per_device,
        mesh=mesh,
        in_specs=(
            P(("rep", "tp"), None),
            P("rep", "tp"),
            P("rep", "tp"),
            P("rep", "tp"),
            P("rep", "tp"),
        ),
        out_specs=(P("rep", "tp"), P("rep", "tp"), P("rep", "tp"), P("rep", "tp"), P(None, "tp")),
        check_vma=False,
    )
```

profile of v0, /device:TPU:1, one launch (start us, length us, event | category | flops | bytes accessed | tf_op | source)
XLA Modules:
  0.0 375.4 jit_solution(15350393756312768842)
XLA Ops:
  8.0 76.3 %all-gather.3.cloned.1.call-done = bf16[4096,1024]{1,0:T(8,128)(2,1)} async-done(((bf16[256,1024]{1,0:T(8,128)(2,1)}), bf16[4096,1024]{1,0:T(8,128)(2,1)}) %all-gather.3.cloned.1.call-update) | async-done | bytes 8388624 | tf_op jit(solution)/shard_map/all_gather | solution.py:48
  84.2 13.1 %fusion.6 = f32[1024,1024]{1,0:T(8,128)S(1)} fusion(bf16[4096,1024]{1,0:T(8,128)(2,1)} %all-gather.3.cloned.1.call-done, bf16[4096,1024]{1,0:T(8,128)(2,1)} %param.6), kind=kOutput, calls=%fused_computation.35 | convolution fusion | flops 8589934592 | bytes 20971520 | tf_op jit(solution)/shard_map/dot_general | solution.py:47
  99.2 2.7 collective-permute-start
  102.0 45.4 %collective-permute-done = f32[512,1024]{1,0:T(8,128)} collective-permute-done((f32[512,1024]{1,0:T(8,128)S(1)}, f32[512,1024]{1,0:T(8,128)}, u32[]{:S(2)}, u32[]{:S(2)}) %collective-permute-start) | collective-permute-done | bytes 2097184 | tf_op jit(solution)/shard_map/ppermute | solution.py:15
  147.4 6.7 %multiply_reduce_fusion.2 = (f32[]{:T(128)}, f32[]{:T(128)}, f32[]{:T(128)}, f32[512,1024]{1,0:T(8,128)}, f32[512,1024]{1,0:T(8,128)}) fusion(f32[512,1024]{1,0:T(8,128)} %collective-permute-done, f32[1024,1024]{1,0:T(8,128)} %copy-done, pred[]{:T(512)S(6)} %eq.11), kind=kLoop, calls=%fused_computation.3 | loop fusion | flops 4718589 | bytes 10485773 | tf_op jit(solution)/shard_map/reduce_sum | solution.py:27
  154.1 2.0 pad_maximum_fusion
  156.1 2.8 collective-permute-start.1
  160.0 2.0 fusion.11
  162.0 31.3 %psum.21 = f32[3]{0:T(128)S(1)} all-reduce(f32[3]{0:T(128)S(1)} %fusion.11), channel_id=1, replica_groups=mesh['rep'=8,'tp'=16] {'tp'}, use_global_device_ids=true, to_apply=%region_3.4 | all-reduce | flops 3 | bytes 24 | tf_op jit(solution)/shard_map/psum | solution.py:34
  196.6 2.7 multiply_add_fusion
  200.7 13.8 %collective-permute-done.2 = f32[256,1024]{1,0:T(8,128)} collective-permute-done((f32[256,1024]{1,0:T(8,128)S(1)}, f32[256,1024]{1,0:T(8,128)}, u32[]{:S(2)}, u32[]{:S(2)}) %collective-permute-start.2) | collective-permute-done | bytes 1048608 | tf_op jit(solution)/shard_map/ppermute | solution.py:15
  214.5 3.2 multiply_reduce_fusion.5
  222.5 2.0 fusion.10
  224.6 2.8 collective-permute-start.4
  228.5 2.0 fusion.13
  230.5 29.0 %psum.22 = f32[3]{0:T(128)S(1)} all-reduce(f32[3]{0:T(128)S(1)} %fusion.13), channel_id=1, replica_groups=mesh['rep'=8,'tp'=16] {'tp'}, use_global_device_ids=true, to_apply=%region_7.8 | all-reduce | flops 3 | bytes 24 | tf_op jit(solution)/shard_map/psum | solution.py:34
  264.2 19.1 %collective-permute-start.5 = (f32[128,1024]{1,0:T(8,128)S(1)}, f32[128,1024]{1,0:T(8,128)S(1)}, u32[]{:S(2)}, u32[]{:S(2)}) collective-permute-start(f32[128,1024]{1,0:T(8,128)S(1)} %slice_select_fusion.5), channel_id=1, source_target_pairs={{0,16},{16,0},{32,48},{48,32},{64,80},{80,64},{96,112},{112,96},{1... | collective-permute-start | bytes 1572872 | tf_op jit(solution)/shard_map/ppermute | solution.py:15
  285.7 2.0 pad_maximum_fusion.2
  289.0 2.0 fusion.9
  293.4 2.0 fusion.12
  295.4 2.8 collective-permute-start.8
  299.3 30.2 %psum.23 = f32[3]{0:T(128)S(1)} all-reduce(f32[3]{0:T(128)S(1)} %add.80), channel_id=1, replica_groups=mesh['rep'=8,'tp'=16] {'tp'}, use_global_device_ids=true, to_apply=%region_11.12 | all-reduce | flops 3 | bytes 24 | tf_op jit(solution)/shard_map/psum | solution.py:34
  334.4 31.1 %all-gather.5.cloned.1.call-done = bf16[1024,1024]{1,0:T(8,128)(2,1)} async-done(((bf16[128,1024]{1,0:T(8,128)(2,1)}), bf16[1024,1024]{1,0:T(8,128)(2,1)}) %all-gather.5.cloned.1.call-update) | async-done | bytes 2097168 | tf_op jit(solution)/shard_map/all_gather | solution.py:69
  365.5 3.1 copy.11
  (34 shorter events, 23.4 us)
Async XLA Ops:
  7.2 77.1 %all-gather.3.cloned.1.call-start = ((), (), s32[]{:S(2)}) async-start(), calls=%async_computation | async-start | bytes 8912896 | tf_op jit(solution)/shard_map/all_gather | solution.py:48
  7.9 357.6 %all-gather.5.cloned.1.call-start = ((), (), s32[]{:S(2)}) async-start(), calls=%async_computation.1 | async-start | bytes 2359296 | tf_op jit(solution)/shard_map/all_gather | solution.py:69
  97.3 1.9 copy-start
  99.2 48.1 %collective-permute-start = (f32[512,1024]{1,0:T(8,128)S(1)}, f32[512,1024]{1,0:T(8,128)}, u32[]{:S(2)}, u32[]{:S(2)}) collective-permute-start(f32[512,1024]{1,0:T(8,128)S(1)} %slice_select_fusion.1), channel_id=1, source_target_pairs={{0,64},{16,80},{32,96},{48,112},{64,0},{80,16},{96,32},{112,48},{1... | collective-permute-start | bytes 6291464 | tf_op jit(solution)/shard_map/ppermute | solution.py:15
  156.1 3.9 %collective-permute-start.1 = (f32[3]{0:T(128)S(1)}, f32[3]{0:T(128)S(1)}, u32[]{:S(2)}, u32[]{:S(2)}) collective-permute-start(f32[3]{0:T(128)S(1)} %pad_maximum_fusion), channel_id=1, source_target_pairs={{0,64},{16,80},{32,96},{48,112},{64,0},{80,16},{96,32},{112,48},{1... | collective-permute-start | bytes 44 | tf_op jit(solution)/shard_map/ppermute | solution.py:15
  199.4 15.1 %collective-permute-start.2 = (f32[256,1024]{1,0:T(8,128)S(1)}, f32[256,1024]{1,0:T(8,128)}, u32[]{:S(2)}, u32[]{:S(2)}) collective-permute-start(f32[256,1024]{1,0:T(8,128)S(1)} %slice_select_fusion.3), channel_id=1, source_target_pairs={{0,32},{16,48},{32,0},{48,16},{64,96},{80,112},{96,64},{112,80},{1... | collective-permute-start | bytes 3145736 | tf_op jit(solution)/shard_map/ppermute | solution.py:15
  219.7 2.9 collective-permute-start.3
  224.6 3.9 %collective-permute-start.4 = (f32[3]{0:T(128)S(1)}, f32[3]{0:T(128)S(1)}, u32[]{:S(2)}, u32[]{:S(2)}) collective-permute-start(f32[3]{0:T(128)S(1)} %fusion.10), channel_id=1, source_target_pairs={{0,64},{16,80},{32,96},{48,112},{64,0},{80,16},{96,32},{112,48},{1... | collective-permute-start | bytes 44 | tf_op jit(solution)/shard_map/ppermute | solution.py:15
  264.1 68.7 %copy-start.1 = (f32[128,1024]{1,0:T(8,128)S(1)}, f32[128,1024]{1,0:T(8,128)}, u32[]{:S(2)}) copy-start(f32[128,1024]{1,0:T(8,128)} %param.7) | copy-start | bytes 1572868
  264.1 68.7 %copy-start.2 = (f32[128,1024]{1,0:T(8,128)S(1)}, f32[128,1024]{1,0:T(8,128)}, u32[]{:S(2)}) copy-start(f32[128,1024]{1,0:T(8,128)} %param.9) | copy-start | bytes 1572868
  264.1 68.7 %copy-start.3 = (f32[128,1024]{1,0:T(8,128)S(1)}, f32[128,1024]{1,0:T(8,128)}, u32[]{:S(2)}) copy-start(f32[128,1024]{1,0:T(8,128)} %param.8) | copy-start | bytes 1572868
  264.2 20.7 %collective-permute-start.5 = (f32[128,1024]{1,0:T(8,128)S(1)}, f32[128,1024]{1,0:T(8,128)S(1)}, u32[]{:S(2)}, u32[]{:S(2)}) collective-permute-start(f32[128,1024]{1,0:T(8,128)S(1)} %slice_select_fusion.5), channel_id=1, source_target_pairs={{0,16},{16,0},{32,48},{48,32},{64,80},{80,64},{96,112},{112,96},{1... | collective-permute-start | bytes 1572872 | tf_op jit(solution)/shard_map/ppermute | solution.py:15
  287.8 1.2 collective-permute-start.6
  291.0 2.4 collective-permute-start.7
  295.4 3.9 %collective-permute-start.8 = (f32[3]{0:T(128)S(1)}, f32[3]{0:T(128)S(1)}, u32[]{:S(2)}, u32[]{:S(2)}) collective-permute-start(f32[3]{0:T(128)S(1)} %fusion.12), channel_id=1, source_target_pairs={{0,64},{16,80},{32,96},{48,112},{64,0},{80,16},{96,32},{112,48},{1... | collective-permute-start | bytes 44 | tf_op jit(solution)/shard_map/ppermute | solution.py:15
Sparse Core Ops, SparseCore 0:
  10.1 74.0 all-gather.2
  334.5 30.9 all-gather.4
where the time goes:
time: 376 us; the launch traced here: 375 us
  waiting for transfers between devices  176 us (47%)
  blocking collectives  90.5 us (24%)
  starting transfers between devices  34.3 us (9%)
  other arithmetic  33.2 us (9%)
  between operations  22 us (6%)
  matrix products  13.1 us (3%)
  local copies, waits for them, and re-layouts  6.38 us (2%)
    psum x3, blocking collectives, combine_level(): partial_value = lax.psum(partial_value, 'tp')  90.5 us
    all_gather x1, waiting for transfers between devices, per_device(): lax.all_gather(inputs, 'tp', axis=0, tiled=True)  76.3 us
    ppermute x9, waiting for transfers between devices, from_partner(): lax.ppermute(value, axis, [(i, i ^ 1 << stride) for i in range(lax.axis_s...  67.8 us
    ppermute x9, starting transfers between devices, from_partner(): lax.ppermute(value, axis, [(i, i ^ 1 << stride) for i in range(lax.axis_s...  34.3 us
    all_gather x1, waiting for transfers between devices, per_device(): lax.all_gather(master_new.astype(jnp.bfloat16), 'rep', axis=0, tiled=True)  31.1 us
    dot_general x1, matrix products, per_device(): lax.dot_general(lax.all_gather(inputs, 'tp', axis=0, tiled=True), cotange...  13.1 us
    reduce_sum x3, other arithmetic, combine_level(): jnp.sum(lower_part * lower_part)  10.8 us
    add x6, other arithmetic, combine_level(): partial_value + from_partner(partial_value, 'rep', inner_bit)  10.1 us
  transfers between devices with their start and end apart: 11, of which 11 were waited for; matrix products, arithmetic and copies ran while one was open for 0% of the time, Pallas kernels for 0%

commit v1 on v0

v1 whole, which is shorter than its diff:
```python
import functools

import jax
import jax.numpy as jnp
from jax import lax
from jax.experimental import pallas as pl
from jax.experimental.pallas import tpu as pltpu
from jax.sharding import PartitionSpec as P

EPS_SUM = 1e-06
BETA_ONE = 0.9
BETA_TWO = 0.999
LEARN = 0.01
CORRECT_ONE = 1.0 - 0.9**50
CORRECT_TWO = 1.0 - 0.999**50

RING = (0, 1, 3, 2)
CHUNKS = (((4, 5), (2, 6)), ((3, 7), (1, 0)))
PAIRS = [(k, l) for k in range(8) for l in range(k, 8)]
ROW = {pair: row for row, pair in enumerate(PAIRS)}
PAIR_ROWS = 40
BLOCK = 128
EXTRA = 8
WHOLE = pl.BlockSpec(memory_space=pltpu.VMEM)
SMEM = pl.BlockSpec(memory_space=pltpu.SMEM)
MIB = 1 << 20


def swap(value, axis, distance):
    return lax.ppermute(value, axis, [(i, i ^ distance) for i in range(lax.axis_size(axis))])


def row_of(k, l):
    return ROW[(min(k, l), max(k, l))]


def turn_kernel(rep_ref, x_ref, a_ref, b_ref):
    rep = rep_ref[0]
    for half, out in ((0, a_ref), (1, b_ref)):
        owners = [k for chunk in CHUNKS for k in chunk[half]]
        for i, k in enumerate(owners):
            column = pl.multiple_of((rep ^ k) * BLOCK, BLOCK)
            out[i * BLOCK : (i + 1) * BLOCK, :] = x_ref[:, pl.ds(column, BLOCK)].T


def turn(rep, x):
    tokens, features = x.shape
    half = jax.ShapeDtypeStruct((features // 2, tokens), x.dtype)
    return pl.pallas_call(
        turn_kernel,
        out_shape=(half, half),
        in_specs=[SMEM, WHOLE],
        out_specs=(WHOLE, WHOLE),
        compiler_params=pltpu.CompilerParams(vmem_limit_bytes=6 * MIB),
    )(rep, x)


def spread(own, axis_step):
    return [own] + [swap(own, "tp", axis_step * d) for d in RING[1:]]


def spread_halves(own, axis_step):
    near = swap(own, "tp", axis_step)
    far = swap(own, "tp", axis_step * 3)
    h = own.shape[0] // 2
    return [own, near, far, swap(far[:h], "tp", axis_step), swap(near[h:], "tp", axis_step * 3)]


def product_kernel(owners, _, *refs):
    a_refs, b_refs, g_refs = refs[:5], refs[5:10], refs[10:14]
    outs, acc = refs[14:-1], refs[-1]
    step = pl.program_id(0)

    def piece(pieces, outer, inner):
        if outer < 3:
            return pieces[outer][inner]
        return pieces[3 + inner // 2][inner % 2]

    for z in range(4):

        @pl.when(step == z)
        def _():
            left = jnp.concatenate(
                [
                    jnp.concatenate([piece(a_refs, z, x) for x in range(4)], axis=1),
                    jnp.concatenate([piece(b_refs, x, z) for x in range(4)], axis=1),
                ],
                axis=0,
            )
            right = jnp.concatenate([g[...] for g in g_refs], axis=0)
            part = jnp.dot(left, right, preferred_element_type=jnp.float32)
            if z == 0:
                acc[...] = part
            else:
                acc[...] += part

    @pl.when(step == 3)
    def _():
        for i, (k, out) in enumerate(zip(owners, outs)):
            block = acc[i * BLOCK : (i + 1) * BLOCK, :]
            if k == 0:
                out[...] = block
                continue
            top = jnp.max(jnp.max(jnp.abs(block), axis=0, keepdims=True), axis=1, keepdims=True)
            power = jnp.floor(15.0 - jnp.log2(jnp.maximum(top, 1e-30)))
            out[:BLOCK, :] = block * jnp.exp2(power)
            out[BLOCK:, :] = jnp.broadcast_to(power, (EXTRA, block.shape[1]))


def product(owners, place, a_pieces, b_pieces, cotangent):
    tokens, columns = cotangent.shape
    rows = tokens // 16
    features = BLOCK * len(owners)

    def g_spec(x):
        return pl.BlockSpec(
            (rows, columns), lambda s, p: (p[0] ^ (4 * RING[x]) ^ s ^ (s >> 1), 0)
        )

    shapes = [
        jax.ShapeDtypeStruct((BLOCK if k == 0 else BLOCK + EXTRA, columns), jnp.float32)
        for k in owners
    ]
    return pl.pallas_call(
        functools.partial(product_kernel, owners),
        grid_spec=pltpu.PrefetchScalarGridSpec(
            num_scalar_prefetch=1,
            grid=(4,),
            in_specs=[WHOLE] * 10 + [g_spec(x) for x in range(4)],
            out_specs=[WHOLE] * len(owners),
            scratch_shapes=[pltpu.VMEM((features, columns), jnp.float32)],
        ),
        out_shape=shapes,
        compiler_params=pltpu.CompilerParams(vmem_limit_bytes=28 * MIB),
        cost_estimate=pl.CostEstimate(
            flops=2 * tokens * columns * features,
            bytes_accessed=2 * tokens * columns + 2 * tokens * features,
            transcendentals=0,
        ),
    )(place, *a_pieces, *b_pieces, *[cotangent] * 4)


def gram_kernel(*refs):
    blocks, out = refs[:8], refs[8]
    rows, columns = blocks[0].shape
    lanes = 128
    sums = tuple(jnp.zeros((8, lanes), jnp.float32) for _ in PAIRS)

    def body(i, sums):
        row = pl.multiple_of(i * 8, 8)
        for c in range(columns // lanes):
            tile = [b[pl.ds(row, 8), c * lanes : (c + 1) * lanes] for b in blocks]
            sums = tuple(s + tile[k] * tile[l] for s, (k, l) in zip(sums, PAIRS))
        return sums

    sums = lax.fori_loop(0, rows // 8, body, sums)
    out[...] = jnp.zeros_like(out)
    for row, total in enumerate(sums):
        out[row : row + 1, :] = jnp.sum(total, axis=0, keepdims=True)


def gram(blocks):
    return pl.pallas_call(
        gram_kernel,
        out_shape=jax.ShapeDtypeStruct((PAIR_ROWS, 128), jnp.float32),
        in_specs=[WHOLE] * 8,
        out_specs=WHOLE,
        compiler_params=pltpu.CompilerParams(vmem_limit_bytes=8 * MIB),
    )(*blocks)


def join_kernel(distances, own, *refs):
    received, out = refs[:-1], refs[-1]
    out[...] = jnp.zeros_like(out)
    for (k, l), row in ROW.items():
        total = own[row : row + 1, :]
        for d, other in zip(distances, received):
            at = row_of(k ^ d, l ^ d)
            total = total + other[at : at + 1, :]
        out[row : row + 1, :] = total


def join(own, distances):
    received = [swap(own, "rep", d) for d in distances]
    return pl.pallas_call(
        functools.partial(join_kernel, distances),
        out_shape=jax.ShapeDtypeStruct(own.shape, own.dtype),
        in_specs=[WHOLE] * (1 + len(received)),
        out_specs=WHOLE,
        compiler_params=pltpu.CompilerParams(vmem_limit_bytes=1 * MIB),
    )(own, *received)


def coefficients(total):
    value = jnp.sum(total, axis=1, keepdims=True)

    def inner(k, l):
        at = row_of(k, l)
        return value[at : at + 1, :]

    def weigh(inner, count):
        half = count // 2
        coef = [None] * count
        for k in range(half):
            a = jnp.maximum(inner(k, k), 0.0)
            b = jnp.maximum(inner(k + half, k + half), 0.0)
            bound = jnp.sqrt(a) * jnp.sqrt(b)
            cross = jnp.clip(inner(k, k + half), -bound, bound)
            coef[k] = 1.0 - cross / (2.0 * (a + EPS_SUM))
            coef[k + half] = 1.0 - cross / (2.0 * (b + EPS_SUM))
        memo = {}

        def following(k, l):
            k, l = min(k, l), max(k, l)
            if (k, l) not in memo:
                low = coef[l] * inner(k, l) + coef[l + half] * inner(k, l + half)
                high = coef[l] * inner(k + half, l) + coef[l + half] * inner(k + half, l + half)
                memo[(k, l)] = coef[k] * low + coef[k + half] * high
            return memo[(k, l)]

        return coef, following

    first, inner_two = weigh(inner, 8)
    second, inner_three = weigh(inner_two, 4)
    third, _ = weigh(inner_three, 2)
    return [first[k] * second[k % 4] * third[k % 2] for k in range(8)]


def adam_kernel(*refs):
    sums, blocks = refs[:4], refs[4:12]
    master, moment, second = refs[12:15]
    combined_out, moment_out, second_out, master_out, weights_out, coef = refs[15:]
    total = sums[0][...] + sums[1][...] + sums[2][...] + sums[3][...]
    for k, c in enumerate(coefficients(total)):
        coef[k : k + 1, :] = jnp.broadcast_to(c, (1, 128))
    rows, columns = blocks[0].shape
    scale = [coef[k : k + 1, 0:1] for k in range(8)]

    def body(i, carry):
        at = pl.ds(pl.multiple_of(i * 16, 16), 16)
        combined = scale[0] * blocks[0][at, :]
        for k in range(1, 8):
            combined = combined + scale[k] * blocks[k][at, :]
        moment_new = BETA_ONE * moment[at, :] + (1.0 - BETA_ONE) * combined
        second_new = BETA_TWO * second[at, :] + (1.0 - BETA_TWO) * combined * combined
        master_new = master[at, :] - LEARN * (moment_new / CORRECT_ONE) / (
            jnp.sqrt(second_new / CORRECT_TWO) + 1e-08
        )
        combined_out[at, :] = combined
        moment_out[at, :] = moment_new
        second_out[at, :] = second_new
        master_out[at, :] = master_new
        weights_out[at, :] = master_new.astype(jnp.bfloat16)
        return carry

    lax.fori_loop(0, rows // 16, body, 0)


def adam(sums, blocks, master, moment, second):
    full = jax.ShapeDtypeStruct(master.shape, jnp.float32)
    return pl.pallas_call(
        adam_kernel,
        out_shape=(full, full, full, full, jax.ShapeDtypeStruct(master.shape, jnp.bfloat16)),
        in_specs=[WHOLE] * 15,
        out_specs=(WHOLE,) * 5,
        scratch_shapes=[pltpu.VMEM((8, 128), jnp.float32)],
        compiler_params=pltpu.CompilerParams(vmem_limit_bytes=16 * MIB),
    )(*sums, *blocks, master, moment, second)


def place_kernel(rep_ref, *refs):
    parts, out, sems = refs[:8], refs[8], refs[9]
    rep = rep_ref[0]
    copies = []
    for k, part in enumerate(parts):
        at = pl.ds(pl.multiple_of((rep ^ k) * BLOCK, BLOCK), BLOCK)
        copies.append(pltpu.make_async_copy(part, out.at[at, :], sems.at[k]))
    for copy in copies:
        copy.start()
    for copy in copies:
        copy.wait()


def assemble(rep, parts):
    rows, columns = parts[0].shape
    anywhere = pl.BlockSpec(memory_space=pl.ANY)
    return pl.pallas_call(
        place_kernel,
        out_shape=jax.ShapeDtypeStruct((8 * rows, columns), parts[0].dtype),
        in_specs=[SMEM] + [anywhere] * 8,
        out_specs=anywhere,
        scratch_shapes=[pltpu.SemaphoreType.DMA((8,))],
        compiler_params=pltpu.CompilerParams(vmem_limit_bytes=1 * MIB),
    )(rep, *parts)


def per_device(inputs, cotangent, master, moment, second):
    rep = lax.axis_index("rep").astype(jnp.int32).reshape((1,))
    place = lax.axis_index("tp").astype(jnp.int32).reshape((1,))
    a, b = turn(rep, inputs)
    a_line = spread(a, 4)
    b_line = spread(b, 1)
    blocks = [None] * 8
    for i, (a_owners, b_owners) in enumerate(CHUNKS):
        rows = slice(i * 2 * BLOCK, (i + 1) * 2 * BLOCK)
        a_pieces = spread_halves(jnp.stack([piece[rows] for piece in a_line]), 1)
        b_pieces = spread_halves(jnp.stack([piece[rows] for piece in b_line]), 4)
        owners = a_owners + b_owners
        for k, value in zip(owners, product(owners, place, a_pieces, b_pieces, cotangent)):
            if k == 0:
                blocks[k] = value
                continue
            got = swap(value.astype(jnp.float16), "rep", k).astype(jnp.float32)
            blocks[k] = got[:BLOCK] * jnp.exp2(-got[BLOCK : BLOCK + 1])
    sums = gram(blocks)
    sums = join(sums, (1,))
    sums = join(sums, (2, 4, 6))
    sums = sums + swap(sums, "tp", 1) + swap(sums, "tp", 2) + swap(sums, "tp", 3)
    sums = [sums] + [swap(sums, "tp", d) for d in (4, 8, 12)]
    combined, moment_new, second_new, master_new, mine = adam(sums, blocks, master, moment, second)
    column = {0: mine, **{k: swap(mine, "rep", k) for k in (4, 2, 6)}}
    parts = [None] * 8
    for k, value in column.items():
        parts[k] = value
        parts[k ^ 1] = swap(value, "rep", 1)
    weights = assemble(rep, parts)
    return (combined, moment_new, second_new, master_new, weights)


def solution(mesh):
    return jax.shard_map(
        per_device,
        mesh=mesh,
        in_specs=(
            P(("rep", "tp"), None),
            P("rep", "tp"),
            P("rep", "tp"),
            P("rep", "tp"),
            P("rep", "tp"),
        ),
        out_specs=(P("rep", "tp"), P("rep", "tp"), P("rep", "tp"), P("rep", "tp"), P(None, "tp")),
        check_vma=False,
    )
```

time: 376 us -> 158 us (0.42)
  waiting for transfers between devices: 176 us -> 46.6 us
  blocking collectives: 90.5 us -> 0 us
  starting transfers between devices: 34.3 us -> 72.3 us
  other arithmetic: 33.2 us -> 1.19 us
  between operations: 22 us -> 1.33 us
  Pallas kernels: 0 us -> 18.5 us
  matrix products: 13.1 us -> 0 us
  local copies, waits for them, and re-layouts: 6.38 us -> 17.7 us
    all_gather x2 -> x0, waiting for transfers between devices: 107 us -> none  [the longest x1 76.3 us: per_device(): lax.all_gather(inputs, 'tp', axis=0, tiled=True)]
    psum x3 -> x0, blocking collectives: 90.5 us -> none  [combine_level(): partial_value = lax.psum(partial_value, 'tp')]
    ppermute x9 -> x46, starting transfers between devices: 34.3 us -> 72.3 us  [swap(): lax.ppermute(value, axis, [(i, i ^ distance) for i in range(lax.axis_size...]
    ppermute x9 -> x46, waiting for transfers between devices: 67.8 us -> 46.6 us  [swap(): lax.ppermute(value, axis, [(i, i ^ distance) for i in range(lax.axis_size...]
    pallas_call x0 -> x8, Pallas kernels: none -> 18.5 us  [the longest x2 12.9 us: product(): pl.pallas_call(functools.partial(product_kernel, owners), grid_spec=pltpu...]
    add x8 -> x1, other arithmetic: 14.2 us -> 0.01 us  [per_device(): sums + swap(sums, 'tp', 1) + swap(sums, 'tp', 2) + swap(sums, 'tp', 3)]
    dot_general x1 -> x0, matrix products: 13.1 us -> none  [per_device(): lax.dot_general(lax.all_gather(inputs, 'tp', axis=0, tiled=True), cotange...]
    reduce_sum x3 -> x0, other arithmetic: 10.8 us -> none  [combine_level(): jnp.sum(lower_part * lower_part)]
  transfers between devices with their start and end apart: 11 -> 46, of which waited for: 11 -> 18; matrix products, arithmetic and copies ran while one was open for 0% -> 5% of each run, Pallas kernels for 0% -> 8%
where the time goes in v1:
time: 158 us
  starting transfers between devices  72.3 us (46%)
  waiting for transfers between devices  46.6 us (29%)
  Pallas kernels  18.5 us (12%)
  local copies, waits for them, and re-layouts  17.7 us (11%)
    ppermute x46, starting transfers between devices, swap(): lax.ppermute(value, axis, [(i, i ^ distance) for i in range(lax.axis_size...  72.3 us
    ppermute x46, waiting for transfers between devices, swap(): lax.ppermute(value, axis, [(i, i ^ distance) for i in range(lax.axis_size...  46.6 us
    pallas_call x2, Pallas kernels, product(): pl.pallas_call(functools.partial(product_kernel, owners), grid_spec=pltpu...  12.9 us
    unnamed x32, local copies, waits for them, and re-layouts  10.7 us
    slice x4, local copies, waits for them, and re-layouts, spread_halves(): far[:h]  3.42 us
    slice x4, local copies, waits for them, and re-layouts, spread_halves(): near[h:]  3.4 us
  transfers between devices with their start and end apart: 46, of which 18 were waited for; matrix products, arithmetic and copies ran while one was open for 5% of the time, Pallas kernels for 8%

profile of v1, /device:TPU:1, one launch (start us, length us, event | category | flops | bytes accessed | tf_op | source)
XLA Modules:
  0.0 157.6 jit_solution(6674521200981187117)
XLA Ops:
  8.1 2.2 %collective-permute-start.8 = (bf16[512,256]{1,0:T(8,128)(2,1)S(1)}, bf16[512,256]{1,0:T(8,128)(2,1)S(1)}, u32[]{:S(2)}, u32[]{:S(2)}) collective-permute-start(bf16[512,256]{1,0:T(8,128)(2,1)S(1)} %get-tuple-element.21), channel_id=1, source_target_pairs={{0,3},{1,2},{2,1},{3,0},{4,7},{5,6},{6,5},{7,4},{8,11},{9,10},{10,... | collective-permute-start | bytes 786440 | tf_op jit(solution)/shard_map/ppermute | solution.py:30
  10.4 3.2 %collective-permute-start.9 = (bf16[512,256]{1,0:T(8,128)(2,1)S(1)}, bf16[512,256]{1,0:T(8,128)(2,1)S(1)}, u32[]{:S(2)}, u32[]{:S(2)}) collective-permute-start(bf16[512,256]{1,0:T(8,128)(2,1)S(1)} %get-tuple-element.21), channel_id=1, source_target_pairs={{0,2},{1,3},{2,0},{3,1},{4,6},{5,7},{6,4},{7,5},{8,10},{9,11},{10,... | collective-permute-start | bytes 786440 | tf_op jit(solution)/shard_map/ppermute | solution.py:30
  13.6 2.4 %collective-permute-done.1 = bf16[512,256]{1,0:T(8,128)(2,1)S(1)} collective-permute-done((bf16[512,256]{1,0:T(8,128)(2,1)S(1)}, bf16[512,256]{1,0:T(8,128)(2,1)S(1)}, u32[]{:S(2)}, u32[]{:S(2)}) %collective-permute-start.1) | collective-permute-done | bytes 262176 | tf_op jit(solution)/shard_map/ppermute | solution.py:30
  17.9 3.8 %collective-permute-start.16 = (bf16[4,256,256]{2,1,0:T(8,128)(2,1)S(1)}, bf16[4,256,256]{2,1,0:T(8,128)(2,1)S(1)}, u32[]{:S(2)}, u32[]{:S(2)}) collective-permute-start(bf16[4,256,256]{2,1,0:T(8,128)(2,1)S(1)} %pad_maximum_fusion.2.refs_0_), channel_id=1, source_target_pairs={{0,3},{1,2},{2,1},{3,0},{4,7},{5,6},{6,5},{7,4},{8,11},{9,10},{10,... | collective-permute-start | bytes 1572872 | tf_op jit(solution)/shard_map/ppermute | solution.py:30
  25.2 8.8 %collective-permute-done.16.refs_2_ = bf16[4,256,256]{2,1,0:T(8,128)(2,1)S(1)} collective-permute-done((bf16[4,256,256]{2,1,0:T(8,128)(2,1)S(1)}, bf16[4,256,256]{2,1,0:T(8,128)(2,1)S(1)}, u32[]{:S(2)}, u32[]{:S(2)}) %collective-permute-start.16) | collective-permute-done | bytes 524320 | tf_op jit(solution)/shard_map/ppermute | solution.py:30
  40.5 5.4 %collective-permute-done.11.refs_7_ = bf16[4,256,256]{2,1,0:T(8,128)(2,1)S(1)} collective-permute-done((bf16[4,256,256]{2,1,0:T(8,128)(2,1)S(1)}, bf16[4,256,256]{2,1,0:T(8,128)(2,1)S(1)}, u32[]{:S(2)}, u32[]{:S(2)}) %collective-permute-start.11) | collective-permute-done | bytes 524320 | tf_op jit(solution)/shard_map/ppermute | solution.py:30
  45.9 2.5 %collective-permute-done.10.refs_6_ = bf16[4,256,256]{2,1,0:T(8,128)(2,1)S(1)} collective-permute-done((bf16[4,256,256]{2,1,0:T(8,128)(2,1)S(1)}, bf16[4,256,256]{2,1,0:T(8,128)(2,1)S(1)}, u32[]{:S(2)}, u32[]{:S(2)}) %collective-permute-start.10) | collective-permute-done | bytes 524320 | tf_op jit(solution)/shard_map/ppermute | solution.py:30
  57.8 3.4 %copy-done = bf16[4096,1024]{1,0:T(8,128)(2,1)S(1)} copy-done((bf16[4096,1024]{1,0:T(8,128)(2,1)S(1)}, bf16[4096,1024]{1,0:T(8,128)(2,1)}, u32[]{:S(2)}) %copy-start) | copy-done | bytes 8388632
  63.2 6.6 %shard_map.94 = (f32[136,1024]{1,0:T(8,128)S(1)}, f32[136,1024]{1,0:T(8,128)S(1)}, f32[136,1024]{1,0:T(8,128)S(1)}, f32[136,1024]{1,0:T(8,128)S(1)}) custom-call(s32[1]{0:T(128)} %bitcast._, bf16[4,256,256]{2,1,0:T(8,128)(2,1)S(1)} %pad_maximum_fusion.2.refs_0_, bf16[4,256,256]{2,1,0:T(8,128)(2,1)S(1)} %collective-permute-done.15.refs_1_, ...), custom_call_target="tpu_custom_call" | custom-call | flops 4294967296 | bytes 12582912 | tf_op jit(solution)/shard_map/pallas_call | solution.py:124
  69.8 2.8 %collective-permute-start.27 = (f16[136,1024]{1,0:T(8,128)(2,1)S(1)}, f16[136,1024]{1,0:T(8,128)(2,1)S(1)}, u32[]{:S(2)}, u32[]{:S(2)}) collective-permute-start(f16[136,1024]{1,0:T(8,128)(2,1)S(1)} %convert_element_type.52), channel_id=1, source_target_pairs={{0,96},{16,112},{32,64},{48,80},{64,32},{80,48},{96,0},{112,16},{1... | collective-permute-start | bytes 835592 | tf_op jit(solution)/shard_map/ppermute | solution.py:30
  72.7 5.8 %collective-permute-start.26 = (f16[136,1024]{1,0:T(8,128)(2,1)S(1)}, f16[136,1024]{1,0:T(8,128)(2,1)S(1)}, u32[]{:S(2)}, u32[]{:S(2)}) collective-permute-start(f16[136,1024]{1,0:T(8,128)(2,1)S(1)} %convert_element_type.50), channel_id=1, source_target_pairs={{0,80},{16,64},{32,112},{48,96},{64,16},{80,0},{96,48},{112,32},{1... | collective-permute-start | bytes 835592 | tf_op jit(solution)/shard_map/ppermute | solution.py:30
  78.5 3.4 %copy-done.1 = bf16[4096,1024]{1,0:T(8,128)(2,1)S(1)} copy-done((bf16[4096,1024]{1,0:T(8,128)(2,1)S(1)}, bf16[4096,1024]{1,0:T(8,128)(2,1)}, u32[]{:S(2)}) %copy-start.1) | copy-done | bytes 8388632
  81.9 6.3 %shard_map.93 = (f32[136,1024]{1,0:T(8,128)S(1)}, f32[136,1024]{1,0:T(8,128)S(1)}, f32[136,1024]{1,0:T(8,128)S(1)}, f32[128,1024]{1,0:T(8,128)S(1)}) custom-call(s32[1]{0:T(128)} %bitcast._, bf16[4,256,256]{2,1,0:T(8,128)(2,1)S(1)} %pad_maximum_fusion.refs_0_, bf16[4,256,256]{2,1,0:T(8,128)(2,1)} %collective-permute-done.3.refs_1_, ...), custom_call_target="tpu_custom_call" | custom-call | flops 4294967296 | bytes 12582912 | tf_op jit(solution)/shard_map/pallas_call | solution.py:124
  88.4 2.7 %collective-permute-start.25 = (f16[136,1024]{1,0:T(8,128)(2,1)S(1)}, f16[136,1024]{1,0:T(8,128)(2,1)S(1)}, u32[]{:S(2)}, u32[]{:S(2)}) collective-permute-start(f16[136,1024]{1,0:T(8,128)(2,1)S(1)} %convert_element_type.48), channel_id=1, source_target_pairs={{0,64},{16,80},{32,96},{48,112},{64,0},{80,16},{96,32},{112,48},{1... | collective-permute-start | bytes 835592 | tf_op jit(solution)/shard_map/ppermute | solution.py:30
  93.9 9.7 %collective-permute-done.28 = f16[136,1024]{1,0:T(8,128)(2,1)S(1)} collective-permute-done((f16[136,1024]{1,0:T(8,128)(2,1)S(1)}, f16[136,1024]{1,0:T(8,128)(2,1)S(1)}, u32[]{:S(2)}, u32[]{:S(2)}) %collective-permute-start.28) | collective-permute-done | bytes 278560 | tf_op jit(solution)/shard_map/ppermute | solution.py:30
  105.6 3.9 %collective-permute-done.23 = f16[136,1024]{1,0:T(8,128)(2,1)S(1)} collective-permute-done((f16[136,1024]{1,0:T(8,128)(2,1)S(1)}, f16[136,1024]{1,0:T(8,128)(2,1)S(1)}, u32[]{:S(2)}, u32[]{:S(2)}) %collective-permute-start.23) | collective-permute-done | bytes 278560 | tf_op jit(solution)/shard_map/ppermute | solution.py:30
  115.2 2.3 %collective-permute-start.32 = (f32[40,128]{1,0:T(8,128)S(1)}, f32[40,128]{1,0:T(8,128)S(1)}, u32[]{:S(2)}, u32[]{:S(2)}) collective-permute-start(f32[40,128]{1,0:T(8,128)S(1)} %shard_map.96.own), channel_id=1, source_target_pairs={{0,96},{16,112},{32,64},{48,80},{64,32},{80,48},{96,0},{112,16},{1... | collective-permute-start | bytes 61448 | tf_op jit(solution)/shard_map/ppermute | solution.py:30
  126.1 3.1 %collective-permute-start.37 = (f32[40,128]{1,0:T(8,128)S(1)}, f32[40,128]{1,0:T(8,128)S(1)}, u32[]{:S(2)}, u32[]{:S(2)}) collective-permute-start(f32[40,128]{1,0:T(8,128)S(1)} %add_add_fusion.refs_0_), channel_id=1, source_target_pairs={{0,8},{1,9},{2,10},{3,11},{4,12},{5,13},{6,14},{7,15},{8,0},{9,1},... | collective-permute-start | bytes 61448 | tf_op jit(solution)/shard_map/ppermute | solution.py:30
  130.5 2.5 %collective-permute-done.38.refs_3_ = f32[40,128]{1,0:T(8,128)S(1)} collective-permute-done((f32[40,128]{1,0:T(8,128)S(1)}, f32[40,128]{1,0:T(8,128)S(1)}, u32[]{:S(2)}, u32[]{:S(2)}) %collective-permute-start.38) | collective-permute-done | bytes 20512 | tf_op jit(solution)/shard_map/ppermute | solution.py:30
  133.0 2.6 %shard_map.98 = (f32[128,1024]{1,0:T(8,128)}, f32[128,1024]{1,0:T(8,128)}, f32[128,1024]{1,0:T(8,128)}, f32[128,1024]{1,0:T(8,128)}, bf16[128,1024]{1,0:T(8,128)(2,1)S(1)}) custom-call(f32[40,128]{1,0:T(8,128)S(1)} %add_add_fusion.refs_0_, f32[40,128]{1,0:T(8,128)S(1)} %collective-permute-done.36.refs_1_, f32[40,128]{1,0:T(8,128)S(1)} %collective-permute-done.37.refs_2_, ...), custom_call_target="tpu_custom_call" | custom-call | tf_op jit(solution)/shard_map/pallas_call | solution.py:261
  135.6 3.3 %collective-permute-start.42 = (bf16[128,1024]{1,0:T(8,128)(2,1)S(1)}, bf16[128,1024]{1,0:T(8,128)(2,1)S(1)}, u32[]{:S(2)}, u32[]{:S(2)}) collective-permute-start(bf16[128,1024]{1,0:T(8,128)(2,1)S(1)} %get-tuple-element.34.refs_0_), channel_id=1, source_target_pairs={{0,64},{16,80},{32,96},{48,112},{64,0},{80,16},{96,32},{112,48},{1... | collective-permute-start | bytes 786440 | tf_op jit(solution)/shard_map/ppermute | solution.py:30
  139.4 6.1 %collective-permute-start.39 = (bf16[128,1024]{1,0:T(8,128)(2,1)S(1)}, bf16[128,1024]{1,0:T(8,128)(2,1)S(1)}, u32[]{:S(2)}, u32[]{:S(2)}) collective-permute-start(bf16[128,1024]{1,0:T(8,128)(2,1)S(1)} %get-tuple-element.34.refs_0_), channel_id=1, source_target_pairs={{0,16},{16,0},{32,48},{48,32},{64,80},{80,64},{96,112},{112,96},{1... | collective-permute-start | bytes 786440 | tf_op jit(solution)/shard_map/ppermute | solution.py:30
  147.2 5.0 %collective-permute-start.43 = (bf16[128,1024]{1,0:T(8,128)(2,1)S(1)}, bf16[128,1024]{1,0:T(8,128)(2,1)S(1)}, u32[]{:S(2)}, u32[]{:S(2)}) collective-permute-start(bf16[128,1024]{1,0:T(8,128)(2,1)S(1)} %collective-permute-done.42.refs_4_), channel_id=1, source_target_pairs={{0,16},{16,0},{32,48},{48,32},{64,80},{80,64},{96,112},{112,96},{1... | collective-permute-start | bytes 786440 | tf_op jit(solution)/shard_map/ppermute | solution.py:30
  152.2 2.7 %collective-permute-start.45 = (bf16[128,1024]{1,0:T(8,128)(2,1)S(1)}, bf16[128,1024]{1,0:T(8,128)(2,1)S(1)}, u32[]{:S(2)}, u32[]{:S(2)}) collective-permute-start(bf16[128,1024]{1,0:T(8,128)(2,1)S(1)} %collective-permute-done.44.refs_6_), channel_id=1, source_target_pairs={{0,16},{16,0},{32,48},{48,32},{64,80},{80,64},{96,112},{112,96},{1... | collective-permute-start | bytes 786440 | tf_op jit(solution)/shard_map/ppermute | solution.py:30
  (156 shorter events, 56.1 us)
Async XLA Ops:
  6.4 15.3 %collective-permute-start.7 = (bf16[512,256]{1,0:T(8,128)(2,1)S(1)}, bf16[512,256]{1,0:T(8,128)(2,1)S(1)}, u32[]{:S(2)}, u32[]{:S(2)}) collective-permute-start(bf16[512,256]{1,0:T(8,128)(2,1)S(1)} %get-tuple-element.21), channel_id=1, source_target_pairs={{0,1},{1,0},{2,3},{3,2},{4,5},{5,4},{6,7},{7,6},{8,9},{9,8},{10,11... | collective-permute-start | bytes 786440 | tf_op jit(solution)/shard_map/ppermute | solution.py:30
  8.1 13.7 %collective-permute-start.8 = (bf16[512,256]{1,0:T(8,128)(2,1)S(1)}, bf16[512,256]{1,0:T(8,128)(2,1)S(1)}, u32[]{:S(2)}, u32[]{:S(2)}) collective-permute-start(bf16[512,256]{1,0:T(8,128)(2,1)S(1)} %get-tuple-element.21), channel_id=1, source_target_pairs={{0,3},{1,2},{2,1},{3,0},{4,7},{5,6},{6,5},{7,4},{8,11},{9,10},{10,... | collective-permute-start | bytes 786440 | tf_op jit(solution)/shard_map/ppermute | solution.py:30
  17.9 16.0 %collective-permute-start.16 = (bf16[4,256,256]{2,1,0:T(8,128)(2,1)S(1)}, bf16[4,256,256]{2,1,0:T(8,128)(2,1)S(1)}, u32[]{:S(2)}, u32[]{:S(2)}) collective-permute-start(bf16[4,256,256]{2,1,0:T(8,128)(2,1)S(1)} %pad_maximum_fusion.2.refs_0_), channel_id=1, source_target_pairs={{0,3},{1,2},{2,1},{3,0},{4,7},{5,6},{6,5},{7,4},{8,11},{9,10},{10,... | collective-permute-start | bytes 1572872 | tf_op jit(solution)/shard_map/ppermute | solution.py:30
  21.8 14.0 %collective-permute-start.15 = (bf16[4,256,256]{2,1,0:T(8,128)(2,1)S(1)}, bf16[4,256,256]{2,1,0:T(8,128)(2,1)S(1)}, u32[]{:S(2)}, u32[]{:S(2)}) collective-permute-start(bf16[4,256,256]{2,1,0:T(8,128)(2,1)S(1)} %pad_maximum_fusion.2.refs_0_), channel_id=1, source_target_pairs={{0,1},{1,0},{2,3},{3,2},{4,5},{5,4},{6,7},{7,6},{8,9},{9,8},{10,11... | collective-permute-start | bytes 1572872 | tf_op jit(solution)/shard_map/ppermute | solution.py:30
  22.2 14.0 %collective-permute-start.20 = (bf16[4,256,256]{2,1,0:T(8,128)(2,1)S(1)}, bf16[4,256,256]{2,1,0:T(8,128)(2,1)S(1)}, u32[]{:S(2)}, u32[]{:S(2)}) collective-permute-start(bf16[4,256,256]{2,1,0:T(8,128)(2,1)S(1)} %pad_maximum_fusion.3.refs_5_), channel_id=1, source_target_pairs={{0,12},{1,13},{2,14},{3,15},{4,8},{5,9},{6,10},{7,11},{8,4},{9,5},... | collective-permute-start | bytes 1572872 | tf_op jit(solution)/shard_map/ppermute | solution.py:30
  24.1 14.3 %collective-permute-start.19 = (bf16[4,256,256]{2,1,0:T(8,128)(2,1)S(1)}, bf16[4,256,256]{2,1,0:T(8,128)(2,1)S(1)}, u32[]{:S(2)}, u32[]{:S(2)}) collective-permute-start(bf16[4,256,256]{2,1,0:T(8,128)(2,1)S(1)} %pad_maximum_fusion.3.refs_5_), channel_id=1, source_target_pairs={{0,4},{1,5},{2,6},{3,7},{4,0},{5,1},{6,2},{7,3},{8,12},{9,13},{10,... | collective-permute-start | bytes 1572872 | tf_op jit(solution)/shard_map/ppermute | solution.py:30
  24.1 21.7 %collective-permute-start.11 = (bf16[4,256,256]{2,1,0:T(8,128)(2,1)S(1)}, bf16[4,256,256]{2,1,0:T(8,128)(2,1)S(1)}, u32[]{:S(2)}, u32[]{:S(2)}) collective-permute-start(bf16[4,256,256]{2,1,0:T(8,128)(2,1)S(1)} %pad_maximum_fusion.1.refs_5_), channel_id=1, source_target_pairs={{0,12},{1,13},{2,14},{3,15},{4,8},{5,9},{6,10},{7,11},{8,4},{9,5},... | collective-permute-start | bytes 1572872 | tf_op jit(solution)/shard_map/ppermute | solution.py:30
  34.0 14.4 %collective-permute-start.10 = (bf16[4,256,256]{2,1,0:T(8,128)(2,1)S(1)}, bf16[4,256,256]{2,1,0:T(8,128)(2,1)S(1)}, u32[]{:S(2)}, u32[]{:S(2)}) collective-permute-start(bf16[4,256,256]{2,1,0:T(8,128)(2,1)S(1)} %pad_maximum_fusion.1.refs_5_), channel_id=1, source_target_pairs={{0,4},{1,5},{2,6},{3,7},{4,0},{5,1},{6,2},{7,3},{8,12},{9,13},{10,... | collective-permute-start | bytes 1572872 | tf_op jit(solution)/shard_map/ppermute | solution.py:30
  35.7 13.8 %collective-permute-start.4 = (bf16[4,256,256]{2,1,0:T(8,128)(2,1)S(1)}, bf16[4,256,256]{2,1,0:T(8,128)(2,1)S(1)}, u32[]{:S(2)}, u32[]{:S(2)}) collective-permute-start(bf16[4,256,256]{2,1,0:T(8,128)(2,1)S(1)} %pad_maximum_fusion.refs_0_), channel_id=1, source_target_pairs={{0,3},{1,2},{2,1},{3,0},{4,7},{5,6},{6,5},{7,4},{8,11},{9,10},{10,... | collective-permute-start | bytes 1572872 | tf_op jit(solution)/shard_map/ppermute | solution.py:30
  36.2 17.8 %collective-permute-start.3 = (bf16[4,256,256]{2,1,0:T(8,128)(2,1)S(1)}, bf16[4,256,256]{2,1,0:T(8,128)(2,1)}, u32[]{:S(2)}, u32[]{:S(2)}) collective-permute-start(bf16[4,256,256]{2,1,0:T(8,128)(2,1)S(1)} %pad_maximum_fusion.refs_0_), channel_id=1, source_target_pairs={{0,1},{1,0},{2,3},{3,2},{4,5},{5,4},{6,7},{7,6},{8,9},{9,8},{10,11... | collective-permute-start | bytes 1572872 | tf_op jit(solution)/shard_map/ppermute | solution.py:30
  38.4 16.6 %collective-permute-start.17 = (bf16[2,256,256]{2,1,0:T(8,128)(2,1)}, bf16[2,256,256]{2,1,0:T(8,128)(2,1)S(1)}, u32[]{:S(2)}, u32[]{:S(2)}) collective-permute-start(bf16[2,256,256]{2,1,0:T(8,128)(2,1)} %slice.167), channel_id=1, source_target_pairs={{0,1},{1,0},{2,3},{3,2},{4,5},{5,4},{6,7},{7,6},{8,9},{9,8},{10,11... | collective-permute-start | bytes 786440 | tf_op jit(solution)/shard_map/ppermute | solution.py:30
  54.0 18.7 %collective-permute-start.12 = (bf16[2,256,256]{2,1,0:T(8,128)(2,1)S(1)}, bf16[2,256,256]{2,1,0:T(8,128)(2,1)S(1)}, u32[]{:S(2)}, u32[]{:S(2)}) collective-permute-start(bf16[2,256,256]{2,1,0:T(8,128)(2,1)S(1)} %slice.160), channel_id=1, source_target_pairs={{0,4},{1,5},{2,6},{3,7},{4,0},{5,1},{6,2},{7,3},{8,12},{9,13},{10,... | collective-permute-start | bytes 786440 | tf_op jit(solution)/shard_map/ppermute | solution.py:30
  55.0 23.4 %collective-permute-start.13 = (bf16[2,256,256]{2,1,0:T(8,128)(2,1)S(1)}, bf16[2,256,256]{2,1,0:T(8,128)(2,1)S(1)}, u32[]{:S(2)}, u32[]{:S(2)}) collective-permute-start(bf16[2,256,256]{2,1,0:T(8,128)(2,1)S(1)} %slice.161), channel_id=1, source_target_pairs={{0,12},{1,13},{2,14},{3,15},{4,8},{5,9},{6,10},{7,11},{8,4},{9,5},... | collective-permute-start | bytes 786440 | tf_op jit(solution)/shard_map/ppermute | solution.py:30
  57.1 21.4 %collective-permute-start.5 = (bf16[2,256,256]{2,1,0:T(8,128)(2,1)S(1)}, bf16[2,256,256]{2,1,0:T(8,128)(2,1)S(1)}, u32[]{:S(2)}, u32[]{:S(2)}) collective-permute-start(bf16[2,256,256]{2,1,0:T(8,128)(2,1)S(1)} %slice.155), channel_id=1, source_target_pairs={{0,1},{1,0},{2,3},{3,2},{4,5},{5,4},{6,7},{7,6},{8,9},{9,8},{10,11... | collective-permute-start | bytes 786440 | tf_op jit(solution)/shard_map/ppermute | solution.py:30
  57.3 21.2 %collective-permute-start.6 = (bf16[2,256,256]{2,1,0:T(8,128)(2,1)S(1)}, bf16[2,256,256]{2,1,0:T(8,128)(2,1)S(1)}, u32[]{:S(2)}, u32[]{:S(2)}) collective-permute-start(bf16[2,256,256]{2,1,0:T(8,128)(2,1)S(1)} %slice.156), channel_id=1, source_target_pairs={{0,3},{1,2},{2,1},{3,0},{4,7},{5,6},{6,5},{7,4},{8,11},{9,10},{10,... | collective-permute-start | bytes 786440 | tf_op jit(solution)/shard_map/ppermute | solution.py:30
  69.8 22.6 %collective-permute-start.27 = (f16[136,1024]{1,0:T(8,128)(2,1)S(1)}, f16[136,1024]{1,0:T(8,128)(2,1)S(1)}, u32[]{:S(2)}, u32[]{:S(2)}) collective-permute-start(f16[136,1024]{1,0:T(8,128)(2,1)S(1)} %convert_element_type.52), channel_id=1, source_target_pairs={{0,96},{16,112},{32,64},{48,80},{64,32},{80,48},{96,0},{112,16},{1... | collective-permute-start | bytes 835592 | tf_op jit(solution)/shard_map/ppermute | solution.py:30
  72.7 20.2 %collective-permute-start.26 = (f16[136,1024]{1,0:T(8,128)(2,1)S(1)}, f16[136,1024]{1,0:T(8,128)(2,1)S(1)}, u32[]{:S(2)}, u32[]{:S(2)}) collective-permute-start(f16[136,1024]{1,0:T(8,128)(2,1)S(1)} %convert_element_type.50), channel_id=1, source_target_pairs={{0,80},{16,64},{32,112},{48,96},{64,16},{80,0},{96,48},{112,32},{1... | collective-permute-start | bytes 835592 | tf_op jit(solution)/shard_map/ppermute | solution.py:30
  88.3 15.3 %collective-permute-start.28 = (f16[136,1024]{1,0:T(8,128)(2,1)S(1)}, f16[136,1024]{1,0:T(8,128)(2,1)S(1)}, u32[]{:S(2)}, u32[]{:S(2)}) collective-permute-start(f16[136,1024]{1,0:T(8,128)(2,1)S(1)} %convert_element_type.54), channel_id=1, source_target_pairs={{0,112},{16,96},{32,80},{48,64},{64,48},{80,32},{96,16},{112,0},{1... | collective-permute-start | bytes 835592 | tf_op jit(solution)/shard_map/ppermute | solution.py:30
  88.4 15.3 %collective-permute-start.25 = (f16[136,1024]{1,0:T(8,128)(2,1)S(1)}, f16[136,1024]{1,0:T(8,128)(2,1)S(1)}, u32[]{:S(2)}, u32[]{:S(2)}) collective-permute-start(f16[136,1024]{1,0:T(8,128)(2,1)S(1)} %convert_element_type.48), channel_id=1, source_target_pairs={{0,64},{16,80},{32,96},{48,112},{64,0},{80,16},{96,32},{112,48},{1... | collective-permute-start | bytes 835592 | tf_op jit(solution)/shard_map/ppermute | solution.py:30
  91.1 14.3 %collective-permute-start.24 = (f16[136,1024]{1,0:T(8,128)(2,1)S(1)}, f16[136,1024]{1,0:T(8,128)(2,1)S(1)}, u32[]{:S(2)}, u32[]{:S(2)}) collective-permute-start(f16[136,1024]{1,0:T(8,128)(2,1)S(1)} %convert_element_type.46), channel_id=1, source_target_pairs={{0,48},{16,32},{32,16},{48,0},{64,112},{80,96},{96,80},{112,64},{1... | collective-permute-start | bytes 835592 | tf_op jit(solution)/shard_map/ppermute | solution.py:30
  92.5 16.9 %collective-permute-start.23 = (f16[136,1024]{1,0:T(8,128)(2,1)S(1)}, f16[136,1024]{1,0:T(8,128)(2,1)S(1)}, u32[]{:S(2)}, u32[]{:S(2)}) collective-permute-start(f16[136,1024]{1,0:T(8,128)(2,1)S(1)} %convert_element_type.44), channel_id=1, source_target_pairs={{0,32},{16,48},{32,0},{48,16},{64,96},{80,112},{96,64},{112,80},{1... | collective-permute-start | bytes 835592 | tf_op jit(solution)/shard_map/ppermute | solution.py:30
  92.9 16.7 %collective-permute-start.14 = (f16[136,1024]{1,0:T(8,128)(2,1)S(1)}, f16[136,1024]{1,0:T(8,128)(2,1)S(1)}, u32[]{:S(2)}, u32[]{:S(2)}) collective-permute-start(f16[136,1024]{1,0:T(8,128)(2,1)S(1)} %convert_element_type.42), channel_id=1, source_target_pairs={{0,16},{16,0},{32,48},{48,32},{64,80},{80,64},{96,112},{112,96},{1... | collective-permute-start | bytes 835592 | tf_op jit(solution)/shard_map/ppermute | solution.py:30
  138.9 13.3 %collective-permute-start.44 = (bf16[128,1024]{1,0:T(8,128)(2,1)S(1)}, bf16[128,1024]{1,0:T(8,128)(2,1)S(1)}, u32[]{:S(2)}, u32[]{:S(2)}) collective-permute-start(bf16[128,1024]{1,0:T(8,128)(2,1)S(1)} %get-tuple-element.34.refs_0_), channel_id=1, source_target_pairs={{0,96},{16,112},{32,64},{48,80},{64,32},{80,48},{96,0},{112,16},{1... | collective-permute-start | bytes 786440 | tf_op jit(solution)/shard_map/ppermute | solution.py:30
  139.4 15.5 %collective-permute-start.39 = (bf16[128,1024]{1,0:T(8,128)(2,1)S(1)}, bf16[128,1024]{1,0:T(8,128)(2,1)S(1)}, u32[]{:S(2)}, u32[]{:S(2)}) collective-permute-start(bf16[128,1024]{1,0:T(8,128)(2,1)S(1)} %get-tuple-element.34.refs_0_), channel_id=1, source_target_pairs={{0,16},{16,0},{32,48},{48,32},{64,80},{80,64},{96,112},{112,96},{1... | collective-permute-start | bytes 786440 | tf_op jit(solution)/shard_map/ppermute | solution.py:30
  (38 other events, 359.1 us)

commit v2 on v1

--- a/solution.py
+++ b/solution.py
@@ -55,51 +55,88 @@
     )(rep, x)
 
 
+def after(value, *others):
+    return lax.optimization_barrier((value, *others))[0]
+
+
 def spread(own, axis_step):
     return [own] + [swap(own, "tp", axis_step * d) for d in RING[1:]]
 
 
-def spread_halves(own, axis_step):
-    near = swap(own, "tp", axis_step)
-    far = swap(own, "tp", axis_step * 3)
-    h = own.shape[0] // 2
-    return [own, near, far, swap(far[:h], "tp", axis_step), swap(near[h:], "tp", axis_step * 3)]
-
-
-def product_kernel(owners, _, *refs):
-    a_refs, b_refs, g_refs = refs[:5], refs[5:10], refs[10:14]
-    outs, acc = refs[14:-1], refs[-1]
-    step = pl.program_id(0)
-
-    def piece(pieces, outer, inner):
-        if outer < 3:
-            return pieces[outer][inner]
-        return pieces[3 + inner // 2][inner % 2]
-
-    for z in range(4):
-
-        @pl.when(step == z)
-        def _():
-            left = jnp.concatenate(
-                [
-                    jnp.concatenate([piece(a_refs, z, x) for x in range(4)], axis=1),
-                    jnp.concatenate([piece(b_refs, x, z) for x in range(4)], axis=1),
-                ],
-                axis=0,
-            )
-            right = jnp.concatenate([g[...] for g in g_refs], axis=0)
-            part = jnp.dot(left, right, preferred_element_type=jnp.float32)
-            if z == 0:
-                acc[...] = part
-            else:
-                acc[...] += part
-
-    @pl.when(step == 3)
-    def _():
-        for i, (k, out) in enumerate(zip(owners, outs)):
-            block = acc[i * BLOCK : (i + 1) * BLOCK, :]
+def forward(near, far, axis_step):
+    h = near.shape[0] // 2
+    return [
+        swap(far[:h], "tp", axis_step),
+        swap(near[h:], "tp", axis_step * 3),
+    ]
+
+
+def slot(x, z):
+    return 4 * z + x
+
+
+def fetch(place, cotangent, buffer, sems, wanted):
+    rows = buffer.shape[1]
+    copies = {}
+    for x, z in wanted:
+        at = place ^ (4 * RING[x]) ^ RING[z]
+        source = cotangent.at[pl.ds(pl.multiple_of(at * rows, rows), rows), :]
+        i = slot(x, z)
+        copies[(x, z)] = pltpu.make_async_copy(source, buffer.at[i], sems.at[i])
+        copies[(x, z)].start()
+    return copies
+
+
+def line_product(pieces, blocks):
+    left = jnp.concatenate(pieces, axis=1)
+    right = jnp.concatenate(blocks, axis=0)
+    return jnp.dot(left, right, preferred_element_type=jnp.float32)
+
+
+def early_kernel(place_ref, *refs):
+    a_refs, b_refs, cotangent = refs[:3], refs[3:6], refs[6]
+    a_acc, b_acc, buffer, sems = refs[7:]
+    wanted = [(x, z) for z in range(4) for x in range(4) if (x, z) != (3, 3)]
+    copies = fetch(place_ref[0], cotangent, buffer, sems, wanted)
+    for z in range(3):
+        for x in range(4):
+            copies[(x, z)].wait()
+        part = line_product(
+            [a_refs[z][x] for x in range(4)], [buffer[slot(x, z)] for x in range(4)]
+        )
+        a_acc[...] = part if z == 0 else a_acc[...] + part
+    for x in range(3):
+        copies[(x, 3)].wait()
+    for x in range(3):
+        part = line_product(
+            [b_refs[x][z] for z in range(4)], [buffer[slot(x, z)] for z in range(4)]
+        )
+        b_acc[...] = part if x == 0 else b_acc[...] + part
+
+
+def late_kernel(owners, place_ref, *refs):
+    a_acc, b_acc, a_halves, b_halves, cotangent = refs[0], refs[1], refs[2:4], refs[4:6], refs[6]
+    outs, buffer, sems = refs[7:-2], refs[-2], refs[-1]
+    wanted = [(x, 3) for x in range(4)] + [(3, z) for z in range(3)]
+    copies = fetch(place_ref[0], cotangent, buffer, sems, wanted)
+    for half, (acc, halves, line) in enumerate(
+        (
+            (a_acc, a_halves, [(x, 3) for x in range(4)]),
+            (b_acc, b_halves, [(3, z) for z in range(4)]),
+        )
+    ):
+        for at in line:
+            if half == 0 or at != (3, 3):
+                copies[at].wait()
+        whole = acc[...] + line_product(
+            [halves[i // 2][i % 2] for i in range(4)], [buffer[slot(*at)] for at in line]
+        )
+        for i in range(2):
+            k, out = owners[2 * half + i], outs[2 * half + i]
+            block = whole[i * BLOCK : (i + 1) * BLOCK]
             if k == 0:
-                out[...] = block
+                out[:BLOCK, :] = block
+                out[BLOCK:, :] = jnp.zeros((EXTRA, block.shape[1]), jnp.float32)
                 continue
             top = jnp.max(jnp.max(jnp.abs(block), axis=0, keepdims=True), axis=1, keepdims=True)
             power = jnp.floor(15.0 - jnp.log2(jnp.maximum(top, 1e-30)))
@@ -107,42 +144,56 @@
             out[BLOCK:, :] = jnp.broadcast_to(power, (EXTRA, block.shape[1]))
 
 
-def product(owners, place, a_pieces, b_pieces, cotangent):
+HBM = pl.BlockSpec(memory_space=pltpu.HBM)
+
+
+def product_scratch(cotangent):
     tokens, columns = cotangent.shape
-    rows = tokens // 16
-    features = BLOCK * len(owners)
-
-    def g_spec(x):
-        return pl.BlockSpec(
-            (rows, columns), lambda s, p: (p[0] ^ (4 * RING[x]) ^ s ^ (s >> 1), 0)
-        )
-
-    shapes = [
-        jax.ShapeDtypeStruct((BLOCK if k == 0 else BLOCK + EXTRA, columns), jnp.float32)
-        for k in owners
+    return [
+        pltpu.VMEM((16, tokens // 16, columns), cotangent.dtype),
+        pltpu.SemaphoreType.DMA((16,)),
     ]
-    return pl.pallas_call(
-        functools.partial(product_kernel, owners),
-        grid_spec=pltpu.PrefetchScalarGridSpec(
-            num_scalar_prefetch=1,
-            grid=(4,),
-            in_specs=[WHOLE] * 10 + [g_spec(x) for x in range(4)],
-            out_specs=[WHOLE] * len(owners),
-            scratch_shapes=[pltpu.VMEM((features, columns), jnp.float32)],
-        ),
-        out_shape=shapes,
-        compiler_params=pltpu.CompilerParams(vmem_limit_bytes=28 * MIB),
+
+
+def early_product(place, a_pieces, b_pieces, cotangent):
+    tokens, columns = cotangent.shape
+    features = a_pieces[0].shape[1]
+    return pl.pallas_call(
+        early_kernel,
+        out_shape=[jax.ShapeDtypeStruct((features, columns), jnp.float32)] * 2,
+        in_specs=[SMEM] + [WHOLE] * 6 + [HBM],
+        out_specs=[WHOLE] * 2,
+        scratch_shapes=product_scratch(cotangent),
+        compiler_params=pltpu.CompilerParams(vmem_limit_bytes=24 * MIB),
         cost_estimate=pl.CostEstimate(
-            flops=2 * tokens * columns * features,
-            bytes_accessed=2 * tokens * columns + 2 * tokens * features,
+            flops=3 * tokens * columns * features,
+            bytes_accessed=2 * tokens * columns,
             transcendentals=0,
         ),
-    )(place, *a_pieces, *b_pieces, *[cotangent] * 4)
+    )(place, *a_pieces, *b_pieces, cotangent)
+
+
+def late_product(owners, place, sums, a_halves, b_halves, cotangent):
+    tokens, columns = cotangent.shape
+    features = a_halves[0].shape[1]
+    return pl.pallas_call(
+        functools.partial(late_kernel, owners),
+        out_shape=[jax.ShapeDtypeStruct((BLOCK + EXTRA, columns), jnp.float32)] * 4,
+        in_specs=[SMEM] + [WHOLE] * 6 + [HBM],
+        out_specs=[WHOLE] * 4,
+        scratch_shapes=product_scratch(cotangent),
+        compiler_params=pltpu.CompilerParams(vmem_limit_bytes=24 * MIB),
+        cost_estimate=pl.CostEstimate(
+            flops=tokens * columns * features,
+            bytes_accessed=tokens * columns,
+            transcendentals=0,
+        ),
+    )(place, *sums, *a_halves, *b_halves, cotangent)
 
 
 def gram_kernel(*refs):
     blocks, out = refs[:8], refs[8]
-    rows, columns = blocks[0].shape
+    rows, columns = BLOCK, blocks[0].shape[1]
     lanes = 128
     sums = tuple(jnp.zeros((8, lanes), jnp.float32) for _ in PAIRS)
 
@@ -155,8 +206,9 @@
 
     sums = lax.fori_loop(0, rows // 8, body, sums)
     out[...] = jnp.zeros_like(out)
-    for row, total in enumerate(sums):
-        out[row : row + 1, :] = jnp.sum(total, axis=0, keepdims=True)
+    scale = [jnp.exp2(-b[rows : rows + 1, :lanes]) for b in blocks]
+    for row, (total, (k, l)) in enumerate(zip(sums, PAIRS)):
+        out[row : row + 1, :] = jnp.sum(total, axis=0, keepdims=True) * scale[k] * scale[l]
 
 
 def gram(blocks):
@@ -232,8 +284,8 @@
     combined_out, moment_out, second_out, master_out, weights_out, coef = refs[15:]
     total = sums[0][...] + sums[1][...] + sums[2][...] + sums[3][...]
     for k, c in enumerate(coefficients(total)):
-        coef[k : k + 1, :] = jnp.broadcast_to(c, (1, 128))
-    rows, columns = blocks[0].shape
+        coef[k : k + 1, :] = c * jnp.exp2(-blocks[k][BLOCK : BLOCK + 1, :128])
+    rows = BLOCK
     scale = [coef[k : k + 1, 0:1] for k in range(8)]
 
     def body(i, carry):
@@ -268,62 +320,76 @@
     )(*sums, *blocks, master, moment, second)
 
 
+CHIPS = (4, 2, 6)
+
+
 def place_kernel(rep_ref, *refs):
-    parts, out, sems = refs[:8], refs[8], refs[9]
+    mine, other, far, swapped, out, sems = refs[:2] + (refs[2:5],) + refs[5:]
     rep = rep_ref[0]
+    parts = {0: mine, 1: other}
+    for i, k in enumerate(CHIPS):
+        parts[k] = far[i]
+        parts[k ^ 1] = swapped.at[pl.ds(i * BLOCK, BLOCK), :]
     copies = []
-    for k, part in enumerate(parts):
+    for k, part in parts.items():
         at = pl.ds(pl.multiple_of((rep ^ k) * BLOCK, BLOCK), BLOCK)
         copies.append(pltpu.make_async_copy(part, out.at[at, :], sems.at[k]))
-    for copy in copies:
-        copy.start()
+        copies[-1].start()
     for copy in copies:
         copy.wait()
 
 
-def assemble(rep, parts):
-    rows, columns = parts[0].shape
+def assemble(rep, mine):
+    rows, columns = mine.shape
     anywhere = pl.BlockSpec(memory_space=pl.ANY)
+    far = [swap(mine, "rep", k) for k in CHIPS]
+    other = swap(mine, "rep", 1)
+    swapped = swap(after(jnp.concatenate(far), other), "rep", 1)
     return pl.pallas_call(
         place_kernel,
-        out_shape=jax.ShapeDtypeStruct((8 * rows, columns), parts[0].dtype),
-        in_specs=[SMEM] + [anywhere] * 8,
+        out_shape=jax.ShapeDtypeStruct((8 * rows, columns), mine.dtype),
+        in_specs=[SMEM] + [anywhere] * 6,
         out_specs=anywhere,
         scratch_shapes=[pltpu.SemaphoreType.DMA((8,))],
         compiler_params=pltpu.CompilerParams(vmem_limit_bytes=1 * MIB),
-    )(rep, *parts)
+    )(rep, mine, other, *far, swapped)
 
 
 def per_device(inputs, cotangent, master, moment, second):
+    cotangent = pltpu.with_memory_space_constraint(cotangent, pltpu.HBM)
     rep = lax.axis_index("rep").astype(jnp.int32).reshape((1,))
     place = lax.axis_index("tp").astype(jnp.int32).reshape((1,))
     a, b = turn(rep, inputs)
     a_line = spread(a, 4)
     b_line = spread(b, 1)
     blocks = [None] * 8
+    before, done = [], []
     for i, (a_owners, b_owners) in enumerate(CHUNKS):
         rows = slice(i * 2 * BLOCK, (i + 1) * 2 * BLOCK)
-        a_pieces = spread_halves(jnp.stack([piece[rows] for piece in a_line]), 1)
-        b_pieces = spread_halves(jnp.stack([piece[rows] for piece in b_line]), 4)
+        a_own = after(jnp.stack([piece[rows] for piece in a_line]), *before)
+        b_own = after(jnp.stack([piece[rows] for piece in b_line]), *before)
+        a_near, a_far = swap(a_own, "tp", 1), swap(a_own, "tp", 3)
+        b_near, b_far = swap(b_own, "tp", 4), swap(b_own, "tp", 12)
+        a_opposite = forward(after(a_near, *done), after(a_far, *done), 1)
+        b_opposite = forward(after(b_near, *done), after(b_far, *done), 4)
+        sums = early_product(
+            place, [a_own, a_near, a_far], [b_own, b_near, b_far], cotangent
+        )
+        before = [*a_opposite, *b_opposite, *sums]
         owners = a_owners + b_owners
-        for k, value in zip(owners, product(owners, place, a_pieces, b_pieces, cotangent)):
-            if k == 0:
-                blocks[k] = value
-                continue
-            got = swap(value.astype(jnp.float16), "rep", k).astype(jnp.float32)
-            blocks[k] = got[:BLOCK] * jnp.exp2(-got[BLOCK : BLOCK + 1])
+        values = late_product(owners, place, sums, a_opposite, b_opposite, cotangent)
+        for k, value in zip(owners, values):
+            if k:
+                done.append(value.astype(jnp.float16))
+                value = swap(done[-1], "rep", k).astype(jnp.float32)
+            blocks[k] = value
     sums = gram(blocks)
     sums = join(sums, (1,))
     sums = join(sums, (2, 4, 6))
     sums = sums + swap(sums, "tp", 1) + swap(sums, "tp", 2) + swap(sums, "tp", 3)
     sums = [sums] + [swap(sums, "tp", d) for d in (4, 8, 12)]
     combined, moment_new, second_new, master_new, mine = adam(sums, blocks, master, moment, second)
-    column = {0: mine, **{k: swap(mine, "rep", k) for k in (4, 2, 6)}}
-    parts = [None] * 8
-    for k, value in column.items():
-        parts[k] = value
-        parts[k ^ 1] = swap(value, "rep", 1)
-    weights = assemble(rep, parts)
+    weights = assemble(rep, mine)
     return (combined, moment_new, second_new, master_new, weights)
 
 

time: 158 us -> 138 us (0.87)
  local copies, waits for them, and re-layouts: 17.7 us -> 4.01 us
  starting transfers between devices: 72.3 us -> 66.3 us
  waiting for transfers between devices: 46.6 us -> 41.6 us
  Pallas kernels: 18.5 us -> 23.3 us
    unnamed x32 -> x10, local copies, waits for them, and re-layouts: 10.7 us -> 1.06 us
    slice x8, local copies, waits for them, and re-layouts: 6.82 us -> 0.14 us  [forward(): return [swap(far[:h], 'tp', axis_step), swap(near[h:], 'tp', axis_step * 3)]]
    ppermute x46 -> x44, starting transfers between devices: 72.3 us -> 66.3 us  [swap(): lax.ppermute(value, axis, [(i, i ^ distance) for i in range(lax.axis_size...]
    ppermute x46 -> x44, waiting for transfers between devices: 46.6 us -> 41.6 us  [swap(): lax.ppermute(value, axis, [(i, i ^ distance) for i in range(lax.axis_size...]
    pallas_call x2 -> x4, Pallas kernels: 12.9 us -> 17.6 us  [the longest x2 10.9 us: early_product(): pl.pallas_call(early_kernel, out_shape=[jax.ShapeDtypeStruct((features, c...]
    another operation x7, local copies, waits for them, and re-layouts: 0.14 us -> 2.81 us  [the longest x4 2.75 us: per_device(): b_own = after(jnp.stack([piece[rows] for piece in b_line]), *before)]
  transfers between devices with their start and end apart: 46 -> 44, of which waited for: 18 -> 19; matrix products, arithmetic and copies ran while one was open for 5% -> 4% of each run, Pallas kernels for 8% -> 13%
where the time goes in v2:
time: 138 us
  starting transfers between devices  66.3 us (48%)
  waiting for transfers between devices  41.6 us (30%)
  Pallas kernels  23.3 us (17%)
  local copies, waits for them, and re-layouts  4.01 us (3%)
  other arithmetic  1.94 us (1%)
    ppermute x44, starting transfers between devices, swap(): lax.ppermute(value, axis, [(i, i ^ distance) for i in range(lax.axis_size...  66.3 us
    ppermute x44, waiting for transfers between devices, swap(): lax.ppermute(value, axis, [(i, i ^ distance) for i in range(lax.axis_size...  41.6 us
    pallas_call x2, Pallas kernels, early_product(): pl.pallas_call(early_kernel, out_shape=[jax.ShapeDtypeStruct((features, c...  10.9 us
    pallas_call x2, Pallas kernels, late_product(): pl.pallas_call(functools.partial(late_kernel, owners), out_shape=[jax.Sha...  6.77 us
  transfers between devices with their start and end apart: 44, of which 19 were waited for; matrix products, arithmetic and copies ran while one was open for 4% of the time, Pallas kernels for 13%

profile of v2, /device:TPU:1, one launch (start us, length us, event | category | flops | bytes accessed | tf_op | source)
XLA Modules:
  0.0 138.3 jit_solution(14220290367718008408)
XLA Ops:
  1.9 2.5 %collective-permute-start.7 = (bf16[512,256]{1,0:T(8,128)(2,1)S(1)}, bf16[512,256]{1,0:T(8,128)(2,1)S(1)}, u32[]{:S(2)}, u32[]{:S(2)}) collective-permute-start(bf16[512,256]{1,0:T(8,128)(2,1)S(1)} %get-tuple-element.32), channel_id=1, source_target_pairs={{0,1},{1,0},{2,3},{3,2},{4,5},{5,4},{6,7},{7,6},{8,9},{9,8},{10,11... | collective-permute-start | bytes 786440 | tf_op jit(solution)/shard_map/ppermute | solution.py:30
  4.4 2.2 %collective-permute-start.8 = (bf16[512,256]{1,0:T(8,128)(2,1)S(1)}, bf16[512,256]{1,0:T(8,128)(2,1)S(1)}, u32[]{:S(2)}, u32[]{:S(2)}) collective-permute-start(bf16[512,256]{1,0:T(8,128)(2,1)S(1)} %get-tuple-element.32), channel_id=1, source_target_pairs={{0,3},{1,2},{2,1},{3,0},{4,7},{5,6},{6,5},{7,4},{8,11},{9,10},{10,... | collective-permute-start | bytes 786440 | tf_op jit(solution)/shard_map/ppermute | solution.py:30
  8.9 1.8 %collective-permute-start.1 = (bf16[512,256]{1,0:T(8,128)(2,1)S(1)}, bf16[512,256]{1,0:T(8,128)(2,1)S(1)}, u32[]{:S(2)}, u32[]{:S(2)}) collective-permute-start(bf16[512,256]{1,0:T(8,128)(2,1)S(1)} %get-tuple-element.31), channel_id=1, source_target_pairs={{0,12},{1,13},{2,14},{3,15},{4,8},{5,9},{6,10},{7,11},{8,4},{9,5},... | collective-permute-start | bytes 786440 | tf_op jit(solution)/shard_map/ppermute | solution.py:30
  13.7 3.0 %collective-permute-done.8 = bf16[512,256]{1,0:T(8,128)(2,1)S(1)} collective-permute-done((bf16[512,256]{1,0:T(8,128)(2,1)S(1)}, bf16[512,256]{1,0:T(8,128)(2,1)S(1)}, u32[]{:S(2)}, u32[]{:S(2)}) %collective-permute-start.8) | collective-permute-done | bytes 262176 | tf_op jit(solution)/shard_map/ppermute | solution.py:30
  19.8 2.6 %collective-permute-start.10 = (bf16[4,256,256]{2,1,0:T(8,128)(2,1)S(1)}, bf16[4,256,256]{2,1,0:T(8,128)(2,1)S(1)}, u32[]{:S(2)}, u32[]{:S(2)}) collective-permute-start(bf16[4,256,256]{2,1,0:T(8,128)(2,1)S(1)} %pad_maximum_fusion.3.refs_3_), channel_id=1, source_target_pairs={{0,12},{1,13},{2,14},{3,15},{4,8},{5,9},{6,10},{7,11},{8,4},{9,5},... | collective-permute-start | bytes 1572872 | tf_op jit(solution)/shard_map/ppermute | solution.py:30
  22.5 2.1 %collective-permute-start.3 = (bf16[4,256,256]{2,1,0:T(8,128)(2,1)S(1)}, bf16[4,256,256]{2,1,0:T(8,128)(2,1)S(1)}, u32[]{:S(2)}, u32[]{:S(2)}) collective-permute-start(bf16[4,256,256]{2,1,0:T(8,128)(2,1)S(1)} %pad_maximum_fusion.2.refs_0_), channel_id=1, source_target_pairs={{0,3},{1,2},{2,1},{3,0},{4,7},{5,6},{6,5},{7,4},{8,11},{9,10},{10,... | collective-permute-start | bytes 1572872 | tf_op jit(solution)/shard_map/ppermute | solution.py:30
  25.8 7.8 %collective-permute-done.10.refs_5_ = bf16[4,256,256]{2,1,0:T(8,128)(2,1)S(1)} collective-permute-done((bf16[4,256,256]{2,1,0:T(8,128)(2,1)S(1)}, bf16[4,256,256]{2,1,0:T(8,128)(2,1)S(1)}, u32[]{:S(2)}, u32[]{:S(2)}) %collective-permute-start.10) | collective-permute-done | bytes 524320 | tf_op jit(solution)/shard_map/ppermute | solution.py:30
  35.8 1.8 %collective-permute-start.6 = (bf16[2,256,256]{2,1,0:T(8,128)(2,1)S(1)}, bf16[2,256,256]{2,1,0:T(8,128)(2,1)S(1)}, u32[]{:S(2)}, u32[]{:S(2)}) collective-permute-start(bf16[2,256,256]{2,1,0:T(8,128)(2,1)S(1)} %slice.103), channel_id=1, source_target_pairs={{0,3},{1,2},{2,1},{3,0},{4,7},{5,6},{6,5},{7,4},{8,11},{9,10},{10,... | collective-permute-start | bytes 786440 | tf_op jit(solution)/shard_map/ppermute | solution.py:30
  37.7 5.4 %shard_map.93 = (f32[256,1024]{1,0:T(8,128)S(1)}, f32[256,1024]{1,0:T(8,128)S(1)}) custom-call(s32[1]{0:T(128)} %bitcast.place_ref, bf16[4,256,256]{2,1,0:T(8,128)(2,1)S(1)} %pad_maximum_fusion.2.refs_0_, bf16[4,256,256]{2,1,0:T(8,128)(2,1)S(1)} %collective-permute-done.5.refs_1_, bf16[4,256,256]{2,1,0:T(8,128)(2,1)S(1)} %collective-permute-done.3.refs_2_, ...), custom_call_target="tpu_custom_call" | custom-call | flops 3221225472 | bytes 8388608 | tf_op jit(solution)/shard_map/pallas_call | solution.py:161
  46.8 3.4 %shard_map.95 = (f32[136,1024]{1,0:T(8,128)S(1)}, f32[136,1024]{1,0:T(8,128)S(1)}, f32[136,1024]{1,0:T(8,128)S(1)}, f32[136,1024]{1,0:T(8,128)S(1)}) custom-call(s32[1]{0:T(128)} %bitcast.place_ref, f32[256,1024]{1,0:T(8,128)S(1)} %get-tuple-element.33.refs_0_, f32[256,1024]{1,0:T(8,128)S(1)} %get-tuple-element.34.refs_1_, ...), custom_call_target="tpu_custom_call" | custom-call | flops 1073741824 | bytes 4194304 | tf_op jit(solution)/shard_map/pallas_call | solution.py:179
  50.4 2.7 %collective-permute-done.16.refs_4_ = bf16[4,256,256]{2,1,0:T(8,128)(2,1)S(1)} collective-permute-done((bf16[4,256,256]{2,1,0:T(8,128)(2,1)S(1)}, bf16[4,256,256]{2,1,0:T(8,128)(2,1)S(1)}, u32[]{:S(2)}, u32[]{:S(2)}) %collective-permute-start.16) | collective-permute-done | bytes 524320 | tf_op jit(solution)/shard_map/ppermute | solution.py:30
  55.2 2.6 %collective-permute-start.25 = (f16[136,1024]{1,0:T(8,128)(2,1)S(1)}, f16[136,1024]{1,0:T(8,128)(2,1)S(1)}, u32[]{:S(2)}, u32[]{:S(2)}) collective-permute-start(f16[136,1024]{1,0:T(8,128)(2,1)S(1)} %convert_element_type.42), channel_id=1, source_target_pairs={{0,64},{16,80},{32,96},{48,112},{64,0},{80,16},{96,32},{112,48},{1... | collective-permute-start | bytes 835592 | tf_op jit(solution)/shard_map/ppermute | solution.py:30
  58.7 3.1 %collective-permute-done.21.refs_5_ = bf16[2,256,256]{2,1,0:T(8,128)(2,1)S(1)} collective-permute-done((bf16[2,256,256]{2,1,0:T(8,128)(2,1)S(1)}, bf16[2,256,256]{2,1,0:T(8,128)(2,1)S(1)}, u32[]{:S(2)}, u32[]{:S(2)}) %collective-permute-start.21) | collective-permute-done | bytes 262176 | tf_op jit(solution)/shard_map/ppermute | solution.py:30
  62.9 5.4 %shard_map.94 = (f32[256,1024]{1,0:T(8,128)S(1)}, f32[256,1024]{1,0:T(8,128)S(1)}) custom-call(s32[1]{0:T(128)} %bitcast.place_ref, bf16[4,256,256]{2,1,0:T(8,128)(2,1)S(1)} %pad_maximum_fusion.1.refs_0_, bf16[4,256,256]{2,1,0:T(8,128)(2,1)S(1)} %collective-permute-done.14.refs_1_, bf16[4,256,256]{2,1,0:T(8,128)(2,1)S(1)} %collective-permute-done.15.refs_2_, ...), custom_call_target="tpu_custom_call" | custom-call | flops 3221225472 | bytes 8388608 | tf_op jit(solution)/shard_map/pallas_call | solution.py:161
  68.3 6.4 %collective-permute-start.26 = (f16[136,1024]{1,0:T(8,128)(2,1)S(1)}, f16[136,1024]{1,0:T(8,128)(2,1)S(1)}, u32[]{:S(2)}, u32[]{:S(2)}) collective-permute-start(f16[136,1024]{1,0:T(8,128)(2,1)S(1)} %convert_element_type.43), channel_id=1, source_target_pairs={{0,80},{16,64},{32,112},{48,96},{64,16},{80,0},{96,48},{112,32},{1... | collective-permute-start | bytes 835592 | tf_op jit(solution)/shard_map/ppermute | solution.py:30
  75.7 3.4 %shard_map.96 = (f32[136,1024]{1,0:T(8,128)S(1)}, f32[136,1024]{1,0:T(8,128)S(1)}, f32[136,1024]{1,0:T(8,128)S(1)}, f32[136,1024]{1,0:T(8,128)S(1)}) custom-call(s32[1]{0:T(128)} %bitcast.place_ref, f32[256,1024]{1,0:T(8,128)S(1)} %get-tuple-element.37.refs_0_, f32[256,1024]{1,0:T(8,128)S(1)} %get-tuple-element.38.refs_1_, ...), custom_call_target="tpu_custom_call" | custom-call | flops 1073741824 | bytes 4194304 | tf_op jit(solution)/shard_map/pallas_call | solution.py:179
  79.6 1.9 %collective-permute-start.28 = (f16[136,1024]{1,0:T(8,128)(2,1)S(1)}, f16[136,1024]{1,0:T(8,128)(2,1)S(1)}, u32[]{:S(2)}, u32[]{:S(2)}) collective-permute-start(f16[136,1024]{1,0:T(8,128)(2,1)S(1)} %convert_element_type.54), channel_id=1, source_target_pairs={{0,112},{16,96},{32,80},{48,64},{64,48},{80,32},{96,16},{112,0},{1... | collective-permute-start | bytes 835592 | tf_op jit(solution)/shard_map/ppermute | solution.py:30
  81.6 6.4 %collective-permute-done.27 = f16[136,1024]{1,0:T(8,128)(2,1)S(1)} collective-permute-done((f16[136,1024]{1,0:T(8,128)(2,1)S(1)}, f16[136,1024]{1,0:T(8,128)(2,1)S(1)}, u32[]{:S(2)}, u32[]{:S(2)}) %collective-permute-start.27) | collective-permute-done | bytes 278560 | tf_op jit(solution)/shard_map/ppermute | solution.py:30
  88.4 5.6 %collective-permute-done.28 = f16[136,1024]{1,0:T(8,128)(2,1)S(1)} collective-permute-done((f16[136,1024]{1,0:T(8,128)(2,1)S(1)}, f16[136,1024]{1,0:T(8,128)(2,1)S(1)}, u32[]{:S(2)}, u32[]{:S(2)}) %collective-permute-start.28) | collective-permute-done | bytes 278560 | tf_op jit(solution)/shard_map/ppermute | solution.py:30
  116.2 2.6 %shard_map.100 = (f32[128,1024]{1,0:T(8,128)}, f32[128,1024]{1,0:T(8,128)}, f32[128,1024]{1,0:T(8,128)}, f32[128,1024]{1,0:T(8,128)}, bf16[128,1024]{1,0:T(8,128)(2,1)S(1)}) custom-call(f32[40,128]{1,0:T(8,128)S(1)} %add_add_fusion.refs_0_, f32[40,128]{1,0:T(8,128)S(1)} %collective-permute-done.36.refs_1_, f32[40,128]{1,0:T(8,128)S(1)} %collective-permute-done.37.refs_2_, ...), custom_call_target="tpu_custom_call" | custom-call | tf_op jit(solution)/shard_map/pallas_call | solution.py:313
  120.2 1.9 %collective-permute-start.42 = (bf16[128,1024]{1,0:T(8,128)(2,1)S(1)}, bf16[128,1024]{1,0:T(8,128)(2,1)S(1)}, u32[]{:S(2)}, u32[]{:S(2)}) collective-permute-start(bf16[128,1024]{1,0:T(8,128)(2,1)S(1)} %get-tuple-element.55.refs_0_), channel_id=1, source_target_pairs={{0,96},{16,112},{32,64},{48,80},{64,32},{80,48},{96,0},{112,16},{1... | collective-permute-start | bytes 786440 | tf_op jit(solution)/shard_map/ppermute | solution.py:30
  122.1 6.0 %collective-permute-start.39 = (bf16[128,1024]{1,0:T(8,128)(2,1)S(1)}, bf16[128,1024]{1,0:T(8,128)(2,1)S(1)}, u32[]{:S(2)}, u32[]{:S(2)}) collective-permute-start(bf16[128,1024]{1,0:T(8,128)(2,1)S(1)} %get-tuple-element.55.refs_0_), channel_id=1, source_target_pairs={{0,16},{16,0},{32,48},{48,32},{64,80},{80,64},{96,112},{112,96},{1... | collective-permute-start | bytes 786440 | tf_op jit(solution)/shard_map/ppermute | solution.py:30
  129.3 5.6 %collective-permute-start.43 = (bf16[384,1024]{1,0:T(8,128)(2,1)S(1)}, bf16[384,1024]{1,0:T(8,128)(2,1)S(1)}, u32[]{:S(2)}, u32[]{:S(2)}) collective-permute-start(bf16[384,1024]{1,0:T(8,128)(2,1)S(1)} %pad_maximum_fusion), channel_id=1, source_target_pairs={{0,16},{16,0},{32,48},{48,32},{64,80},{80,64},{96,112},{112,96},{1... | collective-permute-start | bytes 2359304 | tf_op jit(solution)/shard_map/ppermute | solution.py:30
  134.8 1.9 %collective-permute-done.43.refs_5_ = bf16[384,1024]{1,0:T(8,128)(2,1)S(1)} collective-permute-done((bf16[384,1024]{1,0:T(8,128)(2,1)S(1)}, bf16[384,1024]{1,0:T(8,128)(2,1)S(1)}, u32[]{:S(2)}, u32[]{:S(2)}) %collective-permute-start.43) | collective-permute-done | bytes 786464 | tf_op jit(solution)/shard_map/ppermute | solution.py:30
  (119 shorter events, 48.9 us)
Async XLA Ops:
  1.9 9.6 %collective-permute-start.7 = (bf16[512,256]{1,0:T(8,128)(2,1)S(1)}, bf16[512,256]{1,0:T(8,128)(2,1)S(1)}, u32[]{:S(2)}, u32[]{:S(2)}) collective-permute-start(bf16[512,256]{1,0:T(8,128)(2,1)S(1)} %get-tuple-element.32), channel_id=1, source_target_pairs={{0,1},{1,0},{2,3},{3,2},{4,5},{5,4},{6,7},{7,6},{8,9},{9,8},{10,11... | collective-permute-start | bytes 786440 | tf_op jit(solution)/shard_map/ppermute | solution.py:30
  4.4 12.4 %collective-permute-start.8 = (bf16[512,256]{1,0:T(8,128)(2,1)S(1)}, bf16[512,256]{1,0:T(8,128)(2,1)S(1)}, u32[]{:S(2)}, u32[]{:S(2)}) collective-permute-start(bf16[512,256]{1,0:T(8,128)(2,1)S(1)} %get-tuple-element.32), channel_id=1, source_target_pairs={{0,3},{1,2},{2,1},{3,0},{4,7},{5,6},{6,5},{7,4},{8,11},{9,10},{10,... | collective-permute-start | bytes 786440 | tf_op jit(solution)/shard_map/ppermute | solution.py:30
  6.7 12.4 %collective-permute-start.9 = (bf16[512,256]{1,0:T(8,128)(2,1)S(1)}, bf16[512,256]{1,0:T(8,128)(2,1)S(1)}, u32[]{:S(2)}, u32[]{:S(2)}) collective-permute-start(bf16[512,256]{1,0:T(8,128)(2,1)S(1)} %get-tuple-element.32), channel_id=1, source_target_pairs={{0,2},{1,3},{2,0},{3,1},{4,6},{5,7},{6,4},{7,5},{8,10},{9,11},{10,... | collective-permute-start | bytes 786440 | tf_op jit(solution)/shard_map/ppermute | solution.py:30
  7.7 14.6 %collective-permute-start = (bf16[512,256]{1,0:T(8,128)(2,1)S(1)}, bf16[512,256]{1,0:T(8,128)(2,1)S(1)}, u32[]{:S(2)}, u32[]{:S(2)}) collective-permute-start(bf16[512,256]{1,0:T(8,128)(2,1)S(1)} %get-tuple-element.31), channel_id=1, source_target_pairs={{0,4},{1,5},{2,6},{3,7},{4,0},{5,1},{6,2},{7,3},{8,12},{9,13},{10,... | collective-permute-start | bytes 786440 | tf_op jit(solution)/shard_map/ppermute | solution.py:30
  8.9 13.4 %collective-permute-start.1 = (bf16[512,256]{1,0:T(8,128)(2,1)S(1)}, bf16[512,256]{1,0:T(8,128)(2,1)S(1)}, u32[]{:S(2)}, u32[]{:S(2)}) collective-permute-start(bf16[512,256]{1,0:T(8,128)(2,1)S(1)} %get-tuple-element.31), channel_id=1, source_target_pairs={{0,12},{1,13},{2,14},{3,15},{4,8},{5,9},{6,10},{7,11},{8,4},{9,5},... | collective-permute-start | bytes 786440 | tf_op jit(solution)/shard_map/ppermute | solution.py:30
  11.5 10.9 %collective-permute-start.2 = (bf16[512,256]{1,0:T(8,128)(2,1)S(1)}, bf16[512,256]{1,0:T(8,128)(2,1)S(1)}, u32[]{:S(2)}, u32[]{:S(2)}) collective-permute-start(bf16[512,256]{1,0:T(8,128)(2,1)S(1)} %get-tuple-element.31), channel_id=1, source_target_pairs={{0,8},{1,9},{2,10},{3,11},{4,12},{5,13},{6,14},{7,15},{8,0},{9,1},... | collective-permute-start | bytes 786440 | tf_op jit(solution)/shard_map/ppermute | solution.py:30
  19.8 13.8 %collective-permute-start.10 = (bf16[4,256,256]{2,1,0:T(8,128)(2,1)S(1)}, bf16[4,256,256]{2,1,0:T(8,128)(2,1)S(1)}, u32[]{:S(2)}, u32[]{:S(2)}) collective-permute-start(bf16[4,256,256]{2,1,0:T(8,128)(2,1)S(1)} %pad_maximum_fusion.3.refs_3_), channel_id=1, source_target_pairs={{0,12},{1,13},{2,14},{3,15},{4,8},{5,9},{6,10},{7,11},{8,4},{9,5},... | collective-permute-start | bytes 1572872 | tf_op jit(solution)/shard_map/ppermute | solution.py:30
  22.4 11.6 %collective-permute-start.12 = (bf16[4,256,256]{2,1,0:T(8,128)(2,1)S(1)}, bf16[4,256,256]{2,1,0:T(8,128)(2,1)S(1)}, u32[]{:S(2)}, u32[]{:S(2)}) collective-permute-start(bf16[4,256,256]{2,1,0:T(8,128)(2,1)S(1)} %pad_maximum_fusion.3.refs_3_), channel_id=1, source_target_pairs={{0,4},{1,5},{2,6},{3,7},{4,0},{5,1},{6,2},{7,3},{8,12},{9,13},{10,... | collective-permute-start | bytes 1572872 | tf_op jit(solution)/shard_map/ppermute | solution.py:30
  22.5 13.1 %collective-permute-start.3 = (bf16[4,256,256]{2,1,0:T(8,128)(2,1)S(1)}, bf16[4,256,256]{2,1,0:T(8,128)(2,1)S(1)}, u32[]{:S(2)}, u32[]{:S(2)}) collective-permute-start(bf16[4,256,256]{2,1,0:T(8,128)(2,1)S(1)} %pad_maximum_fusion.2.refs_0_), channel_id=1, source_target_pairs={{0,3},{1,2},{2,1},{3,0},{4,7},{5,6},{6,5},{7,4},{8,11},{9,10},{10,... | collective-permute-start | bytes 1572872 | tf_op jit(solution)/shard_map/ppermute | solution.py:30
  24.6 11.2 %collective-permute-start.5 = (bf16[4,256,256]{2,1,0:T(8,128)(2,1)S(1)}, bf16[4,256,256]{2,1,0:T(8,128)(2,1)S(1)}, u32[]{:S(2)}, u32[]{:S(2)}) collective-permute-start(bf16[4,256,256]{2,1,0:T(8,128)(2,1)S(1)} %pad_maximum_fusion.2.refs_0_), channel_id=1, source_target_pairs={{0,1},{1,0},{2,3},{3,2},{4,5},{5,4},{6,7},{7,6},{8,9},{9,8},{10,11... | collective-permute-start | bytes 1572872 | tf_op jit(solution)/shard_map/ppermute | solution.py:30
  33.6 9.6 %collective-permute-start.11 = (bf16[2,256,256]{2,1,0:T(8,128)(2,1)S(1)}, bf16[2,256,256]{2,1,0:T(8,128)(2,1)S(1)}, u32[]{:S(2)}, u32[]{:S(2)}) collective-permute-start(bf16[2,256,256]{2,1,0:T(8,128)(2,1)S(1)} %slice.107), channel_id=1, source_target_pairs={{0,4},{1,5},{2,6},{3,7},{4,0},{5,1},{6,2},{7,3},{8,12},{9,13},{10,... | collective-permute-start | bytes 786440 | tf_op jit(solution)/shard_map/ppermute | solution.py:30
  43.2 9.9 %collective-permute-start.16 = (bf16[4,256,256]{2,1,0:T(8,128)(2,1)S(1)}, bf16[4,256,256]{2,1,0:T(8,128)(2,1)S(1)}, u32[]{:S(2)}, u32[]{:S(2)}) collective-permute-start(bf16[4,256,256]{2,1,0:T(8,128)(2,1)S(1)} %pad_maximum_fusion.4.refs_3_), channel_id=1, source_target_pairs={{0,4},{1,5},{2,6},{3,7},{4,0},{5,1},{6,2},{7,3},{8,12},{9,13},{10,... | collective-permute-start | bytes 1572872 | tf_op jit(solution)/shard_map/ppermute | solution.py:30
  44.1 11.1 %collective-permute-start.17 = (bf16[4,256,256]{2,1,0:T(8,128)(2,1)S(1)}, bf16[4,256,256]{2,1,0:T(8,128)(2,1)S(1)}, u32[]{:S(2)}, u32[]{:S(2)}) collective-permute-start(bf16[4,256,256]{2,1,0:T(8,128)(2,1)S(1)} %pad_maximum_fusion.4.refs_3_), channel_id=1, source_target_pairs={{0,12},{1,13},{2,14},{3,15},{4,8},{5,9},{6,10},{7,11},{8,4},{9,5},... | collective-permute-start | bytes 1572872 | tf_op jit(solution)/shard_map/ppermute | solution.py:30
  45.1 12.7 %collective-permute-start.14 = (bf16[4,256,256]{2,1,0:T(8,128)(2,1)S(1)}, bf16[4,256,256]{2,1,0:T(8,128)(2,1)S(1)}, u32[]{:S(2)}, u32[]{:S(2)}) collective-permute-start(bf16[4,256,256]{2,1,0:T(8,128)(2,1)S(1)} %pad_maximum_fusion.1.refs_0_), channel_id=1, source_target_pairs={{0,1},{1,0},{2,3},{3,2},{4,5},{5,4},{6,7},{7,6},{8,9},{9,8},{10,11... | collective-permute-start | bytes 1572872 | tf_op jit(solution)/shard_map/ppermute | solution.py:30
  45.9 12.5 %collective-permute-start.15 = (bf16[4,256,256]{2,1,0:T(8,128)(2,1)S(1)}, bf16[4,256,256]{2,1,0:T(8,128)(2,1)S(1)}, u32[]{:S(2)}, u32[]{:S(2)}) collective-permute-start(bf16[4,256,256]{2,1,0:T(8,128)(2,1)S(1)} %pad_maximum_fusion.1.refs_0_), channel_id=1, source_target_pairs={{0,3},{1,2},{2,1},{3,0},{4,7},{5,6},{6,5},{7,4},{8,11},{9,10},{10,... | collective-permute-start | bytes 1572872 | tf_op jit(solution)/shard_map/ppermute | solution.py:30
  53.9 25.4 %collective-permute-start.23 = (f16[136,1024]{1,0:T(8,128)(2,1)S(1)}, f16[136,1024]{1,0:T(8,128)(2,1)S(1)}, u32[]{:S(2)}, u32[]{:S(2)}) collective-permute-start(f16[136,1024]{1,0:T(8,128)(2,1)S(1)} %convert_element_type.44), channel_id=1, source_target_pairs={{0,32},{16,48},{32,0},{48,16},{64,96},{80,112},{96,64},{112,80},{1... | collective-permute-start | bytes 835592 | tf_op jit(solution)/shard_map/ppermute | solution.py:30
  55.2 24.4 %collective-permute-start.25 = (f16[136,1024]{1,0:T(8,128)(2,1)S(1)}, f16[136,1024]{1,0:T(8,128)(2,1)S(1)}, u32[]{:S(2)}, u32[]{:S(2)}) collective-permute-start(f16[136,1024]{1,0:T(8,128)(2,1)S(1)} %convert_element_type.42), channel_id=1, source_target_pairs={{0,64},{16,80},{32,96},{48,112},{64,0},{80,16},{96,32},{112,48},{1... | collective-permute-start | bytes 835592 | tf_op jit(solution)/shard_map/ppermute | solution.py:30
  57.8 10.4 %collective-permute-start.20 = (bf16[2,256,256]{2,1,0:T(8,128)(2,1)S(1)}, bf16[2,256,256]{2,1,0:T(8,128)(2,1)S(1)}, u32[]{:S(2)}, u32[]{:S(2)}) collective-permute-start(bf16[2,256,256]{2,1,0:T(8,128)(2,1)S(1)} %slice.94), channel_id=1, source_target_pairs={{0,4},{1,5},{2,6},{3,7},{4,0},{5,1},{6,2},{7,3},{8,12},{9,13},{10,... | collective-permute-start | bytes 786440 | tf_op jit(solution)/shard_map/ppermute | solution.py:30
  58.5 16.2 %collective-permute-start.19 = (bf16[2,256,256]{2,1,0:T(8,128)(2,1)S(1)}, bf16[2,256,256]{2,1,0:T(8,128)(2,1)S(1)}, u32[]{:S(2)}, u32[]{:S(2)}) collective-permute-start(bf16[2,256,256]{2,1,0:T(8,128)(2,1)S(1)} %slice.93), channel_id=1, source_target_pairs={{0,3},{1,2},{2,1},{3,0},{4,7},{5,6},{6,5},{7,4},{8,11},{9,10},{10,... | collective-permute-start | bytes 786440 | tf_op jit(solution)/shard_map/ppermute | solution.py:30
  61.8 13.9 %collective-permute-start.18 = (bf16[2,256,256]{2,1,0:T(8,128)(2,1)S(1)}, bf16[2,256,256]{2,1,0:T(8,128)(2,1)S(1)}, u32[]{:S(2)}, u32[]{:S(2)}) collective-permute-start(bf16[2,256,256]{2,1,0:T(8,128)(2,1)S(1)} %slice.92), channel_id=1, source_target_pairs={{0,1},{1,0},{2,3},{3,2},{4,5},{5,4},{6,7},{7,6},{8,9},{9,8},{10,11... | collective-permute-start | bytes 786440 | tf_op jit(solution)/shard_map/ppermute | solution.py:30
  68.3 13.3 %collective-permute-start.26 = (f16[136,1024]{1,0:T(8,128)(2,1)S(1)}, f16[136,1024]{1,0:T(8,128)(2,1)S(1)}, u32[]{:S(2)}, u32[]{:S(2)}) collective-permute-start(f16[136,1024]{1,0:T(8,128)(2,1)S(1)} %convert_element_type.43), channel_id=1, source_target_pairs={{0,80},{16,64},{32,112},{48,96},{64,16},{80,0},{96,48},{112,32},{1... | collective-permute-start | bytes 835592 | tf_op jit(solution)/shard_map/ppermute | solution.py:30
  74.7 13.4 %collective-permute-start.27 = (f16[136,1024]{1,0:T(8,128)(2,1)S(1)}, f16[136,1024]{1,0:T(8,128)(2,1)S(1)}, u32[]{:S(2)}, u32[]{:S(2)}) collective-permute-start(f16[136,1024]{1,0:T(8,128)(2,1)S(1)} %convert_element_type.45), channel_id=1, source_target_pairs={{0,96},{16,112},{32,64},{48,80},{64,32},{80,48},{96,0},{112,16},{1... | collective-permute-start | bytes 835592 | tf_op jit(solution)/shard_map/ppermute | solution.py:30
  79.6 14.4 %collective-permute-start.28 = (f16[136,1024]{1,0:T(8,128)(2,1)S(1)}, f16[136,1024]{1,0:T(8,128)(2,1)S(1)}, u32[]{:S(2)}, u32[]{:S(2)}) collective-permute-start(f16[136,1024]{1,0:T(8,128)(2,1)S(1)} %convert_element_type.54), channel_id=1, source_target_pairs={{0,112},{16,96},{32,80},{48,64},{64,48},{80,32},{96,16},{112,0},{1... | collective-permute-start | bytes 835592 | tf_op jit(solution)/shard_map/ppermute | solution.py:30
  118.8 9.3 %collective-permute-start.40 = (bf16[128,1024]{1,0:T(8,128)(2,1)S(1)}, bf16[128,1024]{1,0:T(8,128)(2,1)S(1)}, u32[]{:S(2)}, u32[]{:S(2)}) collective-permute-start(bf16[128,1024]{1,0:T(8,128)(2,1)S(1)} %get-tuple-element.55.refs_0_), channel_id=1, source_target_pairs={{0,64},{16,80},{32,96},{48,112},{64,0},{80,16},{96,32},{112,48},{1... | collective-permute-start | bytes 786440 | tf_op jit(solution)/shard_map/ppermute | solution.py:30
  (25 other events, 195.2 us)

commit v3 on v2

--- a/solution.py
+++ b/solution.py
@@ -57,6 +57,10 @@
 
 def after(value, *others):
     return lax.optimization_barrier((value, *others))[0]
+
+
+def widen(value):
+    return value.astype(jnp.float32)
 
 
 def spread(own, axis_step):
@@ -114,34 +118,36 @@
         b_acc[...] = part if x == 0 else b_acc[...] + part
 
 
-def late_kernel(owners, place_ref, *refs):
-    a_acc, b_acc, a_halves, b_halves, cotangent = refs[0], refs[1], refs[2:4], refs[4:6], refs[6]
-    outs, buffer, sems = refs[7:-2], refs[-2], refs[-1]
+def late_kernel(owners, whole, paired, place_ref, *refs):
+    per_side = 1 if whole else 2
+    a_acc, b_acc, cotangent = *refs[:2], refs[2 + 2 * per_side]
+    a_pieces, b_pieces = refs[2 : 2 + per_side], refs[2 + per_side : 2 + 2 * per_side]
+    outs, buffer, sems = refs[3 + 2 * per_side : -2], refs[-2], refs[-1]
+    if paired:
+        outs = [outs[0].at[: BLOCK + EXTRA], outs[0].at[BLOCK + EXTRA :], *outs[1:]]
     wanted = [(x, 3) for x in range(4)] + [(3, z) for z in range(3)]
     copies = fetch(place_ref[0], cotangent, buffer, sems, wanted)
-    for half, (acc, halves, line) in enumerate(
+    for half, (acc, pieces, line) in enumerate(
         (
-            (a_acc, a_halves, [(x, 3) for x in range(4)]),
-            (b_acc, b_halves, [(3, z) for z in range(4)]),
+            (a_acc, a_pieces, [(x, 3) for x in range(4)]),
+            (b_acc, b_pieces, [(3, z) for z in range(4)]),
         )
     ):
         for at in line:
             if half == 0 or at != (3, 3):
                 copies[at].wait()
-        whole = acc[...] + line_product(
-            [halves[i // 2][i % 2] for i in range(4)], [buffer[slot(*at)] for at in line]
-        )
+        left = [pieces[0][i] if whole else pieces[i // 2][i % 2] for i in range(4)]
+        total = acc[...] + line_product(left, [buffer[slot(*at)] for at in line])
         for i in range(2):
             k, out = owners[2 * half + i], outs[2 * half + i]
-            block = whole[i * BLOCK : (i + 1) * BLOCK]
-            if k == 0:
-                out[:BLOCK, :] = block
-                out[BLOCK:, :] = jnp.zeros((EXTRA, block.shape[1]), jnp.float32)
-                continue
-            top = jnp.max(jnp.max(jnp.abs(block), axis=0, keepdims=True), axis=1, keepdims=True)
-            power = jnp.floor(15.0 - jnp.log2(jnp.maximum(top, 1e-30)))
-            out[:BLOCK, :] = block * jnp.exp2(power)
-            out[BLOCK:, :] = jnp.broadcast_to(power, (EXTRA, block.shape[1]))
+            rows = total[i * BLOCK : (i + 1) * BLOCK]
+            power = jnp.zeros((1, 1), jnp.float32)
+            if k:
+                top = jnp.max(jnp.max(jnp.abs(rows), axis=0, keepdims=True), axis=1, keepdims=True)
+                power = jnp.floor(15.0 - jnp.log2(jnp.maximum(top, 1e-30)))
+                rows = rows * jnp.exp2(power)
+            out[:BLOCK, :] = rows
+            out[BLOCK:, :] = jnp.broadcast_to(power, (EXTRA, rows.shape[1]))
 
 
 HBM = pl.BlockSpec(memory_space=pltpu.HBM)
@@ -164,7 +170,7 @@
         in_specs=[SMEM] + [WHOLE] * 6 + [HBM],
         out_specs=[WHOLE] * 2,
         scratch_shapes=product_scratch(cotangent),
-        compiler_params=pltpu.CompilerParams(vmem_limit_bytes=24 * MIB),
+        compiler_params=pltpu.CompilerParams(vmem_limit_bytes=14 * MIB),
         cost_estimate=pl.CostEstimate(
             flops=3 * tokens * columns * features,
             bytes_accessed=2 * tokens * columns,
@@ -173,22 +179,24 @@
     )(place, *a_pieces, *b_pieces, cotangent)
 
 
-def late_product(owners, place, sums, a_halves, b_halves, cotangent):
+def late_product(owners, paired, place, sums, a_pieces, b_pieces, cotangent):
     tokens, columns = cotangent.shape
-    features = a_halves[0].shape[1]
-    return pl.pallas_call(
-        functools.partial(late_kernel, owners),
-        out_shape=[jax.ShapeDtypeStruct((BLOCK + EXTRA, columns), jnp.float32)] * 4,
-        in_specs=[SMEM] + [WHOLE] * 6 + [HBM],
-        out_specs=[WHOLE] * 4,
+    features = a_pieces[0].shape[1]
+    rows = BLOCK + EXTRA
+    heights = [2 * rows, rows, rows] if paired else [rows] * 4
+    return pl.pallas_call(
+        functools.partial(late_kernel, owners, len(a_pieces) == 1, paired),
+        out_shape=[jax.ShapeDtypeStruct((height, columns), jnp.float32) for height in heights],
+        in_specs=[SMEM] + [WHOLE] * (2 + 2 * len(a_pieces)) + [HBM],
+        out_specs=[WHOLE] * len(heights),
         scratch_shapes=product_scratch(cotangent),
-        compiler_params=pltpu.CompilerParams(vmem_limit_bytes=24 * MIB),
+        compiler_params=pltpu.CompilerParams(vmem_limit_bytes=14 * MIB),
         cost_estimate=pl.CostEstimate(
             flops=tokens * columns * features,
             bytes_accessed=tokens * columns,
             transcendentals=0,
         ),
-    )(place, *sums, *a_halves, *b_halves, cotangent)
+    )(place, *sums, *a_pieces, *b_pieces, cotangent)
 
 
 def gram_kernel(*refs):
@@ -278,14 +286,18 @@
     return [first[k] * second[k % 4] * third[k % 2] for k in range(8)]
 
 
-def adam_kernel(*refs):
-    sums, blocks = refs[:4], refs[4:12]
-    master, moment, second = refs[12:15]
-    combined_out, moment_out, second_out, master_out, weights_out, coef = refs[15:]
-    total = sums[0][...] + sums[1][...] + sums[2][...] + sums[3][...]
-    for k, c in enumerate(coefficients(total)):
-        coef[k : k + 1, :] = c * jnp.exp2(-blocks[k][BLOCK : BLOCK + 1, :128])
-    rows = BLOCK
+def adam_kernel(sums_to, *refs):
+    count = 4 if sums_to else 1
+    given, blocks = refs[:count], refs[count : count + 8]
+    master, moment, second = refs[count + 8 : count + 11]
+    outs = refs[count + 11 :]
+    if sums_to:
+        weights_out, coef = outs
+        total = given[0][...] + given[1][...] + given[2][...] + given[3][...]
+        for k, c in enumerate(coefficients(total)):
+            coef[k : k + 1, :] = c * jnp.exp2(-blocks[k][BLOCK : BLOCK + 1, :128])
+    else:
+        coef = given[0]
     scale = [coef[k : k + 1, 0:1] for k in range(8)]
 
     def body(i, carry):
@@ -298,26 +310,32 @@
         master_new = master[at, :] - LEARN * (moment_new / CORRECT_ONE) / (
             jnp.sqrt(second_new / CORRECT_TWO) + 1e-08
         )
-        combined_out[at, :] = combined
-        moment_out[at, :] = moment_new
-        second_out[at, :] = second_new
-        master_out[at, :] = master_new
-        weights_out[at, :] = master_new.astype(jnp.bfloat16)
+        if sums_to:
+            weights_out[at, :] = master_new.astype(jnp.bfloat16)
+        else:
+            for out, value in zip(outs, (combined, moment_new, second_new, master_new)):
+                out[at, :] = value
         return carry
 
-    lax.fori_loop(0, rows // 16, body, 0)
-
-
-def adam(sums, blocks, master, moment, second):
+    lax.fori_loop(0, BLOCK // 16, body, 0)
+
+
+def adam(given, blocks, master, moment, second):
+    first = len(given) > 1
     full = jax.ShapeDtypeStruct(master.shape, jnp.float32)
-    return pl.pallas_call(
-        adam_kernel,
-        out_shape=(full, full, full, full, jax.ShapeDtypeStruct(master.shape, jnp.bfloat16)),
-        in_specs=[WHOLE] * 15,
-        out_specs=(WHOLE,) * 5,
-        scratch_shapes=[pltpu.VMEM((8, 128), jnp.float32)],
-        compiler_params=pltpu.CompilerParams(vmem_limit_bytes=16 * MIB),
-    )(*sums, *blocks, master, moment, second)
+    outs = [full] * 4
+    if first:
+        outs = [
+            jax.ShapeDtypeStruct(master.shape, jnp.bfloat16),
+            jax.ShapeDtypeStruct((8, 128), jnp.float32),
+        ]
+    return pl.pallas_call(
+        functools.partial(adam_kernel, first),
+        out_shape=outs,
+        in_specs=[WHOLE] * (len(given) + 11),
+        out_specs=[WHOLE] * len(outs),
+        compiler_params=pltpu.CompilerParams(vmem_limit_bytes=12 * MIB),
+    )(*given, *blocks, master, moment, second)
 
 
 CHIPS = (4, 2, 6)
@@ -339,12 +357,12 @@
         copy.wait()
 
 
-def assemble(rep, mine):
+def assemble(rep, mine, *others):
     rows, columns = mine.shape
     anywhere = pl.BlockSpec(memory_space=pl.ANY)
     far = [swap(mine, "rep", k) for k in CHIPS]
     other = swap(mine, "rep", 1)
-    swapped = swap(after(jnp.concatenate(far), other), "rep", 1)
+    swapped = swap(after(jnp.concatenate(far), other, *others), "rep", 1)
     return pl.pallas_call(
         place_kernel,
         out_shape=jax.ShapeDtypeStruct((8 * rows, columns), mine.dtype),
@@ -363,33 +381,45 @@
     a_line = spread(a, 4)
     b_line = spread(b, 1)
     blocks = [None] * 8
-    before, done = [], []
-    for i, (a_owners, b_owners) in enumerate(CHUNKS):
-        rows = slice(i * 2 * BLOCK, (i + 1) * 2 * BLOCK)
+    before, sent = [], []
+    for chunk, (a_owners, b_owners) in enumerate(CHUNKS):
+        rows = slice(chunk * 2 * BLOCK, (chunk + 1) * 2 * BLOCK)
         a_own = after(jnp.stack([piece[rows] for piece in a_line]), *before)
         b_own = after(jnp.stack([piece[rows] for piece in b_line]), *before)
         a_near, a_far = swap(a_own, "tp", 1), swap(a_own, "tp", 3)
         b_near, b_far = swap(b_own, "tp", 4), swap(b_own, "tp", 12)
-        a_opposite = forward(after(a_near, *done), after(a_far, *done), 1)
-        b_opposite = forward(after(b_near, *done), after(b_far, *done), 4)
+        if chunk:
+            a_opposite = forward(after(a_near, *sent), after(a_far, *sent), 1)
+            b_opposite = forward(after(b_near, *sent), after(b_far, *sent), 4)
+        else:
+            a_opposite = forward(a_near, a_far, 1)
+            b_opposite = forward(b_near, b_far, 4)
         sums = early_product(
             place, [a_own, a_near, a_far], [b_own, b_near, b_far], cotangent
         )
         before = [*a_opposite, *b_opposite, *sums]
         owners = a_owners + b_owners
-        values = late_product(owners, place, sums, a_opposite, b_opposite, cotangent)
-        for k, value in zip(owners, values):
-            if k:
-                done.append(value.astype(jnp.float16))
-                value = swap(done[-1], "rep", k).astype(jnp.float32)
-            blocks[k] = value
+        values = late_product(owners, not chunk, place, sums, a_opposite, b_opposite, cotangent)
+        if chunk:
+            for k, value in zip((2, 6), sent[1:]):
+                blocks[k] = widen(swap(after(value, *sums), "rep", k))
+            last = [value.astype(jnp.float16) for value in values[:3]]
+            for k, value in zip(owners[:3], last):
+                blocks[k] = widen(swap(value, "rep", k))
+            blocks[5] = widen(swap(after(pair[BLOCK + EXTRA :], *last), "rep", 1))
+            blocks[0] = values[3]
+        else:
+            sent = [value.astype(jnp.float16) for value in values]
+            pair = swap(sent[0], "rep", 4)
+            blocks[4] = widen(pair[: BLOCK + EXTRA])
     sums = gram(blocks)
     sums = join(sums, (1,))
     sums = join(sums, (2, 4, 6))
     sums = sums + swap(sums, "tp", 1) + swap(sums, "tp", 2) + swap(sums, "tp", 3)
     sums = [sums] + [swap(sums, "tp", d) for d in (4, 8, 12)]
-    combined, moment_new, second_new, master_new, mine = adam(sums, blocks, master, moment, second)
-    weights = assemble(rep, mine)
+    mine, coef = adam(sums, blocks, master, moment, second)
+    combined, moment_new, second_new, master_new = adam([coef], blocks, master, moment, second)
+    weights = assemble(rep, mine, combined)
     return (combined, moment_new, second_new, master_new, weights)
 
 

time: 138 us -> 132 us (0.957)
  waiting for transfers between devices: 41.6 us -> 30.6 us
  starting transfers between devices: 66.3 us -> 69.3 us
    ppermute x44, waiting for transfers between devices: 41.6 us -> 30.6 us  [swap(): lax.ppermute(value, axis, [(i, i ^ distance) for i in range(lax.axis_size...]
    ppermute x44, starting transfers between devices: 66.3 us -> 69.3 us  [swap(): lax.ppermute(value, axis, [(i, i ^ distance) for i in range(lax.axis_size...]
    pallas_call x3 -> x4, Pallas kernels: 9.34 us -> 10.3 us  [the longest x2 6.77 us: late_product(): pl.pallas_call(functools.partial(late_kernel, owners, len(a_pieces) == 1,...]
  transfers between devices with their start and end apart: 44 -> 44, of which waited for: 19 -> 14; matrix products, arithmetic and copies ran while one was open for 4% -> 4% of each run, Pallas kernels for 13% -> 15%
where the time goes in v3:
time: 132 us; the launch traced here: 131 us
  starting transfers between devices  69.3 us (52%)
  waiting for transfers between devices  30.6 us (23%)
  Pallas kernels  24.2 us (18%)
  local copies, waits for them, and re-layouts  4.01 us (3%)
  other arithmetic  2 us (2%)
    ppermute x44, starting transfers between devices, swap(): lax.ppermute(value, axis, [(i, i ^ distance) for i in range(lax.axis_size...  69.3 us
    ppermute x44, waiting for transfers between devices, swap(): lax.ppermute(value, axis, [(i, i ^ distance) for i in range(lax.axis_size...  30.6 us
    pallas_call x2, Pallas kernels, early_product(): pl.pallas_call(early_kernel, out_shape=[jax.ShapeDtypeStruct((features, c...  10.9 us
    pallas_call x2, Pallas kernels, late_product(): pl.pallas_call(functools.partial(late_kernel, owners, len(a_pieces) == 1,...  6.77 us
    pallas_call x2, Pallas kernels, adam(): pl.pallas_call(functools.partial(adam_kernel, first), out_shape=outs, in_...  3.53 us
    another operation x4, local copies, waits for them, and re-layouts, per_device(): b_own = after(jnp.stack([piece[rows] for piece in b_line]), *before)  2.75 us
  transfers between devices with their start and end apart: 44, of which 14 were waited for; matrix products, arithmetic and copies ran while one was open for 4% of the time, Pallas kernels for 15%

profile of v3, /device:TPU:1, one launch (start us, length us, event | category | flops | bytes accessed | tf_op | source)
XLA Modules:
  0.0 131.5 jit_solution(11075175083093563688)
XLA Ops:
  1.9 2.5 %collective-permute-start.7 = (bf16[512,256]{1,0:T(8,128)(2,1)S(1)}, bf16[512,256]{1,0:T(8,128)(2,1)S(1)}, u32[]{:S(2)}, u32[]{:S(2)}) collective-permute-start(bf16[512,256]{1,0:T(8,128)(2,1)S(1)} %get-tuple-element.35), channel_id=1, source_target_pairs={{0,1},{1,0},{2,3},{3,2},{4,5},{5,4},{6,7},{7,6},{8,9},{9,8},{10,11... | collective-permute-start | bytes 786440 | tf_op jit(solution)/shard_map/ppermute | solution.py:30
  4.4 2.2 %collective-permute-start.8 = (bf16[512,256]{1,0:T(8,128)(2,1)S(1)}, bf16[512,256]{1,0:T(8,128)(2,1)S(1)}, u32[]{:S(2)}, u32[]{:S(2)}) collective-permute-start(bf16[512,256]{1,0:T(8,128)(2,1)S(1)} %get-tuple-element.35), channel_id=1, source_target_pairs={{0,3},{1,2},{2,1},{3,0},{4,7},{5,6},{6,5},{7,4},{8,11},{9,10},{10,... | collective-permute-start | bytes 786440 | tf_op jit(solution)/shard_map/ppermute | solution.py:30
  13.7 3.0 %collective-permute-done.8 = bf16[512,256]{1,0:T(8,128)(2,1)S(1)} collective-permute-done((bf16[512,256]{1,0:T(8,128)(2,1)S(1)}, bf16[512,256]{1,0:T(8,128)(2,1)S(1)}, u32[]{:S(2)}, u32[]{:S(2)}) %collective-permute-start.8) | collective-permute-done | bytes 262176 | tf_op jit(solution)/shard_map/ppermute | solution.py:30
  19.8 2.6 %collective-permute-start.10 = (bf16[4,256,256]{2,1,0:T(8,128)(2,1)S(1)}, bf16[4,256,256]{2,1,0:T(8,128)(2,1)S(1)}, u32[]{:S(2)}, u32[]{:S(2)}) collective-permute-start(bf16[4,256,256]{2,1,0:T(8,128)(2,1)S(1)} %pad_maximum_fusion.3.refs_3_), channel_id=1, source_target_pairs={{0,12},{1,13},{2,14},{3,15},{4,8},{5,9},{6,10},{7,11},{8,4},{9,5},... | collective-permute-start | bytes 1572872 | tf_op jit(solution)/shard_map/ppermute | solution.py:30
  22.5 2.1 %collective-permute-start.3 = (bf16[4,256,256]{2,1,0:T(8,128)(2,1)S(1)}, bf16[4,256,256]{2,1,0:T(8,128)(2,1)S(1)}, u32[]{:S(2)}, u32[]{:S(2)}) collective-permute-start(bf16[4,256,256]{2,1,0:T(8,128)(2,1)S(1)} %pad_maximum_fusion.2.refs_0_), channel_id=1, source_target_pairs={{0,3},{1,2},{2,1},{3,0},{4,7},{5,6},{6,5},{7,4},{8,11},{9,10},{10,... | collective-permute-start | bytes 1572872 | tf_op jit(solution)/shard_map/ppermute | solution.py:30
  25.8 7.8 %collective-permute-done.10.refs_5_ = bf16[4,256,256]{2,1,0:T(8,128)(2,1)S(1)} collective-permute-done((bf16[4,256,256]{2,1,0:T(8,128)(2,1)S(1)}, bf16[4,256,256]{2,1,0:T(8,128)(2,1)S(1)}, u32[]{:S(2)}, u32[]{:S(2)}) %collective-permute-start.10) | collective-permute-done | bytes 524320 | tf_op jit(solution)/shard_map/ppermute | solution.py:30
  35.8 1.8 %collective-permute-start.6 = (bf16[2,256,256]{2,1,0:T(8,128)(2,1)S(1)}, bf16[2,256,256]{2,1,0:T(8,128)(2,1)S(1)}, u32[]{:S(2)}, u32[]{:S(2)}) collective-permute-start(bf16[2,256,256]{2,1,0:T(8,128)(2,1)S(1)} %slice.111), channel_id=1, source_target_pairs={{0,3},{1,2},{2,1},{3,0},{4,7},{5,6},{6,5},{7,4},{8,11},{9,10},{10,... | collective-permute-start | bytes 786440 | tf_op jit(solution)/shard_map/ppermute | solution.py:30
  37.7 5.4 %shard_map.93 = (f32[256,1024]{1,0:T(8,128)S(1)}, f32[256,1024]{1,0:T(8,128)S(1)}) custom-call(s32[1]{0:T(128)} %bitcast.place_ref, bf16[4,256,256]{2,1,0:T(8,128)(2,1)S(1)} %pad_maximum_fusion.2.refs_0_, bf16[4,256,256]{2,1,0:T(8,128)(2,1)S(1)} %collective-permute-done.5.refs_1_, bf16[4,256,256]{2,1,0:T(8,128)(2,1)S(1)} %collective-permute-done.3.refs_2_, ...), custom_call_target="tpu_custom_call" | custom-call | flops 3221225472 | bytes 8388608 | tf_op jit(solution)/shard_map/pallas_call | solution.py:167
  46.8 3.4 %shard_map.95 = (f32[272,1024]{1,0:T(8,128)S(1)}, f32[136,1024]{1,0:T(8,128)S(1)}, f32[136,1024]{1,0:T(8,128)S(1)}) custom-call(s32[1]{0:T(128)} %bitcast.place_ref, f32[256,1024]{1,0:T(8,128)S(1)} %get-tuple-element.36.refs_0_, f32[256,1024]{1,0:T(8,128)S(1)} %get-tuple-element.37.refs_1_, bf16[2,256,256]{2,1,0:T(8,128)(2,1)S(1)} %collective-permute-done.4.refs_2_, ...), custom_call_target="tpu_custom_call" | custom-call | flops 1073741824 | bytes 4194304 | tf_op jit(solution)/shard_map/pallas_call | solution.py:187
  50.3 3.0 %collective-permute-start.25 = (f16[272,1024]{1,0:T(8,128)(2,1)S(1)}, f16[272,1024]{1,0:T(8,128)(2,1)S(1)}, u32[]{:S(2)}, u32[]{:S(2)}) collective-permute-start(f16[272,1024]{1,0:T(8,128)(2,1)S(1)} %convert_element_type.39), channel_id=1, source_target_pairs={{0,64},{16,80},{32,96},{48,112},{64,0},{80,16},{96,32},{112,48},{1... | collective-permute-start | bytes 1671176 | tf_op jit(solution)/shard_map/ppermute | solution.py:30
  53.4 2.1 %collective-permute-start.21 = (bf16[2,256,256]{2,1,0:T(8,128)(2,1)S(1)}, bf16[2,256,256]{2,1,0:T(8,128)(2,1)S(1)}, u32[]{:S(2)}, u32[]{:S(2)}) collective-permute-start(bf16[2,256,256]{2,1,0:T(8,128)(2,1)S(1)} %slice.101), channel_id=1, source_target_pairs={{0,12},{1,13},{2,14},{3,15},{4,8},{5,9},{6,10},{7,11},{8,4},{9,5},... | collective-permute-start | bytes 786440 | tf_op jit(solution)/shard_map/ppermute | solution.py:30
  57.6 5.4 %shard_map.94 = (f32[256,1024]{1,0:T(8,128)S(1)}, f32[256,1024]{1,0:T(8,128)S(1)}) custom-call(s32[1]{0:T(128)} %bitcast.place_ref, bf16[4,256,256]{2,1,0:T(8,128)(2,1)S(1)} %pad_maximum_fusion.1.refs_0_, bf16[4,256,256]{2,1,0:T(8,128)(2,1)S(1)} %collective-permute-done.14.refs_1_, bf16[4,256,256]{2,1,0:T(8,128)(2,1)S(1)} %collective-permute-done.15.refs_2_, ...), custom_call_target="tpu_custom_call" | custom-call | flops 3221225472 | bytes 8388608 | tf_op jit(solution)/shard_map/pallas_call | solution.py:167
  65.0 3.4 %shard_map.96 = (f32[136,1024]{1,0:T(8,128)S(1)}, f32[136,1024]{1,0:T(8,128)S(1)}, f32[136,1024]{1,0:T(8,128)S(1)}, f32[136,1024]{1,0:T(8,128)S(1)}) custom-call(s32[1]{0:T(128)} %bitcast.place_ref, f32[256,1024]{1,0:T(8,128)S(1)} %get-tuple-element.40.refs_0_, f32[256,1024]{1,0:T(8,128)S(1)} %get-tuple-element.41.refs_1_, ...), custom_call_target="tpu_custom_call" | custom-call | flops 1073741824 | bytes 4194304 | tf_op jit(solution)/shard_map/pallas_call | solution.py:187
  68.5 8.2 %collective-permute-start.26 = (f16[136,1024]{1,0:T(8,128)(2,1)S(1)}, f16[136,1024]{1,0:T(8,128)(2,1)S(1)}, u32[]{:S(2)}, u32[]{:S(2)}) collective-permute-start(f16[136,1024]{1,0:T(8,128)(2,1)S(1)} %get-tuple-element.54), channel_id=1, source_target_pairs={{0,16},{16,0},{32,48},{48,32},{64,80},{80,64},{96,112},{112,96},{1... | collective-permute-start | bytes 835592 | tf_op jit(solution)/shard_map/ppermute | solution.py:30
  76.8 1.9 %collective-permute-start.24 = (f16[136,1024]{1,0:T(8,128)(2,1)S(1)}, f16[136,1024]{1,0:T(8,128)(2,1)S(1)}, u32[]{:S(2)}, u32[]{:S(2)}) collective-permute-start(f16[136,1024]{1,0:T(8,128)(2,1)S(1)} %convert_element_type.45), channel_id=1, source_target_pairs={{0,48},{16,32},{32,16},{48,0},{64,112},{80,96},{96,80},{112,64},{1... | collective-permute-start | bytes 835592 | tf_op jit(solution)/shard_map/ppermute | solution.py:30
  80.4 5.4 %collective-permute-done.24 = f16[136,1024]{1,0:T(8,128)(2,1)S(1)} collective-permute-done((f16[136,1024]{1,0:T(8,128)(2,1)S(1)}, f16[136,1024]{1,0:T(8,128)(2,1)S(1)}, u32[]{:S(2)}, u32[]{:S(2)}) %collective-permute-start.24) | collective-permute-done | bytes 278560 | tf_op jit(solution)/shard_map/ppermute | solution.py:30
  85.8 2.5 %collective-permute-done.28 = f16[136,1024]{1,0:T(8,128)(2,1)S(1)} collective-permute-done((f16[136,1024]{1,0:T(8,128)(2,1)S(1)}, f16[136,1024]{1,0:T(8,128)(2,1)S(1)}, u32[]{:S(2)}, u32[]{:S(2)}) %collective-permute-start.28) | collective-permute-done | bytes 278560 | tf_op jit(solution)/shard_map/ppermute | solution.py:30
  91.2 1.8 %collective-permute-start.31 = (f32[40,128]{1,0:T(8,128)S(1)}, f32[40,128]{1,0:T(8,128)S(1)}, u32[]{:S(2)}, u32[]{:S(2)}) collective-permute-start(f32[40,128]{1,0:T(8,128)S(1)} %shard_map.98.own), channel_id=1, source_target_pairs={{0,64},{16,80},{32,96},{48,112},{64,0},{80,16},{96,32},{112,48},{1... | collective-permute-start | bytes 61448 | tf_op jit(solution)/shard_map/ppermute | solution.py:30
  93.0 2.0 %collective-permute-start.32 = (f32[40,128]{1,0:T(8,128)S(1)}, f32[40,128]{1,0:T(8,128)S(1)}, u32[]{:S(2)}, u32[]{:S(2)}) collective-permute-start(f32[40,128]{1,0:T(8,128)S(1)} %shard_map.98.own), channel_id=1, source_target_pairs={{0,96},{16,112},{32,64},{48,80},{64,32},{80,48},{96,0},{112,16},{1... | collective-permute-start | bytes 61448 | tf_op jit(solution)/shard_map/ppermute | solution.py:30
  112.3 2.3 %collective-permute-start.41 = (bf16[128,1024]{1,0:T(8,128)(2,1)S(1)}, bf16[128,1024]{1,0:T(8,128)(2,1)S(1)}, u32[]{:S(2)}, u32[]{:S(2)}) collective-permute-start(bf16[128,1024]{1,0:T(8,128)(2,1)S(1)} %get-tuple-element.61.refs_0_), channel_id=1, source_target_pairs={{0,32},{16,48},{32,0},{48,16},{64,96},{80,112},{96,64},{112,80},{1... | collective-permute-start | bytes 786440 | tf_op jit(solution)/shard_map/ppermute | solution.py:30
  115.2 6.0 %collective-permute-start.39 = (bf16[128,1024]{1,0:T(8,128)(2,1)S(1)}, bf16[128,1024]{1,0:T(8,128)(2,1)S(1)}, u32[]{:S(2)}, u32[]{:S(2)}) collective-permute-start(bf16[128,1024]{1,0:T(8,128)(2,1)S(1)} %get-tuple-element.61.refs_0_), channel_id=1, source_target_pairs={{0,16},{16,0},{32,48},{48,32},{64,80},{80,64},{96,112},{112,96},{1... | collective-permute-start | bytes 786440 | tf_op jit(solution)/shard_map/ppermute | solution.py:30
  121.3 2.3 %shard_map.101 = (f32[128,1024]{1,0:T(8,128)}, f32[128,1024]{1,0:T(8,128)}, f32[128,1024]{1,0:T(8,128)}, f32[128,1024]{1,0:T(8,128)}) custom-call(f32[8,128]{1,0:T(8,128)S(1)} %get-tuple-element.56.refs_0_, f32[136,1024]{1,0:T(8,128)S(1)} %get-tuple-element.49.refs_0_.refs_4_.refs_1_, f32[136,1024]{1,0:T(8,128)S(1)} %convert_element_type.43.refs_1_.refs_5_.refs_2_, ...), custom_call_target="tpu_custom_call" | custom-call | tf_op jit(solution)/shard_map/pallas_call | solution.py:332
  123.6 4.4 %collective-permute-start.43 = (bf16[384,1024]{1,0:T(8,128)(2,1)S(1)}, bf16[384,1024]{1,0:T(8,128)(2,1)S(1)}, u32[]{:S(2)}, u32[]{:S(2)}) collective-permute-start(bf16[384,1024]{1,0:T(8,128)(2,1)S(1)} %pad_maximum_fusion), channel_id=1, source_target_pairs={{0,16},{16,0},{32,48},{48,32},{64,80},{80,64},{96,112},{112,96},{1... | collective-permute-start | bytes 2359304 | tf_op jit(solution)/shard_map/ppermute | solution.py:30
  128.0 1.9 %collective-permute-done.43.refs_5_ = bf16[384,1024]{1,0:T(8,128)(2,1)S(1)} collective-permute-done((bf16[384,1024]{1,0:T(8,128)(2,1)S(1)}, bf16[384,1024]{1,0:T(8,128)(2,1)S(1)}, u32[]{:S(2)}, u32[]{:S(2)}) %collective-permute-start.43) | collective-permute-done | bytes 786464 | tf_op jit(solution)/shard_map/ppermute | solution.py:30
  (119 shorter events, 46.6 us)
Async XLA Ops:
  1.9 9.6 %collective-permute-start.7 = (bf16[512,256]{1,0:T(8,128)(2,1)S(1)}, bf16[512,256]{1,0:T(8,128)(2,1)S(1)}, u32[]{:S(2)}, u32[]{:S(2)}) collective-permute-start(bf16[512,256]{1,0:T(8,128)(2,1)S(1)} %get-tuple-element.35), channel_id=1, source_target_pairs={{0,1},{1,0},{2,3},{3,2},{4,5},{5,4},{6,7},{7,6},{8,9},{9,8},{10,11... | collective-permute-start | bytes 786440 | tf_op jit(solution)/shard_map/ppermute | solution.py:30
  4.4 12.4 %collective-permute-start.8 = (bf16[512,256]{1,0:T(8,128)(2,1)S(1)}, bf16[512,256]{1,0:T(8,128)(2,1)S(1)}, u32[]{:S(2)}, u32[]{:S(2)}) collective-permute-start(bf16[512,256]{1,0:T(8,128)(2,1)S(1)} %get-tuple-element.35), channel_id=1, source_target_pairs={{0,3},{1,2},{2,1},{3,0},{4,7},{5,6},{6,5},{7,4},{8,11},{9,10},{10,... | collective-permute-start | bytes 786440 | tf_op jit(solution)/shard_map/ppermute | solution.py:30
  6.7 12.4 %collective-permute-start.9 = (bf16[512,256]{1,0:T(8,128)(2,1)S(1)}, bf16[512,256]{1,0:T(8,128)(2,1)S(1)}, u32[]{:S(2)}, u32[]{:S(2)}) collective-permute-start(bf16[512,256]{1,0:T(8,128)(2,1)S(1)} %get-tuple-element.35), channel_id=1, source_target_pairs={{0,2},{1,3},{2,0},{3,1},{4,6},{5,7},{6,4},{7,5},{8,10},{9,11},{10,... | collective-permute-start | bytes 786440 | tf_op jit(solution)/shard_map/ppermute | solution.py:30
  7.7 14.6 %collective-permute-start = (bf16[512,256]{1,0:T(8,128)(2,1)S(1)}, bf16[512,256]{1,0:T(8,128)(2,1)S(1)}, u32[]{:S(2)}, u32[]{:S(2)}) collective-permute-start(bf16[512,256]{1,0:T(8,128)(2,1)S(1)} %get-tuple-element.34), channel_id=1, source_target_pairs={{0,4},{1,5},{2,6},{3,7},{4,0},{5,1},{6,2},{7,3},{8,12},{9,13},{10,... | collective-permute-start | bytes 786440 | tf_op jit(solution)/shard_map/ppermute | solution.py:30
  8.9 13.4 %collective-permute-start.1 = (bf16[512,256]{1,0:T(8,128)(2,1)S(1)}, bf16[512,256]{1,0:T(8,128)(2,1)S(1)}, u32[]{:S(2)}, u32[]{:S(2)}) collective-permute-start(bf16[512,256]{1,0:T(8,128)(2,1)S(1)} %get-tuple-element.34), channel_id=1, source_target_pairs={{0,12},{1,13},{2,14},{3,15},{4,8},{5,9},{6,10},{7,11},{8,4},{9,5},... | collective-permute-start | bytes 786440 | tf_op jit(solution)/shard_map/ppermute | solution.py:30
  11.5 10.9 %collective-permute-start.2 = (bf16[512,256]{1,0:T(8,128)(2,1)S(1)}, bf16[512,256]{1,0:T(8,128)(2,1)S(1)}, u32[]{:S(2)}, u32[]{:S(2)}) collective-permute-start(bf16[512,256]{1,0:T(8,128)(2,1)S(1)} %get-tuple-element.34), channel_id=1, source_target_pairs={{0,8},{1,9},{2,10},{3,11},{4,12},{5,13},{6,14},{7,15},{8,0},{9,1},... | collective-permute-start | bytes 786440 | tf_op jit(solution)/shard_map/ppermute | solution.py:30
  19.8 13.8 %collective-permute-start.10 = (bf16[4,256,256]{2,1,0:T(8,128)(2,1)S(1)}, bf16[4,256,256]{2,1,0:T(8,128)(2,1)S(1)}, u32[]{:S(2)}, u32[]{:S(2)}) collective-permute-start(bf16[4,256,256]{2,1,0:T(8,128)(2,1)S(1)} %pad_maximum_fusion.3.refs_3_), channel_id=1, source_target_pairs={{0,12},{1,13},{2,14},{3,15},{4,8},{5,9},{6,10},{7,11},{8,4},{9,5},... | collective-permute-start | bytes 1572872 | tf_op jit(solution)/shard_map/ppermute | solution.py:30
  22.4 11.6 %collective-permute-start.12 = (bf16[4,256,256]{2,1,0:T(8,128)(2,1)S(1)}, bf16[4,256,256]{2,1,0:T(8,128)(2,1)S(1)}, u32[]{:S(2)}, u32[]{:S(2)}) collective-permute-start(bf16[4,256,256]{2,1,0:T(8,128)(2,1)S(1)} %pad_maximum_fusion.3.refs_3_), channel_id=1, source_target_pairs={{0,4},{1,5},{2,6},{3,7},{4,0},{5,1},{6,2},{7,3},{8,12},{9,13},{10,... | collective-permute-start | bytes 1572872 | tf_op jit(solution)/shard_map/ppermute | solution.py:30
  22.5 13.1 %collective-permute-start.3 = (bf16[4,256,256]{2,1,0:T(8,128)(2,1)S(1)}, bf16[4,256,256]{2,1,0:T(8,128)(2,1)S(1)}, u32[]{:S(2)}, u32[]{:S(2)}) collective-permute-start(bf16[4,256,256]{2,1,0:T(8,128)(2,1)S(1)} %pad_maximum_fusion.2.refs_0_), channel_id=1, source_target_pairs={{0,3},{1,2},{2,1},{3,0},{4,7},{5,6},{6,5},{7,4},{8,11},{9,10},{10,... | collective-permute-start | bytes 1572872 | tf_op jit(solution)/shard_map/ppermute | solution.py:30
  24.6 11.2 %collective-permute-start.5 = (bf16[4,256,256]{2,1,0:T(8,128)(2,1)S(1)}, bf16[4,256,256]{2,1,0:T(8,128)(2,1)S(1)}, u32[]{:S(2)}, u32[]{:S(2)}) collective-permute-start(bf16[4,256,256]{2,1,0:T(8,128)(2,1)S(1)} %pad_maximum_fusion.2.refs_0_), channel_id=1, source_target_pairs={{0,1},{1,0},{2,3},{3,2},{4,5},{5,4},{6,7},{7,6},{8,9},{9,8},{10,11... | collective-permute-start | bytes 1572872 | tf_op jit(solution)/shard_map/ppermute | solution.py:30
  33.6 9.6 %collective-permute-start.11 = (bf16[2,256,256]{2,1,0:T(8,128)(2,1)S(1)}, bf16[2,256,256]{2,1,0:T(8,128)(2,1)S(1)}, u32[]{:S(2)}, u32[]{:S(2)}) collective-permute-start(bf16[2,256,256]{2,1,0:T(8,128)(2,1)S(1)} %slice.115), channel_id=1, source_target_pairs={{0,4},{1,5},{2,6},{3,7},{4,0},{5,1},{6,2},{7,3},{8,12},{9,13},{10,... | collective-permute-start | bytes 786440 | tf_op jit(solution)/shard_map/ppermute | solution.py:30
  43.2 10.2 %collective-permute-start.16 = (bf16[4,256,256]{2,1,0:T(8,128)(2,1)S(1)}, bf16[4,256,256]{2,1,0:T(8,128)(2,1)S(1)}, u32[]{:S(2)}, u32[]{:S(2)}) collective-permute-start(bf16[4,256,256]{2,1,0:T(8,128)(2,1)S(1)} %pad_maximum_fusion.4.refs_3_), channel_id=1, source_target_pairs={{0,4},{1,5},{2,6},{3,7},{4,0},{5,1},{6,2},{7,3},{8,12},{9,13},{10,... | collective-permute-start | bytes 1572872 | tf_op jit(solution)/shard_map/ppermute | solution.py:30
  44.1 11.4 %collective-permute-start.17 = (bf16[4,256,256]{2,1,0:T(8,128)(2,1)S(1)}, bf16[4,256,256]{2,1,0:T(8,128)(2,1)S(1)}, u32[]{:S(2)}, u32[]{:S(2)}) collective-permute-start(bf16[4,256,256]{2,1,0:T(8,128)(2,1)S(1)} %pad_maximum_fusion.4.refs_3_), channel_id=1, source_target_pairs={{0,12},{1,13},{2,14},{3,15},{4,8},{5,9},{6,10},{7,11},{8,4},{9,5},... | collective-permute-start | bytes 1572872 | tf_op jit(solution)/shard_map/ppermute | solution.py:30
  45.1 10.5 %collective-permute-start.14 = (bf16[4,256,256]{2,1,0:T(8,128)(2,1)S(1)}, bf16[4,256,256]{2,1,0:T(8,128)(2,1)S(1)}, u32[]{:S(2)}, u32[]{:S(2)}) collective-permute-start(bf16[4,256,256]{2,1,0:T(8,128)(2,1)S(1)} %pad_maximum_fusion.1.refs_0_), channel_id=1, source_target_pairs={{0,1},{1,0},{2,3},{3,2},{4,5},{5,4},{6,7},{7,6},{8,9},{9,8},{10,11... | collective-permute-start | bytes 1572872 | tf_op jit(solution)/shard_map/ppermute | solution.py:30
  45.9 11.4 %collective-permute-start.15 = (bf16[4,256,256]{2,1,0:T(8,128)(2,1)S(1)}, bf16[4,256,256]{2,1,0:T(8,128)(2,1)S(1)}, u32[]{:S(2)}, u32[]{:S(2)}) collective-permute-start(bf16[4,256,256]{2,1,0:T(8,128)(2,1)S(1)} %pad_maximum_fusion.1.refs_0_), channel_id=1, source_target_pairs={{0,3},{1,2},{2,1},{3,0},{4,7},{5,6},{6,5},{7,4},{8,11},{9,10},{10,... | collective-permute-start | bytes 1572872 | tf_op jit(solution)/shard_map/ppermute | solution.py:30
  50.3 12.8 %collective-permute-start.25 = (f16[272,1024]{1,0:T(8,128)(2,1)S(1)}, f16[272,1024]{1,0:T(8,128)(2,1)S(1)}, u32[]{:S(2)}, u32[]{:S(2)}) collective-permute-start(f16[272,1024]{1,0:T(8,128)(2,1)S(1)} %convert_element_type.39), channel_id=1, source_target_pairs={{0,64},{16,80},{32,96},{48,112},{64,0},{80,16},{96,32},{112,48},{1... | collective-permute-start | bytes 1671176 | tf_op jit(solution)/shard_map/ppermute | solution.py:30
  53.4 11.5 %collective-permute-start.21 = (bf16[2,256,256]{2,1,0:T(8,128)(2,1)S(1)}, bf16[2,256,256]{2,1,0:T(8,128)(2,1)S(1)}, u32[]{:S(2)}, u32[]{:S(2)}) collective-permute-start(bf16[2,256,256]{2,1,0:T(8,128)(2,1)S(1)} %slice.101), channel_id=1, source_target_pairs={{0,12},{1,13},{2,14},{3,15},{4,8},{5,9},{6,10},{7,11},{8,4},{9,5},... | collective-permute-start | bytes 786440 | tf_op jit(solution)/shard_map/ppermute | solution.py:30
  55.5 9.5 %collective-permute-start.20 = (bf16[2,256,256]{2,1,0:T(8,128)(2,1)S(1)}, bf16[2,256,256]{2,1,0:T(8,128)(2,1)S(1)}, u32[]{:S(2)}, u32[]{:S(2)}) collective-permute-start(bf16[2,256,256]{2,1,0:T(8,128)(2,1)S(1)} %slice.100), channel_id=1, source_target_pairs={{0,4},{1,5},{2,6},{3,7},{4,0},{5,1},{6,2},{7,3},{8,12},{9,13},{10,... | collective-permute-start | bytes 786440 | tf_op jit(solution)/shard_map/ppermute | solution.py:30
  63.1 15.6 %collective-permute-start.27 = (f16[136,1024]{1,0:T(8,128)(2,1)S(1)}, f16[136,1024]{1,0:T(8,128)(2,1)S(1)}, u32[]{:S(2)}, u32[]{:S(2)}) collective-permute-start(f16[136,1024]{1,0:T(8,128)(2,1)S(1)} %convert_element_type.41), channel_id=1, source_target_pairs={{0,96},{16,112},{32,64},{48,80},{64,32},{80,48},{96,0},{112,16},{1... | collective-permute-start | bytes 835592 | tf_op jit(solution)/shard_map/ppermute | solution.py:30
  64.9 15.4 %collective-permute-start.23 = (f16[136,1024]{1,0:T(8,128)(2,1)S(1)}, f16[136,1024]{1,0:T(8,128)(2,1)S(1)}, u32[]{:S(2)}, u32[]{:S(2)}) collective-permute-start(f16[136,1024]{1,0:T(8,128)(2,1)S(1)} %convert_element_type.40), channel_id=1, source_target_pairs={{0,32},{16,48},{32,0},{48,16},{64,96},{80,112},{96,64},{112,80},{1... | collective-permute-start | bytes 835592 | tf_op jit(solution)/shard_map/ppermute | solution.py:30
  68.5 11.8 %collective-permute-start.26 = (f16[136,1024]{1,0:T(8,128)(2,1)S(1)}, f16[136,1024]{1,0:T(8,128)(2,1)S(1)}, u32[]{:S(2)}, u32[]{:S(2)}) collective-permute-start(f16[136,1024]{1,0:T(8,128)(2,1)S(1)} %get-tuple-element.54), channel_id=1, source_target_pairs={{0,16},{16,0},{32,48},{48,32},{64,80},{80,64},{96,112},{112,96},{1... | collective-permute-start | bytes 835592 | tf_op jit(solution)/shard_map/ppermute | solution.py:30
  78.7 9.6 %collective-permute-start.28 = (f16[136,1024]{1,0:T(8,128)(2,1)S(1)}, f16[136,1024]{1,0:T(8,128)(2,1)S(1)}, u32[]{:S(2)}, u32[]{:S(2)}) collective-permute-start(f16[136,1024]{1,0:T(8,128)(2,1)S(1)} %convert_element_type.48), channel_id=1, source_target_pairs={{0,112},{16,96},{32,80},{48,64},{64,48},{80,32},{96,16},{112,0},{1... | collective-permute-start | bytes 835592 | tf_op jit(solution)/shard_map/ppermute | solution.py:30
  111.9 11.7 %collective-permute-start.40 = (bf16[128,1024]{1,0:T(8,128)(2,1)S(1)}, bf16[128,1024]{1,0:T(8,128)(2,1)S(1)}, u32[]{:S(2)}, u32[]{:S(2)}) collective-permute-start(bf16[128,1024]{1,0:T(8,128)(2,1)S(1)} %get-tuple-element.61.refs_0_), channel_id=1, source_target_pairs={{0,64},{16,80},{32,96},{48,112},{64,0},{80,16},{96,32},{112,48},{1... | collective-permute-start | bytes 786440 | tf_op jit(solution)/shard_map/ppermute | solution.py:30
  112.3 11.3 %collective-permute-start.41 = (bf16[128,1024]{1,0:T(8,128)(2,1)S(1)}, bf16[128,1024]{1,0:T(8,128)(2,1)S(1)}, u32[]{:S(2)}, u32[]{:S(2)}) collective-permute-start(bf16[128,1024]{1,0:T(8,128)(2,1)S(1)} %get-tuple-element.61.refs_0_), channel_id=1, source_target_pairs={{0,32},{16,48},{32,0},{48,16},{64,96},{80,112},{96,64},{112,80},{1... | collective-permute-start | bytes 786440 | tf_op jit(solution)/shard_map/ppermute | solution.py:30
  (25 other events, 190.3 us)

commit v4 on v3

--- a/solution.py
+++ b/solution.py
@@ -97,25 +97,38 @@
     return jnp.dot(left, right, preferred_element_type=jnp.float32)
 
 
-def early_kernel(place_ref, *refs):
-    a_refs, b_refs, cotangent = refs[:3], refs[3:6], refs[6]
-    a_acc, b_acc, buffer, sems = refs[7:]
-    wanted = [(x, z) for z in range(4) for x in range(4) if (x, z) != (3, 3)]
+def own_kernel(place_ref, *refs):
+    sides, cotangent, outs, buffer, sems = (refs[:2], refs[2:4]), refs[4], refs[5:7], refs[7], refs[8]
+    lines = [(x, 0) for x in range(4)], [(0, z) for z in range(4)]
+    copies = fetch(place_ref[0], cotangent, buffer, sems, [*lines[0], *lines[1][1:]])
+    for chunks, line, out in zip(sides, lines, outs):
+        for at in line:
+            if at in copies:
+                copies.pop(at).wait()
+        left = [jnp.concatenate([chunk[i] for chunk in chunks], axis=0) for i in range(4)]
+        out[...] = line_product(left, [buffer[slot(*at)] for at in line])
+
+
+def early_kernel(chunk, place_ref, *refs):
+    sides, sums, cotangent = (refs[:2], refs[2:4]), refs[4:6], refs[6]
+    outs, buffer, sems = refs[7:9], refs[9], refs[10]
+    lines = (
+        [[(x, z) for x in range(4)] for z in (1, 2)],
+        [[(x, z) for z in range(4)] for x in (1, 2)],
+    )
+    wanted = list(dict.fromkeys(at for side in lines for line in side for at in line))
     copies = fetch(place_ref[0], cotangent, buffer, sems, wanted)
-    for z in range(3):
-        for x in range(4):
-            copies[(x, z)].wait()
-        part = line_product(
-            [a_refs[z][x] for x in range(4)], [buffer[slot(x, z)] for x in range(4)]
-        )
-        a_acc[...] = part if z == 0 else a_acc[...] + part
-    for x in range(3):
-        copies[(x, 3)].wait()
-    for x in range(3):
-        part = line_product(
-            [b_refs[x][z] for z in range(4)], [buffer[slot(x, z)] for z in range(4)]
-        )
-        b_acc[...] = part if x == 0 else b_acc[...] + part
+    for pieces, before, side, out in zip(sides, sums, lines, outs):
+        rows = out.shape[0]
+        total = before[chunk * rows : (chunk + 1) * rows, :]
+        for piece, line in zip(pieces, side):
+            for at in line:
+                if at in copies:
+                    copies.pop(at).wait()
+            total = total + line_product(
+                [piece[i] for i in range(4)], [buffer[slot(*at)] for at in line]
+            )
+        out[...] = total
 
 
 def late_kernel(owners, whole, paired, place_ref, *refs):
@@ -161,22 +174,21 @@
     ]
 
 
-def early_product(place, a_pieces, b_pieces, cotangent):
+def early_product(kernel, rows, share, place, operands, cotangent):
     tokens, columns = cotangent.shape
-    features = a_pieces[0].shape[1]
-    return pl.pallas_call(
-        early_kernel,
-        out_shape=[jax.ShapeDtypeStruct((features, columns), jnp.float32)] * 2,
-        in_specs=[SMEM] + [WHOLE] * 6 + [HBM],
+    return pl.pallas_call(
+        kernel,
+        out_shape=[jax.ShapeDtypeStruct((rows, columns), jnp.float32)] * 2,
+        in_specs=[SMEM] + [WHOLE] * len(operands) + [HBM],
         out_specs=[WHOLE] * 2,
         scratch_shapes=product_scratch(cotangent),
         compiler_params=pltpu.CompilerParams(vmem_limit_bytes=14 * MIB),
         cost_estimate=pl.CostEstimate(
-            flops=3 * tokens * columns * features,
+            flops=int(share * 4 * tokens * columns * rows),
             bytes_accessed=2 * tokens * columns,
             transcendentals=0,
         ),
-    )(place, *a_pieces, *b_pieces, cotangent)
+    )(place, *operands, cotangent)
 
 
 def late_product(owners, paired, place, sums, a_pieces, b_pieces, cotangent):
@@ -229,22 +241,34 @@
     )(*blocks)
 
 
-def join_kernel(distances, own, *refs):
+def join_kernel(distances, last, own, *refs):
     received, out = refs[:-1], refs[-1]
-    out[...] = jnp.zeros_like(out)
-    for (k, l), row in ROW.items():
-        total = own[row : row + 1, :]
+    rows = []
+    for k, l in PAIRS:
+        total = own[ROW[(k, l)] : ROW[(k, l)] + 1, :]
         for d, other in zip(distances, received):
             at = row_of(k ^ d, l ^ d)
             total = total + other[at : at + 1, :]
-        out[row : row + 1, :] = total
-
-
-def join(own, distances):
+        rows.append(total)
+    if not last:
+        for row, total in enumerate(rows):
+            out[row : row + 1, :] = total
+        out[len(rows) :, :] = jnp.zeros((PAIR_ROWS - len(rows), 128), jnp.float32)
+        return
+    lane = lax.broadcasted_iota(jnp.int32, (8, 128), 1)
+    rows += [jnp.zeros_like(rows[0])] * (PAIR_ROWS - len(rows))
+    packed = jnp.zeros((8, 128), jnp.float32)
+    for i in range(PAIR_ROWS // 8):
+        value = jnp.sum(jnp.concatenate(rows[8 * i : 8 * i + 8], axis=0), axis=1, keepdims=True)
+        packed = jnp.where(lane // 16 == i, value, packed)
+    out[...] = packed
+
+
+def join(own, distances, last):
     received = [swap(own, "rep", d) for d in distances]
     return pl.pallas_call(
-        functools.partial(join_kernel, distances),
-        out_shape=jax.ShapeDtypeStruct(own.shape, own.dtype),
+        functools.partial(join_kernel, distances, last),
+        out_shape=jax.ShapeDtypeStruct((8, 128) if last else own.shape, own.dtype),
         in_specs=[WHOLE] * (1 + len(received)),
         out_specs=WHOLE,
         compiler_params=pltpu.CompilerParams(vmem_limit_bytes=1 * MIB),
@@ -252,11 +276,9 @@
 
 
 def coefficients(total):
-    value = jnp.sum(total, axis=1, keepdims=True)
-
     def inner(k, l):
         at = row_of(k, l)
-        return value[at : at + 1, :]
+        return total[at % 8 : at % 8 + 1, 16 * (at // 8) : 16 * (at // 8) + 1]
 
     def weigh(inner, count):
         half = count // 2
@@ -382,22 +404,30 @@
     b_line = spread(b, 1)
     blocks = [None] * 8
     before, sent = [], []
+    stacks = [
+        [jnp.stack([piece[c * 2 * BLOCK : (c + 1) * 2 * BLOCK] for piece in line]) for c in range(2)]
+        for line in (a_line, b_line)
+    ]
+    own = early_product(own_kernel, 4 * BLOCK, 1 / 4, place, stacks[0] + stacks[1], cotangent)
     for chunk, (a_owners, b_owners) in enumerate(CHUNKS):
-        rows = slice(chunk * 2 * BLOCK, (chunk + 1) * 2 * BLOCK)
-        a_own = after(jnp.stack([piece[rows] for piece in a_line]), *before)
-        b_own = after(jnp.stack([piece[rows] for piece in b_line]), *before)
+        a_own, b_own = (after(line[chunk], *before) for line in stacks)
         a_near, a_far = swap(a_own, "tp", 1), swap(a_own, "tp", 3)
         b_near, b_far = swap(b_own, "tp", 4), swap(b_own, "tp", 12)
         if chunk:
             a_opposite = forward(after(a_near, *sent), after(a_far, *sent), 1)
             b_opposite = forward(after(b_near, *sent), after(b_far, *sent), 4)
         else:
-            a_opposite = forward(a_near, a_far, 1)
-            b_opposite = forward(b_near, b_far, 4)
+            a_opposite = forward(after(a_near, *own), after(a_far, *own), 1)
+            b_opposite = forward(after(b_near, *own), after(b_far, *own), 4)
         sums = early_product(
-            place, [a_own, a_near, a_far], [b_own, b_near, b_far], cotangent
+            functools.partial(early_kernel, chunk),
+            2 * BLOCK,
+            1 / 2,
+            place,
+            [a_near, a_far, b_near, b_far, *own],
+            cotangent,
         )
-        before = [*a_opposite, *b_opposite, *sums]
+        before = sums
         owners = a_owners + b_owners
         values = late_product(owners, not chunk, place, sums, a_opposite, b_opposite, cotangent)
         if chunk:
@@ -413,8 +443,8 @@
             pair = swap(sent[0], "rep", 4)
             blocks[4] = widen(pair[: BLOCK + EXTRA])
     sums = gram(blocks)
-    sums = join(sums, (1,))
-    sums = join(sums, (2, 4, 6))
+    sums = join(sums, (1,), False)
+    sums = join(sums, (2, 4, 6), True)
     sums = sums + swap(sums, "tp", 1) + swap(sums, "tp", 2) + swap(sums, "tp", 3)
     sums = [sums] + [swap(sums, "tp", d) for d in (4, 8, 12)]
     mine, coef = adam(sums, blocks, master, moment, second)

time: 132 us -> 129 us (0.977)
  waiting for transfers between devices: 30.6 us -> 26.4 us
  Pallas kernels: 24.2 us -> 26.6 us
  starting transfers between devices: 69.3 us -> 67.8 us
    ppermute x44, waiting for transfers between devices: 30.6 us -> 26.4 us  [swap(): lax.ppermute(value, axis, [(i, i ^ distance) for i in range(lax.axis_size...]
    pallas_call x4 -> x5, Pallas kernels: 10.9 us -> 13.1 us  [the longest x3 12.9 us: early_product(): pl.pallas_call(kernel, out_shape=[jax.ShapeDtypeStruct((rows, columns), j...]
    ppermute x44, starting transfers between devices: 69.3 us -> 67.8 us  [swap(): lax.ppermute(value, axis, [(i, i ^ distance) for i in range(lax.axis_size...]
  transfers between devices with their start and end apart: 44 -> 44, of which waited for: 14 -> 14; matrix products, arithmetic and copies ran while one was open for 4% -> 5% of each run, Pallas kernels for 15% -> 17%
where the time goes in v4:
time: 129 us
  starting transfers between devices  67.8 us (53%)
  Pallas kernels  26.6 us (21%)
  waiting for transfers between devices  26.4 us (20%)
  local copies, waits for them, and re-layouts  4.01 us (3%)
  other arithmetic  2.9 us (2%)
    ppermute x44, starting transfers between devices, swap(): lax.ppermute(value, axis, [(i, i ^ distance) for i in range(lax.axis_size...  67.8 us
    ppermute x44, waiting for transfers between devices, swap(): lax.ppermute(value, axis, [(i, i ^ distance) for i in range(lax.axis_size...  26.4 us
    pallas_call x3, Pallas kernels, early_product(): pl.pallas_call(kernel, out_shape=[jax.ShapeDtypeStruct((rows, columns), j...  12.9 us
    pallas_call x2, Pallas kernels, late_product(): pl.pallas_call(functools.partial(late_kernel, owners, len(a_pieces) == 1,...  6.77 us
    pallas_call x2, Pallas kernels, adam(): pl.pallas_call(functools.partial(adam_kernel, first), out_shape=outs, in_...  3.74 us
    another operation x7, local copies, waits for them, and re-layouts, per_device(): jnp.stack([piece[c * 2 * BLOCK:(c + 1) * 2 * BLOCK] for piece in line])  2.81 us
  transfers between devices with their start and end apart: 44, of which 14 were waited for; matrix products, arithmetic and copies ran while one was open for 5% of the time, Pallas kernels for 17%

profile of v4, /device:TPU:1, one launch (start us, length us, event | category | flops | bytes accessed | tf_op | source)
XLA Modules:
  0.0 128.9 jit_solution(16364055605370303766)
XLA Ops:
  1.9 2.5 %collective-permute-start.5 = (bf16[512,256]{1,0:T(8,128)(2,1)S(1)}, bf16[512,256]{1,0:T(8,128)(2,1)S(1)}, u32[]{:S(2)}, u32[]{:S(2)}) collective-permute-start(bf16[512,256]{1,0:T(8,128)(2,1)S(1)} %get-tuple-element.41), channel_id=1, source_target_pairs={{0,1},{1,0},{2,3},{3,2},{4,5},{5,4},{6,7},{7,6},{8,9},{9,8},{10,11... | collective-permute-start | bytes 786440 | tf_op jit(solution)/shard_map/ppermute | solution.py:30
  4.4 2.2 %collective-permute-start.6 = (bf16[512,256]{1,0:T(8,128)(2,1)S(1)}, bf16[512,256]{1,0:T(8,128)(2,1)S(1)}, u32[]{:S(2)}, u32[]{:S(2)}) collective-permute-start(bf16[512,256]{1,0:T(8,128)(2,1)S(1)} %get-tuple-element.41), channel_id=1, source_target_pairs={{0,3},{1,2},{2,1},{3,0},{4,7},{5,6},{6,5},{7,4},{8,11},{9,10},{10,... | collective-permute-start | bytes 786440 | tf_op jit(solution)/shard_map/ppermute | solution.py:30
  13.1 3.7 %collective-permute-done.6 = bf16[512,256]{1,0:T(8,128)(2,1)S(1)} collective-permute-done((bf16[512,256]{1,0:T(8,128)(2,1)S(1)}, bf16[512,256]{1,0:T(8,128)(2,1)S(1)}, u32[]{:S(2)}, u32[]{:S(2)}) %collective-permute-start.6) | collective-permute-done | bytes 262176 | tf_op jit(solution)/shard_map/ppermute | solution.py:30
  16.8 2.2 %collective-permute-done.7 = bf16[512,256]{1,0:T(8,128)(2,1)S(1)} collective-permute-done((bf16[512,256]{1,0:T(8,128)(2,1)S(1)}, bf16[512,256]{1,0:T(8,128)(2,1)S(1)}, u32[]{:S(2)}, u32[]{:S(2)}) %collective-permute-start.7) | collective-permute-done | bytes 262176 | tf_op jit(solution)/shard_map/ppermute | solution.py:30
  28.0 4.2 %shard_map.93 = (f32[512,1024]{1,0:T(8,128)S(1)}, f32[512,1024]{1,0:T(8,128)S(1)}) custom-call(s32[1]{0:T(128)} %bitcast.place_ref, bf16[4,256,256]{2,1,0:T(8,128)(2,1)S(1)} %pad_maximum_fusion.2.refs_0_, bf16[4,256,256]{2,1,0:T(8,128)(2,1)S(1)} %pad_maximum_fusion.1.refs_1_, bf16[4,256,256]{2,1,0:T(8,128)(2,1)S(1)} %pad_maximum_fusion.3.refs_2_, ...), custom_call_target="tpu_custom_call" | custom-call | flops 2147483648 | bytes 8388608 | tf_op jit(solution)/shard_map/pallas_call | solution.py:179
  33.8 2.0 %collective-permute-done.3.refs_0_ = bf16[4,256,256]{2,1,0:T(8,128)(2,1)S(1)} collective-permute-done((bf16[4,256,256]{2,1,0:T(8,128)(2,1)S(1)}, bf16[4,256,256]{2,1,0:T(8,128)(2,1)S(1)}, u32[]{:S(2)}, u32[]{:S(2)}) %collective-permute-start.3) | collective-permute-done | bytes 524320 | tf_op jit(solution)/shard_map/ppermute | solution.py:30
  37.2 4.4 %shard_map.94 = (f32[256,1024]{1,0:T(8,128)S(1)}, f32[256,1024]{1,0:T(8,128)S(1)}) custom-call(s32[1]{0:T(128)} %bitcast.place_ref, bf16[4,256,256]{2,1,0:T(8,128)(2,1)S(1)} %collective-permute-done.3.refs_0_, bf16[4,256,256]{2,1,0:T(8,128)(2,1)S(1)} %collective-permute-done.4.refs_1_, bf16[4,256,256]{2,1,0:T(8,128)(2,1)S(1)} %collective-permute-done.8.refs_2_, ...), custom_call_target="tpu_custom_call" | custom-call | flops 2147483648 | bytes 8388608 | tf_op jit(solution)/shard_map/pallas_call | solution.py:179
  45.5 3.4 %shard_map.96 = (f32[272,1024]{1,0:T(8,128)S(1)}, f32[136,1024]{1,0:T(8,128)S(1)}, f32[136,1024]{1,0:T(8,128)S(1)}) custom-call(s32[1]{0:T(128)} %bitcast.place_ref, f32[256,1024]{1,0:T(8,128)S(1)} %get-tuple-element.44.refs_0_, f32[256,1024]{1,0:T(8,128)S(1)} %get-tuple-element.45.refs_1_, bf16[2,256,256]{2,1,0:T(8,128)(2,1)S(1)} %collective-permute-done.14.refs_2_, ...), custom_call_target="tpu_custom_call" | custom-call | flops 1073741824 | bytes 4194304 | tf_op jit(solution)/shard_map/pallas_call | solution.py:199
  49.0 3.0 %collective-permute-start.25 = (f16[272,1024]{1,0:T(8,128)(2,1)S(1)}, f16[272,1024]{1,0:T(8,128)(2,1)S(1)}, u32[]{:S(2)}, u32[]{:S(2)}) collective-permute-start(f16[272,1024]{1,0:T(8,128)(2,1)S(1)} %convert_element_type.39), channel_id=1, source_target_pairs={{0,64},{16,80},{32,96},{48,112},{64,0},{80,16},{96,32},{112,48},{1... | collective-permute-start | bytes 1671176 | tf_op jit(solution)/shard_map/ppermute | solution.py:30
  52.1 2.2 %collective-permute-start.21 = (bf16[2,256,256]{2,1,0:T(8,128)(2,1)S(1)}, bf16[2,256,256]{2,1,0:T(8,128)(2,1)S(1)}, u32[]{:S(2)}, u32[]{:S(2)}) collective-permute-start(bf16[2,256,256]{2,1,0:T(8,128)(2,1)S(1)} %slice.101), channel_id=1, source_target_pairs={{0,12},{1,13},{2,14},{3,15},{4,8},{5,9},{6,10},{7,11},{8,4},{9,5},... | collective-permute-start | bytes 786440 | tf_op jit(solution)/shard_map/ppermute | solution.py:30
  56.0 4.4 %shard_map.95 = (f32[256,1024]{1,0:T(8,128)S(1)}, f32[256,1024]{1,0:T(8,128)S(1)}) custom-call(s32[1]{0:T(128)} %bitcast.place_ref, bf16[4,256,256]{2,1,0:T(8,128)(2,1)S(1)} %collective-permute-done.10.refs_0_, bf16[4,256,256]{2,1,0:T(8,128)(2,1)S(1)} %collective-permute-done.11.refs_1_, bf16[4,256,256]{2,1,0:T(8,128)(2,1)S(1)} %collective-permute-done.12.refs_2_, ...), custom_call_target="tpu_custom_call" | custom-call | flops 2147483648 | bytes 8388608 | tf_op jit(solution)/shard_map/pallas_call | solution.py:179
  60.4 2.6 %collective-permute-start.27 = (f16[136,1024]{1,0:T(8,128)(2,1)S(1)}, f16[136,1024]{1,0:T(8,128)(2,1)S(1)}, u32[]{:S(2)}, u32[]{:S(2)}) collective-permute-start(f16[136,1024]{1,0:T(8,128)(2,1)S(1)} %convert_element_type.41), channel_id=1, source_target_pairs={{0,96},{16,112},{32,64},{48,80},{64,32},{80,48},{96,0},{112,16},{1... | collective-permute-start | bytes 835592 | tf_op jit(solution)/shard_map/ppermute | solution.py:30
  63.1 3.4 %shard_map.97 = (f32[136,1024]{1,0:T(8,128)S(1)}, f32[136,1024]{1,0:T(8,128)S(1)}, f32[136,1024]{1,0:T(8,128)S(1)}, f32[136,1024]{1,0:T(8,128)S(1)}) custom-call(s32[1]{0:T(128)} %bitcast.place_ref, f32[256,1024]{1,0:T(8,128)S(1)} %get-tuple-element.48.refs_0_, f32[256,1024]{1,0:T(8,128)S(1)} %get-tuple-element.49.refs_1_, ...), custom_call_target="tpu_custom_call" | custom-call | flops 1073741824 | bytes 4194304 | tf_op jit(solution)/shard_map/pallas_call | solution.py:199
  66.6 8.6 %collective-permute-start.22 = (f16[136,1024]{1,0:T(8,128)(2,1)S(1)}, f16[136,1024]{1,0:T(8,128)(2,1)S(1)}, u32[]{:S(2)}, u32[]{:S(2)}) collective-permute-start(f16[136,1024]{1,0:T(8,128)(2,1)S(1)} %convert_element_type.42), channel_id=1, source_target_pairs={{0,16},{16,0},{32,48},{48,32},{64,80},{80,64},{96,112},{112,96},{1... | collective-permute-start | bytes 835592 | tf_op jit(solution)/shard_map/ppermute | solution.py:30
  77.5 6.5 %collective-permute-done.24 = f16[136,1024]{1,0:T(8,128)(2,1)S(1)} collective-permute-done((f16[136,1024]{1,0:T(8,128)(2,1)S(1)}, f16[136,1024]{1,0:T(8,128)(2,1)S(1)}, u32[]{:S(2)}, u32[]{:S(2)}) %collective-permute-start.24) | collective-permute-done | bytes 278560 | tf_op jit(solution)/shard_map/ppermute | solution.py:30
  84.0 2.7 %collective-permute-done.28 = f16[136,1024]{1,0:T(8,128)(2,1)S(1)} collective-permute-done((f16[136,1024]{1,0:T(8,128)(2,1)S(1)}, f16[136,1024]{1,0:T(8,128)(2,1)S(1)}, u32[]{:S(2)}, u32[]{:S(2)}) %collective-permute-start.28) | collective-permute-done | bytes 278560 | tf_op jit(solution)/shard_map/ppermute | solution.py:30
  90.8 2.7 %collective-permute-start.32 = (f32[40,128]{1,0:T(8,128)S(1)}, f32[40,128]{1,0:T(8,128)S(1)}, u32[]{:S(2)}, u32[]{:S(2)}) collective-permute-start(f32[40,128]{1,0:T(8,128)S(1)} %shard_map.99.own), channel_id=1, source_target_pairs={{0,96},{16,112},{32,64},{48,80},{64,32},{80,48},{96,0},{112,16},{1... | collective-permute-start | bytes 61448 | tf_op jit(solution)/shard_map/ppermute | solution.py:30
  101.6 2.5 %collective-permute-start.37 = (f32[8,128]{1,0:T(8,128)S(1)}, f32[8,128]{1,0:T(8,128)S(1)}, u32[]{:S(2)}, u32[]{:S(2)}) collective-permute-start(f32[8,128]{1,0:T(8,128)S(1)} %add_add_fusion.refs_0_), channel_id=1, source_target_pairs={{0,8},{1,9},{2,10},{3,11},{4,12},{5,13},{6,14},{7,15},{8,0},{9,1},... | collective-permute-start | bytes 12296 | tf_op jit(solution)/shard_map/ppermute | solution.py:30
  105.6 2.2 %collective-permute-done.38.refs_3_ = f32[8,128]{1,0:T(8,128)S(1)} collective-permute-done((f32[8,128]{1,0:T(8,128)S(1)}, f32[8,128]{1,0:T(8,128)S(1)}, u32[]{:S(2)}, u32[]{:S(2)}) %collective-permute-start.38) | collective-permute-done | bytes 4128 | tf_op jit(solution)/shard_map/ppermute | solution.py:30
  110.0 2.0 %collective-permute-start.41 = (bf16[128,1024]{1,0:T(8,128)(2,1)S(1)}, bf16[128,1024]{1,0:T(8,128)(2,1)S(1)}, u32[]{:S(2)}, u32[]{:S(2)}) collective-permute-start(bf16[128,1024]{1,0:T(8,128)(2,1)S(1)} %get-tuple-element.73.refs_0_), channel_id=1, source_target_pairs={{0,32},{16,48},{32,0},{48,16},{64,96},{80,112},{96,64},{112,80},{1... | collective-permute-start | bytes 786440 | tf_op jit(solution)/shard_map/ppermute | solution.py:30
  112.6 5.7 %collective-permute-start.39 = (bf16[128,1024]{1,0:T(8,128)(2,1)S(1)}, bf16[128,1024]{1,0:T(8,128)(2,1)S(1)}, u32[]{:S(2)}, u32[]{:S(2)}) collective-permute-start(bf16[128,1024]{1,0:T(8,128)(2,1)S(1)} %get-tuple-element.73.refs_0_), channel_id=1, source_target_pairs={{0,16},{16,0},{32,48},{48,32},{64,80},{80,64},{96,112},{112,96},{1... | collective-permute-start | bytes 786440 | tf_op jit(solution)/shard_map/ppermute | solution.py:30
  118.2 2.3 %shard_map.102 = (f32[128,1024]{1,0:T(8,128)}, f32[128,1024]{1,0:T(8,128)}, f32[128,1024]{1,0:T(8,128)}, f32[128,1024]{1,0:T(8,128)}) custom-call(f32[8,128]{1,0:T(8,128)S(1)} %get-tuple-element.68.refs_0_, f32[136,1024]{1,0:T(8,128)S(1)} %get-tuple-element.61.refs_0_.refs_4_.refs_1_, f32[136,1024]{1,0:T(8,128)S(1)} %convert_element_type.43.refs_1_.refs_5_.refs_2_, ...), custom_call_target="tpu_custom_call" | custom-call | tf_op jit(solution)/shard_map/pallas_call | solution.py:354
  120.6 4.8 %collective-permute-start.43 = (bf16[384,1024]{1,0:T(8,128)(2,1)S(1)}, bf16[384,1024]{1,0:T(8,128)(2,1)S(1)}, u32[]{:S(2)}, u32[]{:S(2)}) collective-permute-start(bf16[384,1024]{1,0:T(8,128)(2,1)S(1)} %pad_maximum_fusion), channel_id=1, source_target_pairs={{0,16},{16,0},{32,48},{48,32},{64,80},{80,64},{96,112},{112,96},{1... | collective-permute-start | bytes 2359304 | tf_op jit(solution)/shard_map/ppermute | solution.py:30
  125.5 1.9 %collective-permute-done.43.refs_5_ = bf16[384,1024]{1,0:T(8,128)(2,1)S(1)} collective-permute-done((bf16[384,1024]{1,0:T(8,128)(2,1)S(1)}, bf16[384,1024]{1,0:T(8,128)(2,1)S(1)}, u32[]{:S(2)}, u32[]{:S(2)}) %collective-permute-start.43) | collective-permute-done | bytes 786464 | tf_op jit(solution)/shard_map/ppermute | solution.py:30
  (118 shorter events, 45.7 us)
Async XLA Ops:
  1.9 9.6 %collective-permute-start.5 = (bf16[512,256]{1,0:T(8,128)(2,1)S(1)}, bf16[512,256]{1,0:T(8,128)(2,1)S(1)}, u32[]{:S(2)}, u32[]{:S(2)}) collective-permute-start(bf16[512,256]{1,0:T(8,128)(2,1)S(1)} %get-tuple-element.41), channel_id=1, source_target_pairs={{0,1},{1,0},{2,3},{3,2},{4,5},{5,4},{6,7},{7,6},{8,9},{9,8},{10,11... | collective-permute-start | bytes 786440 | tf_op jit(solution)/shard_map/ppermute | solution.py:30
  4.4 12.4 %collective-permute-start.6 = (bf16[512,256]{1,0:T(8,128)(2,1)S(1)}, bf16[512,256]{1,0:T(8,128)(2,1)S(1)}, u32[]{:S(2)}, u32[]{:S(2)}) collective-permute-start(bf16[512,256]{1,0:T(8,128)(2,1)S(1)} %get-tuple-element.41), channel_id=1, source_target_pairs={{0,3},{1,2},{2,1},{3,0},{4,7},{5,6},{6,5},{7,4},{8,11},{9,10},{10,... | collective-permute-start | bytes 786440 | tf_op jit(solution)/shard_map/ppermute | solution.py:30
  6.7 12.4 %collective-permute-start.7 = (bf16[512,256]{1,0:T(8,128)(2,1)S(1)}, bf16[512,256]{1,0:T(8,128)(2,1)S(1)}, u32[]{:S(2)}, u32[]{:S(2)}) collective-permute-start(bf16[512,256]{1,0:T(8,128)(2,1)S(1)} %get-tuple-element.41), channel_id=1, source_target_pairs={{0,2},{1,3},{2,0},{3,1},{4,6},{5,7},{6,4},{7,5},{8,10},{9,11},{10,... | collective-permute-start | bytes 786440 | tf_op jit(solution)/shard_map/ppermute | solution.py:30
  7.7 14.5 %collective-permute-start = (bf16[512,256]{1,0:T(8,128)(2,1)S(1)}, bf16[512,256]{1,0:T(8,128)(2,1)S(1)}, u32[]{:S(2)}, u32[]{:S(2)}) collective-permute-start(bf16[512,256]{1,0:T(8,128)(2,1)S(1)} %get-tuple-element.40), channel_id=1, source_target_pairs={{0,4},{1,5},{2,6},{3,7},{4,0},{5,1},{6,2},{7,3},{8,12},{9,13},{10,... | collective-permute-start | bytes 786440 | tf_op jit(solution)/shard_map/ppermute | solution.py:30
  8.9 14.0 %collective-permute-start.1 = (bf16[512,256]{1,0:T(8,128)(2,1)S(1)}, bf16[512,256]{1,0:T(8,128)(2,1)S(1)}, u32[]{:S(2)}, u32[]{:S(2)}) collective-permute-start(bf16[512,256]{1,0:T(8,128)(2,1)S(1)} %get-tuple-element.40), channel_id=1, source_target_pairs={{0,12},{1,13},{2,14},{3,15},{4,8},{5,9},{6,10},{7,11},{8,4},{9,5},... | collective-permute-start | bytes 786440 | tf_op jit(solution)/shard_map/ppermute | solution.py:30
  11.5 12.1 %collective-permute-start.2 = (bf16[512,256]{1,0:T(8,128)(2,1)S(1)}, bf16[512,256]{1,0:T(8,128)(2,1)S(1)}, u32[]{:S(2)}, u32[]{:S(2)}) collective-permute-start(bf16[512,256]{1,0:T(8,128)(2,1)S(1)} %get-tuple-element.40), channel_id=1, source_target_pairs={{0,8},{1,9},{2,10},{3,11},{4,12},{5,13},{6,14},{7,15},{8,0},{9,1},... | collective-permute-start | bytes 786440 | tf_op jit(solution)/shard_map/ppermute | solution.py:30
  19.1 13.1 %collective-permute-start.8 = (bf16[4,256,256]{2,1,0:T(8,128)(2,1)S(1)}, bf16[4,256,256]{2,1,0:T(8,128)(2,1)S(1)}, u32[]{:S(2)}, u32[]{:S(2)}) collective-permute-start(bf16[4,256,256]{2,1,0:T(8,128)(2,1)S(1)} %pad_maximum_fusion.3.refs_2_), channel_id=1, source_target_pairs={{0,4},{1,5},{2,6},{3,7},{4,0},{5,1},{6,2},{7,3},{8,12},{9,13},{10,... | collective-permute-start | bytes 1572872 | tf_op jit(solution)/shard_map/ppermute | solution.py:30
  20.4 13.2 %collective-permute-start.9 = (bf16[4,256,256]{2,1,0:T(8,128)(2,1)S(1)}, bf16[4,256,256]{2,1,0:T(8,128)(2,1)S(1)}, u32[]{:S(2)}, u32[]{:S(2)}) collective-permute-start(bf16[4,256,256]{2,1,0:T(8,128)(2,1)S(1)} %pad_maximum_fusion.3.refs_2_), channel_id=1, source_target_pairs={{0,12},{1,13},{2,14},{3,15},{4,8},{5,9},{6,10},{7,11},{8,4},{9,5},... | collective-permute-start | bytes 1572872 | tf_op jit(solution)/shard_map/ppermute | solution.py:30
  24.4 11.4 %collective-permute-start.3 = (bf16[4,256,256]{2,1,0:T(8,128)(2,1)S(1)}, bf16[4,256,256]{2,1,0:T(8,128)(2,1)S(1)}, u32[]{:S(2)}, u32[]{:S(2)}) collective-permute-start(bf16[4,256,256]{2,1,0:T(8,128)(2,1)S(1)} %pad_maximum_fusion.2.refs_0_), channel_id=1, source_target_pairs={{0,1},{1,0},{2,3},{3,2},{4,5},{5,4},{6,7},{7,6},{8,9},{9,8},{10,11... | collective-permute-start | bytes 1572872 | tf_op jit(solution)/shard_map/ppermute | solution.py:30
  24.5 12.6 %collective-permute-start.4 = (bf16[4,256,256]{2,1,0:T(8,128)(2,1)S(1)}, bf16[4,256,256]{2,1,0:T(8,128)(2,1)S(1)}, u32[]{:S(2)}, u32[]{:S(2)}) collective-permute-start(bf16[4,256,256]{2,1,0:T(8,128)(2,1)S(1)} %pad_maximum_fusion.2.refs_0_), channel_id=1, source_target_pairs={{0,3},{1,2},{2,1},{3,0},{4,7},{5,6},{6,5},{7,4},{8,11},{9,10},{10,... | collective-permute-start | bytes 1572872 | tf_op jit(solution)/shard_map/ppermute | solution.py:30
  32.3 9.7 %collective-permute-start.17 = (bf16[2,256,256]{2,1,0:T(8,128)(2,1)S(1)}, bf16[2,256,256]{2,1,0:T(8,128)(2,1)S(1)}, u32[]{:S(2)}, u32[]{:S(2)}) collective-permute-start(bf16[2,256,256]{2,1,0:T(8,128)(2,1)S(1)} %slice.97), channel_id=1, source_target_pairs={{0,12},{1,13},{2,14},{3,15},{4,8},{5,9},{6,10},{7,11},{8,4},{9,5},... | collective-permute-start | bytes 786440 | tf_op jit(solution)/shard_map/ppermute | solution.py:30
  33.7 9.6 %collective-permute-start.16 = (bf16[2,256,256]{2,1,0:T(8,128)(2,1)S(1)}, bf16[2,256,256]{2,1,0:T(8,128)(2,1)S(1)}, u32[]{:S(2)}, u32[]{:S(2)}) collective-permute-start(bf16[2,256,256]{2,1,0:T(8,128)(2,1)S(1)} %slice.96), channel_id=1, source_target_pairs={{0,4},{1,5},{2,6},{3,7},{4,0},{5,1},{6,2},{7,3},{8,12},{9,13},{10,... | collective-permute-start | bytes 786440 | tf_op jit(solution)/shard_map/ppermute | solution.py:30
  41.6 10.5 %collective-permute-start.12 = (bf16[4,256,256]{2,1,0:T(8,128)(2,1)S(1)}, bf16[4,256,256]{2,1,0:T(8,128)(2,1)S(1)}, u32[]{:S(2)}, u32[]{:S(2)}) collective-permute-start(bf16[4,256,256]{2,1,0:T(8,128)(2,1)S(1)} %pad_maximum_fusion.4.refs_3_), channel_id=1, source_target_pairs={{0,4},{1,5},{2,6},{3,7},{4,0},{5,1},{6,2},{7,3},{8,12},{9,13},{10,... | collective-permute-start | bytes 1572872 | tf_op jit(solution)/shard_map/ppermute | solution.py:30
  42.0 12.3 %collective-permute-start.13 = (bf16[4,256,256]{2,1,0:T(8,128)(2,1)S(1)}, bf16[4,256,256]{2,1,0:T(8,128)(2,1)S(1)}, u32[]{:S(2)}, u32[]{:S(2)}) collective-permute-start(bf16[4,256,256]{2,1,0:T(8,128)(2,1)S(1)} %pad_maximum_fusion.4.refs_3_), channel_id=1, source_target_pairs={{0,12},{1,13},{2,14},{3,15},{4,8},{5,9},{6,10},{7,11},{8,4},{9,5},... | collective-permute-start | bytes 1572872 | tf_op jit(solution)/shard_map/ppermute | solution.py:30
  43.3 11.1 %collective-permute-start.10 = (bf16[4,256,256]{2,1,0:T(8,128)(2,1)S(1)}, bf16[4,256,256]{2,1,0:T(8,128)(2,1)S(1)}, u32[]{:S(2)}, u32[]{:S(2)}) collective-permute-start(bf16[4,256,256]{2,1,0:T(8,128)(2,1)S(1)} %pad_maximum_fusion.1.refs_1_), channel_id=1, source_target_pairs={{0,1},{1,0},{2,3},{3,2},{4,5},{5,4},{6,7},{7,6},{8,9},{9,8},{10,11... | collective-permute-start | bytes 1572872 | tf_op jit(solution)/shard_map/ppermute | solution.py:30
  44.7 11.0 %collective-permute-start.11 = (bf16[4,256,256]{2,1,0:T(8,128)(2,1)S(1)}, bf16[4,256,256]{2,1,0:T(8,128)(2,1)S(1)}, u32[]{:S(2)}, u32[]{:S(2)}) collective-permute-start(bf16[4,256,256]{2,1,0:T(8,128)(2,1)S(1)} %pad_maximum_fusion.1.refs_1_), channel_id=1, source_target_pairs={{0,3},{1,2},{2,1},{3,0},{4,7},{5,6},{6,5},{7,4},{8,11},{9,10},{10,... | collective-permute-start | bytes 1572872 | tf_op jit(solution)/shard_map/ppermute | solution.py:30
  49.0 27.7 %collective-permute-start.25 = (f16[272,1024]{1,0:T(8,128)(2,1)S(1)}, f16[272,1024]{1,0:T(8,128)(2,1)S(1)}, u32[]{:S(2)}, u32[]{:S(2)}) collective-permute-start(f16[272,1024]{1,0:T(8,128)(2,1)S(1)} %convert_element_type.39), channel_id=1, source_target_pairs={{0,64},{16,80},{32,96},{48,112},{64,0},{80,16},{96,32},{112,48},{1... | collective-permute-start | bytes 1671176 | tf_op jit(solution)/shard_map/ppermute | solution.py:30
  60.4 16.6 %collective-permute-start.27 = (f16[136,1024]{1,0:T(8,128)(2,1)S(1)}, f16[136,1024]{1,0:T(8,128)(2,1)S(1)}, u32[]{:S(2)}, u32[]{:S(2)}) collective-permute-start(f16[136,1024]{1,0:T(8,128)(2,1)S(1)} %convert_element_type.41), channel_id=1, source_target_pairs={{0,96},{16,112},{32,64},{48,80},{64,32},{80,48},{96,0},{112,16},{1... | collective-permute-start | bytes 835592 | tf_op jit(solution)/shard_map/ppermute | solution.py:30
  63.0 14.3 %collective-permute-start.23 = (f16[136,1024]{1,0:T(8,128)(2,1)S(1)}, f16[136,1024]{1,0:T(8,128)(2,1)S(1)}, u32[]{:S(2)}, u32[]{:S(2)}) collective-permute-start(f16[136,1024]{1,0:T(8,128)(2,1)S(1)} %convert_element_type.40), channel_id=1, source_target_pairs={{0,32},{16,48},{32,0},{48,16},{64,96},{80,112},{96,64},{112,80},{1... | collective-permute-start | bytes 835592 | tf_op jit(solution)/shard_map/ppermute | solution.py:30
  66.6 10.9 %collective-permute-start.22 = (f16[136,1024]{1,0:T(8,128)(2,1)S(1)}, f16[136,1024]{1,0:T(8,128)(2,1)S(1)}, u32[]{:S(2)}, u32[]{:S(2)}) collective-permute-start(f16[136,1024]{1,0:T(8,128)(2,1)S(1)} %convert_element_type.42), channel_id=1, source_target_pairs={{0,16},{16,0},{32,48},{48,32},{64,80},{80,64},{96,112},{112,96},{1... | collective-permute-start | bytes 835592 | tf_op jit(solution)/shard_map/ppermute | solution.py:30
  76.7 9.9 %collective-permute-start.28 = (f16[136,1024]{1,0:T(8,128)(2,1)S(1)}, f16[136,1024]{1,0:T(8,128)(2,1)S(1)}, u32[]{:S(2)}, u32[]{:S(2)}) collective-permute-start(f16[136,1024]{1,0:T(8,128)(2,1)S(1)} %convert_element_type.48), channel_id=1, source_target_pairs={{0,112},{16,96},{32,80},{48,64},{64,48},{80,32},{96,16},{112,0},{1... | collective-permute-start | bytes 835592 | tf_op jit(solution)/shard_map/ppermute | solution.py:30
  77.1 9.6 %collective-permute-start.26 = (f16[136,1024]{1,0:T(8,128)(2,1)S(1)}, f16[136,1024]{1,0:T(8,128)(2,1)S(1)}, u32[]{:S(2)}, u32[]{:S(2)}) collective-permute-start(f16[136,1024]{1,0:T(8,128)(2,1)S(1)} %get-tuple-element.66), channel_id=1, source_target_pairs={{0,16},{16,0},{32,48},{48,32},{64,80},{80,64},{96,112},{112,96},{1... | collective-permute-start | bytes 835592 | tf_op jit(solution)/shard_map/ppermute | solution.py:30
  109.2 11.3 %collective-permute-start.40 = (bf16[128,1024]{1,0:T(8,128)(2,1)S(1)}, bf16[128,1024]{1,0:T(8,128)(2,1)S(1)}, u32[]{:S(2)}, u32[]{:S(2)}) collective-permute-start(bf16[128,1024]{1,0:T(8,128)(2,1)S(1)} %get-tuple-element.73.refs_0_), channel_id=1, source_target_pairs={{0,64},{16,80},{32,96},{48,112},{64,0},{80,16},{96,32},{112,48},{1... | collective-permute-start | bytes 786440 | tf_op jit(solution)/shard_map/ppermute | solution.py:30
  110.0 10.6 %collective-permute-start.41 = (bf16[128,1024]{1,0:T(8,128)(2,1)S(1)}, bf16[128,1024]{1,0:T(8,128)(2,1)S(1)}, u32[]{:S(2)}, u32[]{:S(2)}) collective-permute-start(bf16[128,1024]{1,0:T(8,128)(2,1)S(1)} %get-tuple-element.73.refs_0_), channel_id=1, source_target_pairs={{0,32},{16,48},{32,0},{48,16},{64,96},{80,112},{96,64},{112,80},{1... | collective-permute-start | bytes 786440 | tf_op jit(solution)/shard_map/ppermute | solution.py:30
  (24 other events, 183.3 us)

commit v5 on v4

--- a/solution.py
+++ b/solution.py
@@ -414,8 +414,8 @@
         a_near, a_far = swap(a_own, "tp", 1), swap(a_own, "tp", 3)
         b_near, b_far = swap(b_own, "tp", 4), swap(b_own, "tp", 12)
         if chunk:
-            a_opposite = forward(after(a_near, *sent), after(a_far, *sent), 1)
-            b_opposite = forward(after(b_near, *sent), after(b_far, *sent), 4)
+            a_opposite = forward(after(a_near, sent[0]), after(a_far, sent[0]), 1)
+            b_opposite = forward(b_near, b_far, 4)
         else:
             a_opposite = forward(after(a_near, *own), after(a_far, *own), 1)
             b_opposite = forward(after(b_near, *own), after(b_far, *own), 4)

time: 129 us -> 129 us (level)
  starting transfers between devices: 67.8 us -> 64.1 us
  waiting for transfers between devices: 26.4 us -> 29.6 us
    ppermute x44, starting transfers between devices: 67.8 us -> 64.1 us  [swap(): lax.ppermute(value, axis, [(i, i ^ distance) for i in range(lax.axis_size...]
    ppermute x44, waiting for transfers between devices: 26.4 us -> 29.6 us  [swap(): lax.ppermute(value, axis, [(i, i ^ distance) for i in range(lax.axis_size...]
  transfers between devices with their start and end apart: 44 -> 44, of which waited for: 14 -> 15; matrix products, arithmetic and copies ran while one was open for 5% -> 5% of each run, Pallas kernels for 17% -> 17%
where the time goes in v5:
time: 129 us; the launch traced here: 128 us
  starting transfers between devices  64.1 us (50%)
  waiting for transfers between devices  29.6 us (23%)
  Pallas kernels  26.6 us (21%)
  local copies, waits for them, and re-layouts  4 us (3%)
  other arithmetic  2.9 us (2%)
    ppermute x44, starting transfers between devices, swap(): lax.ppermute(value, axis, [(i, i ^ distance) for i in range(lax.axis_size...  64.1 us
    ppermute x44, waiting for transfers between devices, swap(): lax.ppermute(value, axis, [(i, i ^ distance) for i in range(lax.axis_size...  29.6 us
    pallas_call x3, Pallas kernels, early_product(): pl.pallas_call(kernel, out_shape=[jax.ShapeDtypeStruct((rows, columns), j...  12.9 us
    pallas_call x2, Pallas kernels, late_product(): pl.pallas_call(functools.partial(late_kernel, owners, len(a_pieces) == 1,...  6.78 us
    pallas_call x2, Pallas kernels, adam(): pl.pallas_call(functools.partial(adam_kernel, first), out_shape=outs, in_...  3.74 us
    another operation x7, local copies, waits for them, and re-layouts, per_device(): jnp.stack([piece[c * 2 * BLOCK:(c + 1) * 2 * BLOCK] for piece in line])  2.81 us
  transfers between devices with their start and end apart: 44, of which 15 were waited for; matrix products, arithmetic and copies ran while one was open for 5% of the time, Pallas kernels for 17%

profile of v5, /device:TPU:1, one launch (start us, length us, event | category | flops | bytes accessed | tf_op | source)
XLA Modules:
  0.0 128.4 jit_solution(5093039110527911868)
XLA Ops:
  1.9 2.5 %collective-permute-start.5 = (bf16[512,256]{1,0:T(8,128)(2,1)S(1)}, bf16[512,256]{1,0:T(8,128)(2,1)S(1)}, u32[]{:S(2)}, u32[]{:S(2)}) collective-permute-start(bf16[512,256]{1,0:T(8,128)(2,1)S(1)} %get-tuple-element.39), channel_id=1, source_target_pairs={{0,1},{1,0},{2,3},{3,2},{4,5},{5,4},{6,7},{7,6},{8,9},{9,8},{10,11... | collective-permute-start | bytes 786440 | tf_op jit(solution)/shard_map/ppermute | solution.py:30
  4.4 2.2 %collective-permute-start.6 = (bf16[512,256]{1,0:T(8,128)(2,1)S(1)}, bf16[512,256]{1,0:T(8,128)(2,1)S(1)}, u32[]{:S(2)}, u32[]{:S(2)}) collective-permute-start(bf16[512,256]{1,0:T(8,128)(2,1)S(1)} %get-tuple-element.39), channel_id=1, source_target_pairs={{0,3},{1,2},{2,1},{3,0},{4,7},{5,6},{6,5},{7,4},{8,11},{9,10},{10,... | collective-permute-start | bytes 786440 | tf_op jit(solution)/shard_map/ppermute | solution.py:30
  8.9 1.8 %collective-permute-start.1 = (bf16[512,256]{1,0:T(8,128)(2,1)S(1)}, bf16[512,256]{1,0:T(8,128)(2,1)S(1)}, u32[]{:S(2)}, u32[]{:S(2)}) collective-permute-start(bf16[512,256]{1,0:T(8,128)(2,1)S(1)} %get-tuple-element.38), channel_id=1, source_target_pairs={{0,12},{1,13},{2,14},{3,15},{4,8},{5,9},{6,10},{7,11},{8,4},{9,5},... | collective-permute-start | bytes 786440 | tf_op jit(solution)/shard_map/ppermute | solution.py:30
  13.1 3.7 %collective-permute-done.6 = bf16[512,256]{1,0:T(8,128)(2,1)S(1)} collective-permute-done((bf16[512,256]{1,0:T(8,128)(2,1)S(1)}, bf16[512,256]{1,0:T(8,128)(2,1)S(1)}, u32[]{:S(2)}, u32[]{:S(2)}) %collective-permute-start.6) | collective-permute-done | bytes 262176 | tf_op jit(solution)/shard_map/ppermute | solution.py:30
  16.8 2.2 %collective-permute-done.7 = bf16[512,256]{1,0:T(8,128)(2,1)S(1)} collective-permute-done((bf16[512,256]{1,0:T(8,128)(2,1)S(1)}, bf16[512,256]{1,0:T(8,128)(2,1)S(1)}, u32[]{:S(2)}, u32[]{:S(2)}) %collective-permute-start.7) | collective-permute-done | bytes 262176 | tf_op jit(solution)/shard_map/ppermute | solution.py:30
  20.4 1.8 %collective-permute-start.9 = (bf16[4,256,256]{2,1,0:T(8,128)(2,1)S(1)}, bf16[4,256,256]{2,1,0:T(8,128)(2,1)S(1)}, u32[]{:S(2)}, u32[]{:S(2)}) collective-permute-start(bf16[4,256,256]{2,1,0:T(8,128)(2,1)S(1)} %pad_maximum_fusion.3.refs_2_), channel_id=1, source_target_pairs={{0,12},{1,13},{2,14},{3,15},{4,8},{5,9},{6,10},{7,11},{8,4},{9,5},... | collective-permute-start | bytes 1572872 | tf_op jit(solution)/shard_map/ppermute | solution.py:30
  28.0 4.2 %shard_map.93 = (f32[512,1024]{1,0:T(8,128)S(1)}, f32[512,1024]{1,0:T(8,128)S(1)}) custom-call(s32[1]{0:T(128)} %bitcast.place_ref, bf16[4,256,256]{2,1,0:T(8,128)(2,1)S(1)} %pad_maximum_fusion.2.refs_0_, bf16[4,256,256]{2,1,0:T(8,128)(2,1)S(1)} %pad_maximum_fusion.1.refs_1_, bf16[4,256,256]{2,1,0:T(8,128)(2,1)S(1)} %pad_maximum_fusion.3.refs_2_, ...), custom_call_target="tpu_custom_call" | custom-call | flops 2147483648 | bytes 8388608 | tf_op jit(solution)/shard_map/pallas_call | solution.py:179
  33.8 2.0 %collective-permute-done.3.refs_0_ = bf16[4,256,256]{2,1,0:T(8,128)(2,1)S(1)} collective-permute-done((bf16[4,256,256]{2,1,0:T(8,128)(2,1)S(1)}, bf16[4,256,256]{2,1,0:T(8,128)(2,1)S(1)}, u32[]{:S(2)}, u32[]{:S(2)}) %collective-permute-start.3) | collective-permute-done | bytes 524320 | tf_op jit(solution)/shard_map/ppermute | solution.py:30
  37.2 4.4 %shard_map.94 = (f32[256,1024]{1,0:T(8,128)S(1)}, f32[256,1024]{1,0:T(8,128)S(1)}) custom-call(s32[1]{0:T(128)} %bitcast.place_ref, bf16[4,256,256]{2,1,0:T(8,128)(2,1)S(1)} %collective-permute-done.3.refs_0_, bf16[4,256,256]{2,1,0:T(8,128)(2,1)S(1)} %collective-permute-done.4.refs_1_, bf16[4,256,256]{2,1,0:T(8,128)(2,1)S(1)} %collective-permute-done.8.refs_2_, ...), custom_call_target="tpu_custom_call" | custom-call | flops 2147483648 | bytes 8388608 | tf_op jit(solution)/shard_map/pallas_call | solution.py:179
  45.0 3.4 %shard_map.96 = (f32[272,1024]{1,0:T(8,128)S(1)}, f32[136,1024]{1,0:T(8,128)S(1)}, f32[136,1024]{1,0:T(8,128)S(1)}) custom-call(s32[1]{0:T(128)} %bitcast.place_ref, f32[256,1024]{1,0:T(8,128)S(1)} %get-tuple-element.42.refs_0_, f32[256,1024]{1,0:T(8,128)S(1)} %get-tuple-element.43.refs_1_, bf16[2,256,256]{2,1,0:T(8,128)(2,1)S(1)} %collective-permute-done.14.refs_2_, ...), custom_call_target="tpu_custom_call" | custom-call | flops 1073741824 | bytes 4194304 | tf_op jit(solution)/shard_map/pallas_call | solution.py:199
  48.6 3.0 %collective-permute-start.25 = (f16[272,1024]{1,0:T(8,128)(2,1)S(1)}, f16[272,1024]{1,0:T(8,128)(2,1)S(1)}, u32[]{:S(2)}, u32[]{:S(2)}) collective-permute-start(f16[272,1024]{1,0:T(8,128)(2,1)S(1)} %convert_element_type.39), channel_id=1, source_target_pairs={{0,64},{16,80},{32,96},{48,112},{64,0},{80,16},{96,32},{112,48},{1... | collective-permute-start | bytes 1671176 | tf_op jit(solution)/shard_map/ppermute | solution.py:30
  51.6 3.6 %collective-permute-done.10.refs_0_ = bf16[4,256,256]{2,1,0:T(8,128)(2,1)S(1)} collective-permute-done((bf16[4,256,256]{2,1,0:T(8,128)(2,1)S(1)}, bf16[4,256,256]{2,1,0:T(8,128)(2,1)S(1)}, u32[]{:S(2)}, u32[]{:S(2)}) %collective-permute-start.10) | collective-permute-done | bytes 524320 | tf_op jit(solution)/shard_map/ppermute | solution.py:30
  59.1 4.4 %shard_map.95 = (f32[256,1024]{1,0:T(8,128)S(1)}, f32[256,1024]{1,0:T(8,128)S(1)}) custom-call(s32[1]{0:T(128)} %bitcast.place_ref, bf16[4,256,256]{2,1,0:T(8,128)(2,1)S(1)} %collective-permute-done.10.refs_0_, bf16[4,256,256]{2,1,0:T(8,128)(2,1)S(1)} %collective-permute-done.11.refs_1_, bf16[4,256,256]{2,1,0:T(8,128)(2,1)S(1)} %collective-permute-done.12.refs_2_, ...), custom_call_target="tpu_custom_call" | custom-call | flops 2147483648 | bytes 8388608 | tf_op jit(solution)/shard_map/pallas_call | solution.py:179
  63.5 2.8 %collective-permute-start.27 = (f16[136,1024]{1,0:T(8,128)(2,1)S(1)}, f16[136,1024]{1,0:T(8,128)(2,1)S(1)}, u32[]{:S(2)}, u32[]{:S(2)}) collective-permute-start(f16[136,1024]{1,0:T(8,128)(2,1)S(1)} %convert_element_type.49), channel_id=1, source_target_pairs={{0,96},{16,112},{32,64},{48,80},{64,32},{80,48},{96,0},{112,16},{1... | collective-permute-start | bytes 835592 | tf_op jit(solution)/shard_map/ppermute | solution.py:30
  66.3 3.4 %shard_map.97 = (f32[136,1024]{1,0:T(8,128)S(1)}, f32[136,1024]{1,0:T(8,128)S(1)}, f32[136,1024]{1,0:T(8,128)S(1)}, f32[136,1024]{1,0:T(8,128)S(1)}) custom-call(s32[1]{0:T(128)} %bitcast.place_ref, f32[256,1024]{1,0:T(8,128)S(1)} %get-tuple-element.46.refs_0_, f32[256,1024]{1,0:T(8,128)S(1)} %get-tuple-element.47.refs_1_, ...), custom_call_target="tpu_custom_call" | custom-call | flops 1073741824 | bytes 4194304 | tf_op jit(solution)/shard_map/pallas_call | solution.py:199
  69.8 4.4 %collective-permute-start.22 = (f16[136,1024]{1,0:T(8,128)(2,1)S(1)}, f16[136,1024]{1,0:T(8,128)(2,1)S(1)}, u32[]{:S(2)}, u32[]{:S(2)}) collective-permute-start(f16[136,1024]{1,0:T(8,128)(2,1)S(1)} %convert_element_type.40), channel_id=1, source_target_pairs={{0,16},{16,0},{32,48},{48,32},{64,80},{80,64},{96,112},{112,96},{1... | collective-permute-start | bytes 835592 | tf_op jit(solution)/shard_map/ppermute | solution.py:30
  76.7 6.3 %collective-permute-done.24 = f16[136,1024]{1,0:T(8,128)(2,1)S(1)} collective-permute-done((f16[136,1024]{1,0:T(8,128)(2,1)S(1)}, f16[136,1024]{1,0:T(8,128)(2,1)S(1)}, u32[]{:S(2)}, u32[]{:S(2)}) %collective-permute-start.24) | collective-permute-done | bytes 278560 | tf_op jit(solution)/shard_map/ppermute | solution.py:30
  83.1 2.7 %collective-permute-done.28 = f16[136,1024]{1,0:T(8,128)(2,1)S(1)} collective-permute-done((f16[136,1024]{1,0:T(8,128)(2,1)S(1)}, f16[136,1024]{1,0:T(8,128)(2,1)S(1)}, u32[]{:S(2)}, u32[]{:S(2)}) %collective-permute-start.28) | collective-permute-done | bytes 278560 | tf_op jit(solution)/shard_map/ppermute | solution.py:30
  90.1 2.5 %collective-permute-start.32 = (f32[40,128]{1,0:T(8,128)S(1)}, f32[40,128]{1,0:T(8,128)S(1)}, u32[]{:S(2)}, u32[]{:S(2)}) collective-permute-start(f32[40,128]{1,0:T(8,128)S(1)} %shard_map.99.own), channel_id=1, source_target_pairs={{0,96},{16,112},{32,64},{48,80},{64,32},{80,48},{96,0},{112,16},{1... | collective-permute-start | bytes 61448 | tf_op jit(solution)/shard_map/ppermute | solution.py:30
  108.6 2.6 %collective-permute-start.41 = (bf16[128,1024]{1,0:T(8,128)(2,1)S(1)}, bf16[128,1024]{1,0:T(8,128)(2,1)S(1)}, u32[]{:S(2)}, u32[]{:S(2)}) collective-permute-start(bf16[128,1024]{1,0:T(8,128)(2,1)S(1)} %get-tuple-element.69.refs_0_), channel_id=1, source_target_pairs={{0,32},{16,48},{32,0},{48,16},{64,96},{80,112},{96,64},{112,80},{1... | collective-permute-start | bytes 786440 | tf_op jit(solution)/shard_map/ppermute | solution.py:30
  111.5 6.2 %collective-permute-start.39 = (bf16[128,1024]{1,0:T(8,128)(2,1)S(1)}, bf16[128,1024]{1,0:T(8,128)(2,1)S(1)}, u32[]{:S(2)}, u32[]{:S(2)}) collective-permute-start(bf16[128,1024]{1,0:T(8,128)(2,1)S(1)} %get-tuple-element.69.refs_0_), channel_id=1, source_target_pairs={{0,16},{16,0},{32,48},{48,32},{64,80},{80,64},{96,112},{112,96},{1... | collective-permute-start | bytes 786440 | tf_op jit(solution)/shard_map/ppermute | solution.py:30
  117.7 2.3 %shard_map.102 = (f32[128,1024]{1,0:T(8,128)}, f32[128,1024]{1,0:T(8,128)}, f32[128,1024]{1,0:T(8,128)}, f32[128,1024]{1,0:T(8,128)}) custom-call(f32[8,128]{1,0:T(8,128)S(1)} %get-tuple-element.64.refs_0_, f32[136,1024]{1,0:T(8,128)S(1)} %get-tuple-element.55.refs_0_.refs_4_.refs_1_, f32[136,1024]{1,0:T(8,128)S(1)} %convert_element_type.41.refs_1_.refs_5_.refs_2_, ...), custom_call_target="tpu_custom_call" | custom-call | tf_op jit(solution)/shard_map/pallas_call | solution.py:354
  120.0 4.9 %collective-permute-start.43 = (bf16[384,1024]{1,0:T(8,128)(2,1)S(1)}, bf16[384,1024]{1,0:T(8,128)(2,1)S(1)}, u32[]{:S(2)}, u32[]{:S(2)}) collective-permute-start(bf16[384,1024]{1,0:T(8,128)(2,1)S(1)} %pad_maximum_fusion), channel_id=1, source_target_pairs={{0,16},{16,0},{32,48},{48,32},{64,80},{80,64},{96,112},{112,96},{1... | collective-permute-start | bytes 2359304 | tf_op jit(solution)/shard_map/ppermute | solution.py:30
  124.9 1.9 %collective-permute-done.43.refs_5_ = bf16[384,1024]{1,0:T(8,128)(2,1)S(1)} collective-permute-done((bf16[384,1024]{1,0:T(8,128)(2,1)S(1)}, bf16[384,1024]{1,0:T(8,128)(2,1)S(1)}, u32[]{:S(2)}, u32[]{:S(2)}) %collective-permute-start.43) | collective-permute-done | bytes 786464 | tf_op jit(solution)/shard_map/ppermute | solution.py:30
  (118 shorter events, 48.0 us)
Async XLA Ops:
  1.9 9.6 %collective-permute-start.5 = (bf16[512,256]{1,0:T(8,128)(2,1)S(1)}, bf16[512,256]{1,0:T(8,128)(2,1)S(1)}, u32[]{:S(2)}, u32[]{:S(2)}) collective-permute-start(bf16[512,256]{1,0:T(8,128)(2,1)S(1)} %get-tuple-element.39), channel_id=1, source_target_pairs={{0,1},{1,0},{2,3},{3,2},{4,5},{5,4},{6,7},{7,6},{8,9},{9,8},{10,11... | collective-permute-start | bytes 786440 | tf_op jit(solution)/shard_map/ppermute | solution.py:30
  4.4 12.4 %collective-permute-start.6 = (bf16[512,256]{1,0:T(8,128)(2,1)S(1)}, bf16[512,256]{1,0:T(8,128)(2,1)S(1)}, u32[]{:S(2)}, u32[]{:S(2)}) collective-permute-start(bf16[512,256]{1,0:T(8,128)(2,1)S(1)} %get-tuple-element.39), channel_id=1, source_target_pairs={{0,3},{1,2},{2,1},{3,0},{4,7},{5,6},{6,5},{7,4},{8,11},{9,10},{10,... | collective-permute-start | bytes 786440 | tf_op jit(solution)/shard_map/ppermute | solution.py:30
  6.7 12.4 %collective-permute-start.7 = (bf16[512,256]{1,0:T(8,128)(2,1)S(1)}, bf16[512,256]{1,0:T(8,128)(2,1)S(1)}, u32[]{:S(2)}, u32[]{:S(2)}) collective-permute-start(bf16[512,256]{1,0:T(8,128)(2,1)S(1)} %get-tuple-element.39), channel_id=1, source_target_pairs={{0,2},{1,3},{2,0},{3,1},{4,6},{5,7},{6,4},{7,5},{8,10},{9,11},{10,... | collective-permute-start | bytes 786440 | tf_op jit(solution)/shard_map/ppermute | solution.py:30
  7.7 14.5 %collective-permute-start = (bf16[512,256]{1,0:T(8,128)(2,1)S(1)}, bf16[512,256]{1,0:T(8,128)(2,1)S(1)}, u32[]{:S(2)}, u32[]{:S(2)}) collective-permute-start(bf16[512,256]{1,0:T(8,128)(2,1)S(1)} %get-tuple-element.38), channel_id=1, source_target_pairs={{0,4},{1,5},{2,6},{3,7},{4,0},{5,1},{6,2},{7,3},{8,12},{9,13},{10,... | collective-permute-start | bytes 786440 | tf_op jit(solution)/shard_map/ppermute | solution.py:30
  8.9 14.0 %collective-permute-start.1 = (bf16[512,256]{1,0:T(8,128)(2,1)S(1)}, bf16[512,256]{1,0:T(8,128)(2,1)S(1)}, u32[]{:S(2)}, u32[]{:S(2)}) collective-permute-start(bf16[512,256]{1,0:T(8,128)(2,1)S(1)} %get-tuple-element.38), channel_id=1, source_target_pairs={{0,12},{1,13},{2,14},{3,15},{4,8},{5,9},{6,10},{7,11},{8,4},{9,5},... | collective-permute-start | bytes 786440 | tf_op jit(solution)/shard_map/ppermute | solution.py:30
  11.5 12.1 %collective-permute-start.2 = (bf16[512,256]{1,0:T(8,128)(2,1)S(1)}, bf16[512,256]{1,0:T(8,128)(2,1)S(1)}, u32[]{:S(2)}, u32[]{:S(2)}) collective-permute-start(bf16[512,256]{1,0:T(8,128)(2,1)S(1)} %get-tuple-element.38), channel_id=1, source_target_pairs={{0,8},{1,9},{2,10},{3,11},{4,12},{5,13},{6,14},{7,15},{8,0},{9,1},... | collective-permute-start | bytes 786440 | tf_op jit(solution)/shard_map/ppermute | solution.py:30
  19.1 13.1 %collective-permute-start.8 = (bf16[4,256,256]{2,1,0:T(8,128)(2,1)S(1)}, bf16[4,256,256]{2,1,0:T(8,128)(2,1)S(1)}, u32[]{:S(2)}, u32[]{:S(2)}) collective-permute-start(bf16[4,256,256]{2,1,0:T(8,128)(2,1)S(1)} %pad_maximum_fusion.3.refs_2_), channel_id=1, source_target_pairs={{0,4},{1,5},{2,6},{3,7},{4,0},{5,1},{6,2},{7,3},{8,12},{9,13},{10,... | collective-permute-start | bytes 1572872 | tf_op jit(solution)/shard_map/ppermute | solution.py:30
  20.4 13.2 %collective-permute-start.9 = (bf16[4,256,256]{2,1,0:T(8,128)(2,1)S(1)}, bf16[4,256,256]{2,1,0:T(8,128)(2,1)S(1)}, u32[]{:S(2)}, u32[]{:S(2)}) collective-permute-start(bf16[4,256,256]{2,1,0:T(8,128)(2,1)S(1)} %pad_maximum_fusion.3.refs_2_), channel_id=1, source_target_pairs={{0,12},{1,13},{2,14},{3,15},{4,8},{5,9},{6,10},{7,11},{8,4},{9,5},... | collective-permute-start | bytes 1572872 | tf_op jit(solution)/shard_map/ppermute | solution.py:30
  24.4 11.4 %collective-permute-start.3 = (bf16[4,256,256]{2,1,0:T(8,128)(2,1)S(1)}, bf16[4,256,256]{2,1,0:T(8,128)(2,1)S(1)}, u32[]{:S(2)}, u32[]{:S(2)}) collective-permute-start(bf16[4,256,256]{2,1,0:T(8,128)(2,1)S(1)} %pad_maximum_fusion.2.refs_0_), channel_id=1, source_target_pairs={{0,1},{1,0},{2,3},{3,2},{4,5},{5,4},{6,7},{7,6},{8,9},{9,8},{10,11... | collective-permute-start | bytes 1572872 | tf_op jit(solution)/shard_map/ppermute | solution.py:30
  24.5 12.6 %collective-permute-start.4 = (bf16[4,256,256]{2,1,0:T(8,128)(2,1)S(1)}, bf16[4,256,256]{2,1,0:T(8,128)(2,1)S(1)}, u32[]{:S(2)}, u32[]{:S(2)}) collective-permute-start(bf16[4,256,256]{2,1,0:T(8,128)(2,1)S(1)} %pad_maximum_fusion.2.refs_0_), channel_id=1, source_target_pairs={{0,3},{1,2},{2,1},{3,0},{4,7},{5,6},{6,5},{7,4},{8,11},{9,10},{10,... | collective-permute-start | bytes 1572872 | tf_op jit(solution)/shard_map/ppermute | solution.py:30
  32.3 10.8 %collective-permute-start.17 = (bf16[2,256,256]{2,1,0:T(8,128)(2,1)S(1)}, bf16[2,256,256]{2,1,0:T(8,128)(2,1)S(1)}, u32[]{:S(2)}, u32[]{:S(2)}) collective-permute-start(bf16[2,256,256]{2,1,0:T(8,128)(2,1)S(1)} %slice.97), channel_id=1, source_target_pairs={{0,12},{1,13},{2,14},{3,15},{4,8},{5,9},{6,10},{7,11},{8,4},{9,5},... | collective-permute-start | bytes 786440 | tf_op jit(solution)/shard_map/ppermute | solution.py:30
  33.7 10.9 %collective-permute-start.16 = (bf16[2,256,256]{2,1,0:T(8,128)(2,1)S(1)}, bf16[2,256,256]{2,1,0:T(8,128)(2,1)S(1)}, u32[]{:S(2)}, u32[]{:S(2)}) collective-permute-start(bf16[2,256,256]{2,1,0:T(8,128)(2,1)S(1)} %slice.96), channel_id=1, source_target_pairs={{0,4},{1,5},{2,6},{3,7},{4,0},{5,1},{6,2},{7,3},{8,12},{9,13},{10,... | collective-permute-start | bytes 786440 | tf_op jit(solution)/shard_map/ppermute | solution.py:30
  41.6 13.6 %collective-permute-start.10 = (bf16[4,256,256]{2,1,0:T(8,128)(2,1)S(1)}, bf16[4,256,256]{2,1,0:T(8,128)(2,1)S(1)}, u32[]{:S(2)}, u32[]{:S(2)}) collective-permute-start(bf16[4,256,256]{2,1,0:T(8,128)(2,1)S(1)} %pad_maximum_fusion.1.refs_1_), channel_id=1, source_target_pairs={{0,1},{1,0},{2,3},{3,2},{4,5},{5,4},{6,7},{7,6},{8,9},{9,8},{10,11... | collective-permute-start | bytes 1572872 | tf_op jit(solution)/shard_map/ppermute | solution.py:30
  43.1 13.0 %collective-permute-start.11 = (bf16[4,256,256]{2,1,0:T(8,128)(2,1)S(1)}, bf16[4,256,256]{2,1,0:T(8,128)(2,1)S(1)}, u32[]{:S(2)}, u32[]{:S(2)}) collective-permute-start(bf16[4,256,256]{2,1,0:T(8,128)(2,1)S(1)} %pad_maximum_fusion.1.refs_1_), channel_id=1, source_target_pairs={{0,3},{1,2},{2,1},{3,0},{4,7},{5,6},{6,5},{7,4},{8,11},{9,10},{10,... | collective-permute-start | bytes 1572872 | tf_op jit(solution)/shard_map/ppermute | solution.py:30
  44.6 13.0 %collective-permute-start.13 = (bf16[4,256,256]{2,1,0:T(8,128)(2,1)S(1)}, bf16[4,256,256]{2,1,0:T(8,128)(2,1)S(1)}, u32[]{:S(2)}, u32[]{:S(2)}) collective-permute-start(bf16[4,256,256]{2,1,0:T(8,128)(2,1)S(1)} %pad_maximum_fusion.4.refs_3_), channel_id=1, source_target_pairs={{0,12},{1,13},{2,14},{3,15},{4,8},{5,9},{6,10},{7,11},{8,4},{9,5},... | collective-permute-start | bytes 1572872 | tf_op jit(solution)/shard_map/ppermute | solution.py:30
  45.0 12.7 %collective-permute-start.12 = (bf16[4,256,256]{2,1,0:T(8,128)(2,1)S(1)}, bf16[4,256,256]{2,1,0:T(8,128)(2,1)S(1)}, u32[]{:S(2)}, u32[]{:S(2)}) collective-permute-start(bf16[4,256,256]{2,1,0:T(8,128)(2,1)S(1)} %pad_maximum_fusion.4.refs_3_), channel_id=1, source_target_pairs={{0,4},{1,5},{2,6},{3,7},{4,0},{5,1},{6,2},{7,3},{8,12},{9,13},{10,... | collective-permute-start | bytes 1572872 | tf_op jit(solution)/shard_map/ppermute | solution.py:30
  48.6 27.3 %collective-permute-start.25 = (f16[272,1024]{1,0:T(8,128)(2,1)S(1)}, f16[272,1024]{1,0:T(8,128)(2,1)S(1)}, u32[]{:S(2)}, u32[]{:S(2)}) collective-permute-start(f16[272,1024]{1,0:T(8,128)(2,1)S(1)} %convert_element_type.39), channel_id=1, source_target_pairs={{0,64},{16,80},{32,96},{48,112},{64,0},{80,16},{96,32},{112,48},{1... | collective-permute-start | bytes 1671176 | tf_op jit(solution)/shard_map/ppermute | solution.py:30
  56.1 10.2 %collective-permute-start.18 = (bf16[2,256,256]{2,1,0:T(8,128)(2,1)S(1)}, bf16[2,256,256]{2,1,0:T(8,128)(2,1)S(1)}, u32[]{:S(2)}, u32[]{:S(2)}) collective-permute-start(bf16[2,256,256]{2,1,0:T(8,128)(2,1)S(1)} %slice.98), channel_id=1, source_target_pairs={{0,1},{1,0},{2,3},{3,2},{4,5},{5,4},{6,7},{7,6},{8,9},{9,8},{10,11... | collective-permute-start | bytes 786440 | tf_op jit(solution)/shard_map/ppermute | solution.py:30
  63.5 12.9 %collective-permute-start.27 = (f16[136,1024]{1,0:T(8,128)(2,1)S(1)}, f16[136,1024]{1,0:T(8,128)(2,1)S(1)}, u32[]{:S(2)}, u32[]{:S(2)}) collective-permute-start(f16[136,1024]{1,0:T(8,128)(2,1)S(1)} %convert_element_type.49), channel_id=1, source_target_pairs={{0,96},{16,112},{32,64},{48,80},{64,32},{80,48},{96,0},{112,16},{1... | collective-permute-start | bytes 835592 | tf_op jit(solution)/shard_map/ppermute | solution.py:30
  66.3 10.3 %collective-permute-start.23 = (f16[136,1024]{1,0:T(8,128)(2,1)S(1)}, f16[136,1024]{1,0:T(8,128)(2,1)S(1)}, u32[]{:S(2)}, u32[]{:S(2)}) collective-permute-start(f16[136,1024]{1,0:T(8,128)(2,1)S(1)} %convert_element_type.42), channel_id=1, source_target_pairs={{0,32},{16,48},{32,0},{48,16},{64,96},{80,112},{96,64},{112,80},{1... | collective-permute-start | bytes 835592 | tf_op jit(solution)/shard_map/ppermute | solution.py:30
  75.8 9.9 %collective-permute-start.28 = (f16[136,1024]{1,0:T(8,128)(2,1)S(1)}, f16[136,1024]{1,0:T(8,128)(2,1)S(1)}, u32[]{:S(2)}, u32[]{:S(2)}) collective-permute-start(f16[136,1024]{1,0:T(8,128)(2,1)S(1)} %convert_element_type.47), channel_id=1, source_target_pairs={{0,112},{16,96},{32,80},{48,64},{64,48},{80,32},{96,16},{112,0},{1... | collective-permute-start | bytes 835592 | tf_op jit(solution)/shard_map/ppermute | solution.py:30
  76.4 9.4 %collective-permute-start.26 = (f16[136,1024]{1,0:T(8,128)(2,1)S(1)}, f16[136,1024]{1,0:T(8,128)(2,1)S(1)}, u32[]{:S(2)}, u32[]{:S(2)}) collective-permute-start(f16[136,1024]{1,0:T(8,128)(2,1)S(1)} %get-tuple-element.61), channel_id=1, source_target_pairs={{0,16},{16,0},{32,48},{48,32},{64,80},{80,64},{96,112},{112,96},{1... | collective-permute-start | bytes 835592 | tf_op jit(solution)/shard_map/ppermute | solution.py:30
  108.2 11.8 %collective-permute-start.40 = (bf16[128,1024]{1,0:T(8,128)(2,1)S(1)}, bf16[128,1024]{1,0:T(8,128)(2,1)S(1)}, u32[]{:S(2)}, u32[]{:S(2)}) collective-permute-start(bf16[128,1024]{1,0:T(8,128)(2,1)S(1)} %get-tuple-element.69.refs_0_), channel_id=1, source_target_pairs={{0,64},{16,80},{32,96},{48,112},{64,0},{80,16},{96,32},{112,48},{1... | collective-permute-start | bytes 786440 | tf_op jit(solution)/shard_map/ppermute | solution.py:30
  108.6 11.4 %collective-permute-start.41 = (bf16[128,1024]{1,0:T(8,128)(2,1)S(1)}, bf16[128,1024]{1,0:T(8,128)(2,1)S(1)}, u32[]{:S(2)}, u32[]{:S(2)}) collective-permute-start(bf16[128,1024]{1,0:T(8,128)(2,1)S(1)} %get-tuple-element.69.refs_0_), channel_id=1, source_target_pairs={{0,32},{16,48},{32,0},{48,16},{64,96},{80,112},{96,64},{112,80},{1... | collective-permute-start | bytes 786440 | tf_op jit(solution)/shard_map/ppermute | solution.py:30
  (24 other events, 182.7 us)
